TPU v7x, 1024 devices: a whole 4x8x16 slice. The times are simulated.
1024 devices in a mesh: row: 128 (over z, y), col: 8 (over x, core).
Axes of the slice: x: 4, y: 8, z: 16, core: 2. Of those that a mesh axis runs over, the one named last changes fastest.
Arguments:
- features: bfloat16 [65536, 512], P('row', 'col'), may hold values from -6 to 6
- adjacency: bfloat16 [65536, 5, 512], P('row'), may hold values from 0 to 1, as said below
- tile_mask: int32 [512, 5, 4], P('row'), may hold values from 0 to 1, as said below
- w_self: bfloat16 [512, 512], P('col'), may hold values from -0.25 to 0.25
- w_neigh: bfloat16 [512, 512], P('col'), may hold values from -0.25 to 0.25
- cotangent: bfloat16 [65536, 512], P('row', 'col'), may hold values from -6 to 6
Outputs:
- activated: bfloat16 [65536, 512], P('row', 'col')
- grad_features: bfloat16 [65536, 512], P('row', 'col')
- grad_self: float32 [512, 512], P('col')
- grad_neigh: float32 [512, 512], P('col')
Inputs may be any that keep to these rules, and one draw needn't show every extreme that they name: `adjacency`: edge weights. Each node has at most 24 edges; every edge links to a node near the node's own position within its panel, in its own panel or in one up to 2 panels away. `tile_mask`: exactly the tiles that hold an edge are marked 1; how many varies from panel to panel.
All inputs are finite; a program needn't handle non-finite values.
Results may differ from a plain program's by a relative error of at most 0.0052.
Values may be sent and summed in bfloat16 or wider, within the bound.
No kernel may reach another device: no remote copies, remote signals or barrier semaphores. Data moves between devices by JAX's collectives and lax.ppermute only.
A program may use at most 32 MiB of HBM per device.

v0:
```python
import math

import jax
import jax.numpy as jnp
from jax import lax
from jax.sharding import PartitionSpec as P


def from_behind(value, axis, steps):
    count = lax.axis_size(axis)
    pairs = [(source, (source + steps) % count) for source in range(count)]
    return lax.ppermute(value, axis, pairs)


def masked_band(adj_block, mask_block):
    tile_rows = mask_block.shape[0]
    band_count = mask_block.shape[1]
    tile_cols = mask_block.shape[2]
    blocks = adj_block.reshape(tile_rows, 128, band_count, tile_cols, 128)
    tile_keep = mask_block.astype(jnp.bfloat16)[:, None, :, :, None]
    return (blocks * tile_keep).reshape(adj_block.shape)


def body(features, adjacency, tile_mask, w_self, w_neigh, cotangent):
    weighted = masked_band(adjacency, tile_mask)
    band_reach = (tile_mask.shape[1] - 1) // 2
    degree = jnp.sum(weighted, axis=(1, 2), dtype=jnp.float32)
    inverse = 1.0 / jnp.maximum(degree, 1.0)
    summed = jnp.dot(weighted[:, band_reach, :], features, preferred_element_type=jnp.float32)
    for offset in range(-band_reach, band_reach + 1):
        if offset != 0:
            neighbour = from_behind(features, "row", -offset)
            summed = summed + jnp.dot(
                weighted[:, band_reach + offset, :], neighbour, preferred_element_type=jnp.float32
            )
    mean_neigh = (summed * inverse[:, None]).astype(jnp.bfloat16)
    partial_pre = jnp.dot(features, w_self, preferred_element_type=jnp.float32)
    partial_pre = partial_pre + jnp.dot(mean_neigh, w_neigh, preferred_element_type=jnp.float32)
    preact = lax.psum_scatter(partial_pre, "col", scatter_dimension=1, tiled=True)
    sigmoid_z = jax.nn.sigmoid(preact)
    activated = (preact * sigmoid_z).astype(jnp.bfloat16)
    slope = sigmoid_z * (1.0 + preact * (1.0 - sigmoid_z))
    grad_preact = (cotangent.astype(jnp.float32) * slope).astype(jnp.bfloat16)
    node_rows = features.shape[0]
    columns_in = lax.all_gather(grad_preact, "col", axis=1, tiled=True)
    contract_last = (((1,), (1,)), ((), ()))
    contract_rows = (((0,), (0,)), ((), ()))
    self_grad = lax.dot_general(
        columns_in, w_self, contract_last, preferred_element_type=jnp.float32
    )
    neigh_grad = lax.dot_general(
        columns_in, w_neigh, contract_last, preferred_element_type=jnp.float32
    )
    wself_part = lax.dot_general(
        features, columns_in, contract_rows, preferred_element_type=jnp.float32
    )
    wneigh_part = lax.dot_general(
        mean_neigh, columns_in, contract_rows, preferred_element_type=jnp.float32
    )
    self_grad, neigh_grad, wself_local, wneigh_local = (
        self_grad,
        neigh_grad,
        wself_part,
        wneigh_part,
    )
    spread = (neigh_grad * inverse[:, None]).astype(jnp.bfloat16)
    contract_rows = (((0,), (0,)), ((), ()))
    transposed = [
        lax.dot_general(
            weighted[:, band_id, :], spread, contract_rows, preferred_element_type=jnp.float32
        )
        for band_id in range(2 * band_reach + 1)
    ]
    returned = transposed[band_reach]
    for offset in range(-band_reach, band_reach + 1):
        if offset != 0:
            returned = returned + from_behind(
                transposed[band_reach + offset].astype(jnp.bfloat16), "row", offset
            ).astype(jnp.float32)
    grad_features = (self_grad + returned).astype(jnp.bfloat16)
    node_total = lax.axis_size("row") * node_rows
    grad_scale = 1.0 / math.sqrt(node_total)
    grad_self, grad_neigh = lax.psum((wself_local * grad_scale, wneigh_local * grad_scale), "row")
    return (activated, grad_features, grad_self, grad_neigh)


def solution(mesh):
    return jax.shard_map(
        body,
        mesh=mesh,
        in_specs=(
            P("row", "col"),
            P("row", None, None),
            P("row", None, None),
            P("col", None),
            P("col", None),
            P("row", "col"),
        ),
        out_specs=(P("row", "col"), P("row", "col"), P("col", None), P("col", None)),
        check_vma=False,
    )
```

profile of v0, /device:TPU:24, one launch (start us, length us, event | category | flops | bytes accessed | tf_op | source)
XLA Modules:
  0.0 398.8 jit_solution(15281172974764538683)
XLA Ops:
  7.2 4.8 %collective-permute-start = (bf16[512,64]{0,1:T(8,128)(2,1)}, bf16[512,64]{0,1:T(8,128)(2,1)S(1)}, u32[]{:S(2)}, u32[]{:S(2)}) collective-permute-start(bf16[512,64]{0,1:T(8,128)(2,1)} %param.6), channel_id=1, source_target_pairs={{0,16},{8,24},{16,32},{24,40},{32,48},{40,56},{48,64},{56,72},{64,... | collective-permute-start | bytes 196616 | tf_op jit(solution)/shard_map/ppermute | solution.py:12
  12.0 3.3 collective-permute-start.2
  15.3 11.1 %collective-permute-start.3 = (bf16[512,64]{0,1:T(8,128)(2,1)}, bf16[512,64]{0,1:T(8,128)(2,1)S(1)}, u32[]{:S(2)}, u32[]{:S(2)}) collective-permute-start(bf16[512,64]{0,1:T(8,128)(2,1)} %param.6), channel_id=1, source_target_pairs={{0,1008},{8,1016},{16,0},{24,8},{32,16},{40,24},{48,32},{56,40},{6... | collective-permute-start | bytes 196616 | tf_op jit(solution)/shard_map/ppermute | solution.py:12
  26.4 1.9 collective-permute-start.1
  28.4 0.7 convert_element_type.48
  29.2 0.7 mul.46
  29.9 3.0 mul.47
  33.0 3.5 convert_reduce_fusion
  36.5 0.3 fusion.7
  36.8 0.3 fusion.10
  37.2 0.3 convolution_add_fusion.2
  37.5 0.3 fusion.8
  38.0 0.3 fusion.4
  38.3 1.3 convolution_add_fusion
  39.7 42.9 %reduce-scatter.2.cloned.1.call-done = f32[512,64]{0,1:T(8,128)} async-done(((f32[512,512]{0,1:T(8,128)}), f32[512,64]{0,1:T(8,128)}) %reduce-scatter.2.cloned.1.call-update) | async-done | bytes 131088 | tf_op jit(solution)/shard_map/reduce_scatter | solution.py:39
  82.6 1.6 multiply_convert_fusion
  84.2 13.1 %all_gather.3 = bf16[512,512]{0,1:T(8,128)(2,1)S(1)} all-gather(bf16[512,64]{0,1:T(8,128)(2,1)S(1)} %get-tuple-element.8), channel_id=1, replica_groups=mesh['row'=128,'col'=8] {'col'}, dimensions={1}, use_global_device_ids=true | all-gather | bytes 589824 | tf_op jit(solution)/shard_map/all_gather | solution.py:45
  97.3 0.9 convolution_multiply_fusion.1
  98.2 0.9 fusion
  99.4 0.8 convolution_convert_fusion.3
  100.2 0.8 convolution_convert_fusion.2
  101.0 0.8 convolution_convert_fusion.1
  102.1 2.4 collective-permute-start.4
  104.5 2.5 collective-permute-start.5
  107.0 4.5 %collective-permute-start.6 = (bf16[512,64]{0,1:T(8,128)(2,1)}, bf16[512,64]{0,1:T(8,128)(2,1)}, u32[]{:S(2)}, u32[]{:S(2)}) collective-permute-start(bf16[512,64]{0,1:T(8,128)(2,1)} %convolution_convert_fusion.1), channel_id=1, source_target_pairs={{0,8},{8,16},{16,24},{24,32},{32,40},{40,48},{48,56},{56,64},{64,7... | collective-permute-start | bytes 196616 | tf_op jit(solution)/shard_map/ppermute | solution.py:12
  111.6 4.3 %collective-permute-start.7 = (bf16[512,64]{0,1:T(8,128)(2,1)S(1)}, bf16[512,64]{0,1:T(8,128)(2,1)}, u32[]{:S(2)}, u32[]{:S(2)}) collective-permute-start(bf16[512,64]{0,1:T(8,128)(2,1)S(1)} %convolution_convert_fusion), channel_id=1, source_target_pairs={{0,16},{8,24},{16,32},{24,40},{32,48},{40,56},{48,64},{56,72},{64,... | collective-permute-start | bytes 196616 | tf_op jit(solution)/shard_map/ppermute | solution.py:12
  116.2 2.9 collective-permute-done.6
  119.0 4.4 %collective-permute-done.7 = bf16[512,64]{0,1:T(8,128)(2,1)} collective-permute-done((bf16[512,64]{0,1:T(8,128)(2,1)S(1)}, bf16[512,64]{0,1:T(8,128)(2,1)}, u32[]{:S(2)}, u32[]{:S(2)}) %collective-permute-start.7) | collective-permute-done | bytes 65568 | tf_op jit(solution)/shard_map/ppermute | solution.py:12
  123.5 1.7 add_convert_fusion
  125.2 263.6 %all-reduce.3.cloned.1.call-done = (f32[64,512]{1,0:T(8,128)}, f32[64,512]{1,0:T(8,128)}) async-done(((f32[64,512]{1,0:T(8,128)}, f32[64,512]{1,0:T(8,128)}), (f32[64,512]{1,0:T(8,128)}, f32[64,512]{1,0:T(8,128)})) %all-reduce.3.cloned.1.call-update) | async-done | bytes 262160 | tf_op jit(solution)/shard_map/psum | solution.py:83
  388.8 1.6 copy.13
  390.4 1.6 copy.14
  (24 shorter events, 1.2 us)
Async XLA Ops:
  7.2 31.2 %copy-start = (bf16[64,512]{1,0:T(8,128)(2,1)S(1)}, bf16[64,512]{1,0:T(8,128)(2,1)}, u32[]{:S(2)}) copy-start(bf16[64,512]{1,0:T(8,128)(2,1)} %param.10) | copy-start | bytes 196612
  7.2 75.4 %reduce-scatter.2.cloned.1.call-start = ((), (), s32[]{:S(2)}) async-start(), calls=%async_computation.1 | async-start | bytes 1179648 | tf_op jit(solution)/shard_map/reduce_scatter | solution.py:39
  7.2 29.9 %collective-permute-start = (bf16[512,64]{0,1:T(8,128)(2,1)}, bf16[512,64]{0,1:T(8,128)(2,1)S(1)}, u32[]{:S(2)}, u32[]{:S(2)}) collective-permute-start(bf16[512,64]{0,1:T(8,128)(2,1)} %param.6), channel_id=1, source_target_pairs={{0,16},{8,24},{16,32},{24,40},{32,48},{40,56},{48,64},{56,72},{64,... | collective-permute-start | bytes 196616 | tf_op jit(solution)/shard_map/ppermute | solution.py:12
  12.0 25.4 %collective-permute-start.2 = (bf16[512,64]{0,1:T(8,128)(2,1)}, bf16[512,64]{0,1:T(8,128)(2,1)S(1)}, u32[]{:S(2)}, u32[]{:S(2)}) collective-permute-start(bf16[512,64]{0,1:T(8,128)(2,1)} %param.6), channel_id=1, source_target_pairs={{0,1016},{8,0},{16,8},{24,16},{32,24},{40,32},{48,40},{56,48},{64,... | collective-permute-start | bytes 196616 | tf_op jit(solution)/shard_map/ppermute | solution.py:12
  15.3 22.4 %collective-permute-start.3 = (bf16[512,64]{0,1:T(8,128)(2,1)}, bf16[512,64]{0,1:T(8,128)(2,1)S(1)}, u32[]{:S(2)}, u32[]{:S(2)}) collective-permute-start(bf16[512,64]{0,1:T(8,128)(2,1)} %param.6), channel_id=1, source_target_pairs={{0,1008},{8,1016},{16,0},{24,8},{32,16},{40,24},{48,32},{56,40},{6... | collective-permute-start | bytes 196616 | tf_op jit(solution)/shard_map/ppermute | solution.py:12
  26.4 11.6 %collective-permute-start.1 = (bf16[512,64]{0,1:T(8,128)(2,1)}, bf16[512,64]{0,1:T(8,128)(2,1)S(1)}, u32[]{:S(2)}, u32[]{:S(2)}) collective-permute-start(bf16[512,64]{0,1:T(8,128)(2,1)} %param.6), channel_id=1, source_target_pairs={{0,8},{8,16},{16,24},{24,32},{32,40},{40,48},{48,56},{56,64},{64,7... | collective-permute-start | bytes 196616 | tf_op jit(solution)/shard_map/ppermute | solution.py:12
  33.0 3.5 copy-start.2
  33.0 3.8 copy-start.1
  37.7 44.9 %copy-start.3 = (bf16[512,64]{0,1:T(8,128)(2,1)S(1)}, bf16[512,64]{0,1:T(8,128)(2,1)}, u32[]{:S(2)}) copy-start(bf16[512,64]{0,1:T(8,128)(2,1)} %param.11) | copy-start | bytes 196612
  39.7 349.1 %all-reduce.3.cloned.1.call-start = ((), (), s32[]{:S(2)}) async-start(), calls=%async_computation.2 | async-start | bytes 524288 | tf_op jit(solution)/shard_map/psum | solution.py:83
  102.1 14.1 %collective-permute-start.4 = (bf16[512,64]{0,1:T(8,128)(2,1)}, bf16[512,64]{0,1:T(8,128)(2,1)S(1)}, u32[]{:S(2)}, u32[]{:S(2)}) collective-permute-start(bf16[512,64]{0,1:T(8,128)(2,1)} %convolution_convert_fusion.3), channel_id=1, source_target_pairs={{0,1008},{8,1016},{16,0},{24,8},{32,16},{40,24},{48,32},{56,40},{6... | collective-permute-start | bytes 196616 | tf_op jit(solution)/shard_map/ppermute | solution.py:12
  104.5 11.7 %collective-permute-start.5 = (bf16[512,64]{0,1:T(8,128)(2,1)}, bf16[512,64]{0,1:T(8,128)(2,1)S(1)}, u32[]{:S(2)}, u32[]{:S(2)}) collective-permute-start(bf16[512,64]{0,1:T(8,128)(2,1)} %convolution_convert_fusion.2), channel_id=1, source_target_pairs={{0,1016},{8,0},{16,8},{24,16},{32,24},{40,32},{48,40},{56,48},{64,... | collective-permute-start | bytes 196616 | tf_op jit(solution)/shard_map/ppermute | solution.py:12
  107.0 12.0 %collective-permute-start.6 = (bf16[512,64]{0,1:T(8,128)(2,1)}, bf16[512,64]{0,1:T(8,128)(2,1)}, u32[]{:S(2)}, u32[]{:S(2)}) collective-permute-start(bf16[512,64]{0,1:T(8,128)(2,1)} %convolution_convert_fusion.1), channel_id=1, source_target_pairs={{0,8},{8,16},{16,24},{24,32},{32,40},{40,48},{48,56},{56,64},{64,7... | collective-permute-start | bytes 196616 | tf_op jit(solution)/shard_map/ppermute | solution.py:12
  111.6 11.9 %collective-permute-start.7 = (bf16[512,64]{0,1:T(8,128)(2,1)S(1)}, bf16[512,64]{0,1:T(8,128)(2,1)}, u32[]{:S(2)}, u32[]{:S(2)}) collective-permute-start(bf16[512,64]{0,1:T(8,128)(2,1)S(1)} %convolution_convert_fusion), channel_id=1, source_target_pairs={{0,16},{8,24},{16,32},{24,40},{32,48},{40,56},{48,64},{56,72},{64,... | collective-permute-start | bytes 196616 | tf_op jit(solution)/shard_map/ppermute | solution.py:12
Sparse Core Ops, SparseCore 0:
  39.8 42.7 reduce-scatter.1
  116.1 272.6 all-reduce.2
where the time goes:
time: 399 us
  waiting for transfers between devices  314 us (79%)
  starting transfers between devices  35 us (9%)
  between operations  14.2 us (4%)
  blocking collectives  13.1 us (3%)
  matrix products  9.74 us (2%)
  local copies, waits for them, and re-layouts  7.06 us (2%)
  other arithmetic  5.83 us (1%)
    psum x1, waiting for transfers between devices, body(): lax.psum((wself_local * grad_scale, wneigh_local * grad_scale), 'row')  264 us
    reduce_scatter x1, waiting for transfers between devices, body(): lax.psum_scatter(partial_pre, 'col', scatter_dimension=1, tiled=True)  42.9 us
    ppermute x8, starting transfers between devices, from_behind(): return lax.ppermute(value, axis, pairs)  34.9 us
    all_gather x1, blocking collectives, body(): columns_in = lax.all_gather(grad_preact, 'col', axis=1, tiled=True)  13.1 us
  transfers between devices with their start and end apart: 10, of which 4 were waited for; matrix products, arithmetic and copies ran while one was open for 3% of the time, Pallas kernels for 0%

commit v1 on v0

v1 whole, which is shorter than its diff:
```python
import math

import jax
import jax.numpy as jnp
from jax import lax
from jax.experimental import pallas as pl
from jax.experimental.pallas import tpu as pltpu
from jax.sharding import Mesh
from jax.sharding import PartitionSpec as P

ROW = ("z", "y")
COL = ("x", "core")
TILE = 128
DOT = dict(preferred_element_type=jnp.float32)


def mask_kernel(mask_ref, adj_ref, out_ref):
    band = pl.program_id(0)
    for row in range(adj_ref.shape[1] // TILE):
        for column in range(adj_ref.shape[2] // TILE):
            rows = pl.ds(row * TILE, TILE)
            columns = pl.ds(column * TILE, TILE)
            keep = mask_ref[row, band, column].astype(jnp.float32).astype(jnp.bfloat16)
            out_ref[0, rows, columns] = adj_ref[0, rows, columns] * keep


def masked_bands(bands, mask):
    count, rows, columns = bands.shape
    block = pl.BlockSpec((1, rows, columns), lambda band: (band, 0, 0))
    return pl.pallas_call(
        mask_kernel,
        grid=(count,),
        out_shape=jax.ShapeDtypeStruct(bands.shape, bands.dtype),
        in_specs=[pl.BlockSpec(memory_space=pltpu.SMEM), block],
        out_specs=block,
        cost_estimate=pl.CostEstimate(
            flops=bands.size, bytes_accessed=4 * bands.size, transcendentals=0
        ),
    )(mask, bands)


def from_behind(value, steps):
    count = lax.axis_size(ROW)
    pairs = [(source, (source + steps) % count) for source in range(count)]
    return lax.ppermute(value, ROW, pairs)


def exchange(chunks, axes):
    return lax.all_to_all(chunks, axes, 0, 0, tiled=True)


def to_all(value, axes):
    copies = jnp.broadcast_to(value, (lax.axis_size(axes),) + value.shape)
    return exchange(copies, axes)


def body(features, adjacency, tile_mask, w_self, w_neigh, cotangent):
    own = features.T
    width, nodes = own.shape
    groups = lax.axis_size(COL)
    lines = lax.axis_size("y")
    total = groups * width
    band_reach = (tile_mask.shape[1] - 1) // 2
    offsets = [k for k in range(-band_reach, band_reach + 1) if k != 0]

    columns_out = jnp.concatenate(
        [
            jnp.broadcast_to(own, (groups, width, nodes)),
            w_self.reshape(width, groups, width).transpose(1, 0, 2),
            w_neigh.reshape(width, groups, width).transpose(1, 0, 2),
        ],
        axis=2,
    )
    neighbours = {k: from_behind(own, -k) for k in offsets}
    early = exchange(columns_out, COL)
    feats = early[:, :, :nodes]
    self_cols = early[:, :, nodes : nodes + width].reshape(total, width)
    neigh_cols = early[:, :, nodes + width :].reshape(total, width)

    weighted = masked_bands(adjacency.transpose(1, 0, 2), tile_mask)
    degree = jnp.sum(weighted, axis=(0, 2), dtype=jnp.float32)
    inverse = 1.0 / jnp.maximum(degree, 1.0)
    last = (((1,), (1,)), ((), ()))
    first = (((0,), (0,)), ((), ()))
    summed = lax.dot_general(own, weighted[band_reach], last, **DOT)
    for k in offsets:
        summed = summed + lax.dot_general(neighbours[k], weighted[band_reach + k], last, **DOT)
    mean = (summed * inverse[None, :]).astype(jnp.bfloat16)
    means = to_all(mean, COL)

    preact = lax.dot_general(self_cols, feats.reshape(total, nodes), first, **DOT)
    preact = preact + lax.dot_general(neigh_cols, means.reshape(total, nodes), first, **DOT)
    sigmoid_z = jax.nn.sigmoid(preact)
    activated = (preact * sigmoid_z).astype(jnp.bfloat16)
    slope = sigmoid_z * (1.0 + preact * (1.0 - sigmoid_z))
    grad_preact = (cotangent.T.astype(jnp.float32) * slope).astype(jnp.bfloat16)

    grad_scale = 1.0 / math.sqrt(lax.axis_size(ROW) * nodes)
    stacked = jnp.concatenate([feats, means], axis=1).reshape(2 * total, nodes)
    partial = lax.dot_general(grad_preact, stacked, last, **DOT) * grad_scale
    pieces = partial.astype(jnp.bfloat16).reshape(lines, width // lines, 2 * total)
    over_y = jnp.sum(exchange(pieces, "y").astype(jnp.float32), axis=0)
    over_z = jnp.sum(to_all(over_y.astype(jnp.bfloat16), "z").astype(jnp.float32), axis=0)
    shares = over_z.reshape(width // lines, groups, 2 * width).transpose(1, 0, 2)
    shares = jnp.broadcast_to(shares[:, None], (groups, lines) + shares.shape[1:])
    shares = shares.reshape((groups * lines,) + shares.shape[2:])
    gathered = exchange(shares, COL + ("y",)).reshape(total, 2 * width).T

    grads = to_all(grad_preact, COL).reshape(total, nodes)
    spread = (jnp.dot(w_neigh, grads, **DOT) * inverse[None, :]).astype(jnp.bfloat16)
    terms = {
        k: jnp.dot(spread, weighted[band_reach + k], **DOT).astype(jnp.bfloat16) for k in offsets
    }
    returned = jnp.dot(w_self, grads, **DOT) + jnp.dot(spread, weighted[band_reach], **DOT)
    for k in offsets:
        returned = returned + from_behind(terms[k], k).astype(jnp.float32)
    grad_features = returned.astype(jnp.bfloat16)
    return (activated.T, grad_features.T, gathered[:width], gathered[width:])


def solution(mesh):
    rows, columns = mesh.devices.shape
    lines = math.gcd(rows, 8)
    cores = math.gcd(columns, 2)
    fine = Mesh(
        mesh.devices.reshape(rows // lines, lines, columns // cores, cores), ROW + COL
    )
    return jax.shard_map(
        body,
        mesh=fine,
        in_specs=(
            P(ROW, COL),
            P(ROW, None, None),
            P(ROW, None, None),
            P(COL, None),
            P(COL, None),
            P(ROW, COL),
        ),
        out_specs=(P(ROW, COL), P(ROW, COL), P(COL, None), P(COL, None)),
        check_vma=False,
    )
```

time: 399 us -> 160 us (0.40)
  the two profiles are of different devices: /device:TPU:24 before, /device:TPU:1 now
where the time goes in v1:
time: 160 us; the launch traced here: 158 us
  starting transfers between devices  73.8 us (46%)
  waiting for transfers between devices  34.9 us (22%)
  blocking collectives  25.4 us (16%)
  matrix products  8.2 us (5%)
  local copies, waits for them, and re-layouts  6.61 us (4%)
  Pallas kernels  4.96 us (3%)
  other arithmetic  3.33 us (2%)
    ppermute x8, starting transfers between devices, from_behind(): return lax.ppermute(value, ROW, pairs)  44.8 us
    all_to_all x4, starting transfers between devices, exchange(): return lax.all_to_all(chunks, axes, 0, 0, tiled=True)  29.1 us
    all_to_all x4, waiting for transfers between devices, exchange(): return lax.all_to_all(chunks, axes, 0, 0, tiled=True)  27.8 us
    all_to_all x2, blocking collectives, exchange(): return lax.all_to_all(chunks, axes, 0, 0, tiled=True)  25.4 us
    ppermute x8, waiting for transfers between devices, from_behind(): return lax.ppermute(value, ROW, pairs)  7.08 us
    pallas_call x1, Pallas kernels, masked_bands(): pl.pallas_call(mask_kernel, grid=(count,), out_shape=jax.ShapeDtypeStruct...  4.96 us
  transfers between devices with their start and end apart: 12, of which 5 were waited for; matrix products, arithmetic and copies ran while one was open for 7% of the time, Pallas kernels for 3%

profile of v1, /device:TPU:1, one launch (start us, length us, event | category | flops | bytes accessed | tf_op | source)
XLA Modules:
  0.0 158.2 jit_solution(6614766040106745070)
XLA Ops:
  0.6 5.0 %collective-permute-start = (bf16[64,512]{1,0:T(8,128)(2,1)}, bf16[64,512]{1,0:T(8,128)(2,1)S(1)}, u32[]{:S(2)}, u32[]{:S(2)}) collective-permute-start(bf16[64,512]{1,0:T(8,128)(2,1)} %bitcast.99), channel_id=1, source_target_pairs={{0,16},{8,24},{16,32},{24,40},{32,48},{40,56},{48,64},{56,72},{64,... | collective-permute-start | bytes 196616 | tf_op jit(solution)/shard_map/ppermute | solution.py:45
  5.7 18.6 %collective-permute-start.2 = (bf16[64,512]{1,0:T(8,128)(2,1)}, bf16[64,512]{1,0:T(8,128)(2,1)S(1)}, u32[]{:S(2)}, u32[]{:S(2)}) collective-permute-start(bf16[64,512]{1,0:T(8,128)(2,1)} %bitcast.100), channel_id=1, source_target_pairs={{0,1016},{8,0},{16,8},{24,16},{32,24},{40,32},{48,40},{56,48},{64,... | collective-permute-start | bytes 196616 | tf_op jit(solution)/shard_map/ppermute | solution.py:45
  24.2 4.3 %collective-permute-start.3 = (bf16[64,512]{1,0:T(8,128)(2,1)}, bf16[64,512]{1,0:T(8,128)(2,1)S(1)}, u32[]{:S(2)}, u32[]{:S(2)}) collective-permute-start(bf16[64,512]{1,0:T(8,128)(2,1)} %bitcast.101), channel_id=1, source_target_pairs={{0,1008},{8,1016},{16,0},{24,8},{32,16},{40,24},{48,32},{56,40},{6... | collective-permute-start | bytes 196616 | tf_op jit(solution)/shard_map/ppermute | solution.py:45
  28.5 1.9 %collective-permute-start.1 = (bf16[64,512]{1,0:T(8,128)(2,1)}, bf16[64,512]{1,0:T(8,128)(2,1)S(1)}, u32[]{:S(2)}, u32[]{:S(2)}) collective-permute-start(bf16[64,512]{1,0:T(8,128)(2,1)} %bitcast.102), channel_id=1, source_target_pairs={{0,8},{8,16},{16,24},{24,32},{32,40},{40,48},{48,56},{56,64},{64,7... | collective-permute-start | bytes 196616 | tf_op jit(solution)/shard_map/ppermute | solution.py:45
  30.5 1.4 copy.24.mask_ref
  31.9 5.0 %shard_map.93 = bf16[5,512,512]{2,1,0:T(8,128)(2,1)} custom-call(s32[4,5,4]{2,1,0:T(8,128)} %copy.24.mask_ref, bf16[5,512,512]{2,1,0:T(8,128)(2,1)} %bitcast.94), custom_call_target="tpu_custom_call" | custom-call | flops 1310720 | bytes 5242880 | tf_op jit(solution)/shard_map/pallas_call | solution.py:30
  36.8 1.5 fusion.11
  38.3 2.2 %convert_reduce_fusion = f32[512]{0:T(512)S(1)} fusion(bf16[5,512,512]{2,1,0:T(8,128)(2,1)} %shard_map.93), kind=kLoop, calls=%fused_computation | loop fusion | flops 2620928 | bytes 2623488 | tf_op jit(solution)/shard_map/reduce_sum | solution.py:81
  41.7 0.8 broadcast_in_dim.21
  42.5 5.8 %all-to-all-start.1 = ((bf16[8,64,512]{2,1,0:T(8,128)(2,1)}), bf16[8,64,512]{2,1,0:T(8,128)(2,1)S(1)}, u32[]{:S(2)}, u32[]{:S(2)}) async-start(bf16[8,64,512]{2,1,0:T(8,128)(2,1)} %broadcast_in_dim.21), calls=%async_computation.1 | async-start | bytes 1048576 | tf_op jit(solution)/shard_map/all_to_all | solution.py:49
  48.7 1.0 pad_maximum_fusion.1
  49.7 8.1 %all-to-all-done.1 = bf16[8,64,512]{2,1,0:T(8,128)(2,1)S(1)} async-done(((bf16[8,64,512]{2,1,0:T(8,128)(2,1)}), bf16[8,64,512]{2,1,0:T(8,128)(2,1)S(1)}, u32[]{:S(2)}, u32[]{:S(2)}) %all-to-all-start.1) | async-done | bytes 524320 | tf_op jit(solution)/shard_map/all_to_all | solution.py:49
  57.8 15.2 %all_to_all.30 = bf16[8,64,640]{2,1,0:T(8,128)(2,1)S(1)} all-to-all(bf16[8,64,640]{2,1,0:T(8,128)(2,1)} %pad_maximum_fusion.1), channel_id=1, replica_groups=mesh['z'=16,'y'=8,'x'=4,'core'=2] {'x','core'}, dimensions={0} | all-to-all | bytes 1310720 | tf_op jit(solution)/shard_map/all_to_all | solution.py:49
  73.4 0.9 fusion.20
  74.9 10.1 %all_to_all.31 = bf16[8,8,1024]{2,1,0:T(8,128)(2,1)S(1)} all-to-all(bf16[8,8,1024]{2,1,0:T(8,128)(2,1)S(1)} %fusion.6), channel_id=1, replica_groups=mesh['z'=16,'y'=8,'x'=4,'core'=2] {'y'}, dimensions={0} | all-to-all | bytes 262144 | tf_op jit(solution)/shard_map/all_to_all | solution.py:49
  85.0 0.8 broadcast_in_dim.22
  85.9 5.7 %all-to-all-start.2 = ((bf16[8,64,512]{2,1,0:T(8,128)(2,1)}), bf16[8,64,512]{2,1,0:T(8,128)(2,1)S(1)}, u32[]{:S(2)}, u32[]{:S(2)}) async-start(bf16[8,64,512]{2,1,0:T(8,128)(2,1)} %broadcast_in_dim.22), calls=%async_computation.2 | async-start | bytes 1048576 | tf_op jit(solution)/shard_map/all_to_all | solution.py:49
  91.6 9.5 %all-to-all-done.2 = bf16[8,64,512]{2,1,0:T(8,128)(2,1)S(1)} async-done(((bf16[8,64,512]{2,1,0:T(8,128)(2,1)}), bf16[8,64,512]{2,1,0:T(8,128)(2,1)S(1)}, u32[]{:S(2)}, u32[]{:S(2)}) %all-to-all-start.2) | async-done | bytes 524320 | tf_op jit(solution)/shard_map/all_to_all | solution.py:49
  101.8 7.0 %all-to-all-start.4 = ((bf16[16,8,1024]{2,1,0:T(8,128)(2,1)}), bf16[16,8,1024]{2,1,0:T(8,128)(2,1)S(1)}, u32[]{:S(2)}, u32[]{:S(2)}) async-start(bf16[16,8,1024]{2,1,0:T(8,128)(2,1)} %broadcast_in_dim.23), calls=%async_computation.4 | async-start | bytes 524288 | tf_op jit(solution)/shard_map/all_to_all | solution.py:49
  109.0 0.8 convolution_convert_fusion.3
  109.8 0.8 convolution_convert_fusion.2
  110.7 0.8 convolution_convert_fusion.1
  111.5 10.2 %all-to-all-done.4 = bf16[16,8,1024]{2,1,0:T(8,128)(2,1)S(1)} async-done(((bf16[16,8,1024]{2,1,0:T(8,128)(2,1)}), bf16[16,8,1024]{2,1,0:T(8,128)(2,1)S(1)}, u32[]{:S(2)}, u32[]{:S(2)}) %all-to-all-start.4) | async-done | bytes 262176 | tf_op jit(solution)/shard_map/all_to_all | solution.py:49
  122.5 10.6 %all-to-all-start.5 = ((f32[64,8,128]{2,1,0:T(8,128)}), f32[64,8,128]{2,1,0:T(8,128)S(1)}, u32[]{:S(2)}, u32[]{:S(2)}) async-start(f32[64,8,128]{2,1,0:T(8,128)} %bitcast.96), calls=%async_computation.5 | async-start | bytes 524288 | tf_op jit(solution)/shard_map/all_to_all | solution.py:49
  133.4 7.8 %collective-permute-start.4 = (bf16[64,512]{1,0:T(8,128)(2,1)}, bf16[64,512]{1,0:T(8,128)(2,1)S(1)}, u32[]{:S(2)}, u32[]{:S(2)}) collective-permute-start(bf16[64,512]{1,0:T(8,128)(2,1)} %convolution_convert_fusion.3), channel_id=1, source_target_pairs={{0,1008},{8,1016},{16,0},{24,8},{32,16},{40,24},{48,32},{56,40},{6... | collective-permute-start | bytes 196616 | tf_op jit(solution)/shard_map/ppermute | solution.py:45
  141.1 3.1 %collective-permute-start.5 = (bf16[64,512]{1,0:T(8,128)(2,1)}, bf16[64,512]{1,0:T(8,128)(2,1)S(1)}, u32[]{:S(2)}, u32[]{:S(2)}) collective-permute-start(bf16[64,512]{1,0:T(8,128)(2,1)} %convolution_convert_fusion.2), channel_id=1, source_target_pairs={{0,1016},{8,0},{16,8},{24,16},{32,24},{40,32},{48,40},{56,48},{64,... | collective-permute-start | bytes 196616 | tf_op jit(solution)/shard_map/ppermute | solution.py:45
  144.2 2.2 %collective-permute-start.6 = (bf16[64,512]{1,0:T(8,128)(2,1)}, bf16[64,512]{1,0:T(8,128)(2,1)S(1)}, u32[]{:S(2)}, u32[]{:S(2)}) collective-permute-start(bf16[64,512]{1,0:T(8,128)(2,1)} %convolution_convert_fusion.1), channel_id=1, source_target_pairs={{0,8},{8,16},{16,24},{24,32},{32,40},{40,48},{48,56},{56,64},{64,7... | collective-permute-start | bytes 196616 | tf_op jit(solution)/shard_map/ppermute | solution.py:45
  146.4 1.9 %collective-permute-start.7 = (bf16[64,512]{1,0:T(8,128)(2,1)S(1)}, bf16[64,512]{1,0:T(8,128)(2,1)S(1)}, u32[]{:S(2)}, u32[]{:S(2)}) collective-permute-start(bf16[64,512]{1,0:T(8,128)(2,1)S(1)} %convolution_convert_fusion), channel_id=1, source_target_pairs={{0,16},{8,24},{16,32},{24,40},{32,48},{40,56},{48,64},{56,72},{64,... | collective-permute-start | bytes 196616 | tf_op jit(solution)/shard_map/ppermute | solution.py:45
  148.6 4.2 %collective-permute-done.6 = bf16[64,512]{1,0:T(8,128)(2,1)S(1)} collective-permute-done((bf16[64,512]{1,0:T(8,128)(2,1)}, bf16[64,512]{1,0:T(8,128)(2,1)S(1)}, u32[]{:S(2)}, u32[]{:S(2)}) %collective-permute-start.6) | collective-permute-done | bytes 65568 | tf_op jit(solution)/shard_map/ppermute | solution.py:45
  152.8 2.9 %collective-permute-done.7 = bf16[64,512]{1,0:T(8,128)(2,1)S(1)} collective-permute-done((bf16[64,512]{1,0:T(8,128)(2,1)S(1)}, bf16[64,512]{1,0:T(8,128)(2,1)S(1)}, u32[]{:S(2)}, u32[]{:S(2)}) %collective-permute-start.7) | collective-permute-done | bytes 65568 | tf_op jit(solution)/shard_map/ppermute | solution.py:45
  155.7 0.9 fusion.21
  156.7 0.8 copy.27
  (46 shorter events, 5.4 us)
Async XLA Ops:
  0.6 39.9 %collective-permute-start = (bf16[64,512]{1,0:T(8,128)(2,1)}, bf16[64,512]{1,0:T(8,128)(2,1)S(1)}, u32[]{:S(2)}, u32[]{:S(2)}) collective-permute-start(bf16[64,512]{1,0:T(8,128)(2,1)} %bitcast.99), channel_id=1, source_target_pairs={{0,16},{8,24},{16,32},{24,40},{32,48},{40,56},{48,64},{56,72},{64,... | collective-permute-start | bytes 196616 | tf_op jit(solution)/shard_map/ppermute | solution.py:45
  5.7 35.1 %collective-permute-start.2 = (bf16[64,512]{1,0:T(8,128)(2,1)}, bf16[64,512]{1,0:T(8,128)(2,1)S(1)}, u32[]{:S(2)}, u32[]{:S(2)}) collective-permute-start(bf16[64,512]{1,0:T(8,128)(2,1)} %bitcast.100), channel_id=1, source_target_pairs={{0,1016},{8,0},{16,8},{24,16},{32,24},{40,32},{48,40},{56,48},{64,... | collective-permute-start | bytes 196616 | tf_op jit(solution)/shard_map/ppermute | solution.py:45
  24.2 16.8 %collective-permute-start.3 = (bf16[64,512]{1,0:T(8,128)(2,1)}, bf16[64,512]{1,0:T(8,128)(2,1)S(1)}, u32[]{:S(2)}, u32[]{:S(2)}) collective-permute-start(bf16[64,512]{1,0:T(8,128)(2,1)} %bitcast.101), channel_id=1, source_target_pairs={{0,1008},{8,1016},{16,0},{24,8},{32,16},{40,24},{48,32},{56,40},{6... | collective-permute-start | bytes 196616 | tf_op jit(solution)/shard_map/ppermute | solution.py:45
  28.5 12.9 %collective-permute-start.1 = (bf16[64,512]{1,0:T(8,128)(2,1)}, bf16[64,512]{1,0:T(8,128)(2,1)S(1)}, u32[]{:S(2)}, u32[]{:S(2)}) collective-permute-start(bf16[64,512]{1,0:T(8,128)(2,1)} %bitcast.102), channel_id=1, source_target_pairs={{0,8},{8,16},{16,24},{24,32},{32,40},{40,48},{48,56},{56,64},{64,7... | collective-permute-start | bytes 196616 | tf_op jit(solution)/shard_map/ppermute | solution.py:45
  31.9 5.0 %copy-start.4 = (bf16[512,64]{0,1:T(8,128)(2,1)S(1)}, bf16[512,64]{0,1:T(8,128)(2,1)}, u32[]{:S(2)}) copy-start(bf16[512,64]{0,1:T(8,128)(2,1)} %param.6) | copy-start | bytes 196612
  36.8 3.7 %copy-start = (bf16[5,512,512]{2,1,0:T(8,128)(2,1)S(1)}, bf16[5,512,512]{2,1,0:T(8,128)(2,1)}, u32[]{:S(2)}) copy-start(bf16[5,512,512]{2,1,0:T(8,128)(2,1)} %shard_map.93) | copy-start | bytes 7864324
  40.5 7.9 %copy-start.2 = (bf16[64,512]{1,0:T(8,128)(2,1)S(1)}, bf16[64,512]{1,0:T(8,128)(2,1)}, u32[]{:S(2)}) copy-start(bf16[64,512]{1,0:T(8,128)(2,1)} %param.9) | copy-start | bytes 196612
  40.5 8.0 %copy-start.1 = (bf16[64,512]{1,0:T(8,128)(2,1)S(1)}, bf16[64,512]{1,0:T(8,128)(2,1)}, u32[]{:S(2)}) copy-start(bf16[64,512]{1,0:T(8,128)(2,1)} %param.10) | copy-start | bytes 196612
  40.8 7.9 %copy-start.5 = (bf16[512,64]{0,1:T(8,128)(2,1)S(1)}, bf16[512,64]{0,1:T(8,128)(2,1)}, u32[]{:S(2)}) copy-start(bf16[512,64]{0,1:T(8,128)(2,1)} %param.6) | copy-start | bytes 196612
  42.5 15.3 %all-to-all-start.1 = ((bf16[8,64,512]{2,1,0:T(8,128)(2,1)}), bf16[8,64,512]{2,1,0:T(8,128)(2,1)S(1)}, u32[]{:S(2)}, u32[]{:S(2)}) async-start(bf16[8,64,512]{2,1,0:T(8,128)(2,1)} %broadcast_in_dim.21), calls=%async_computation.1 | async-start | bytes 1048576 | tf_op jit(solution)/shard_map/all_to_all | solution.py:49
  48.7 25.5 %copy-start.6 = (bf16[512,64]{0,1:T(8,128)(2,1)S(1)}, bf16[512,64]{0,1:T(8,128)(2,1)}, u32[]{:S(2)}) copy-start(bf16[512,64]{0,1:T(8,128)(2,1)} %param.11) | copy-start | bytes 196612
  85.9 15.2 %all-to-all-start.2 = ((bf16[8,64,512]{2,1,0:T(8,128)(2,1)}), bf16[8,64,512]{2,1,0:T(8,128)(2,1)S(1)}, u32[]{:S(2)}, u32[]{:S(2)}) async-start(bf16[8,64,512]{2,1,0:T(8,128)(2,1)} %broadcast_in_dim.22), calls=%async_computation.2 | async-start | bytes 1048576 | tf_op jit(solution)/shard_map/all_to_all | solution.py:49
  101.8 20.0 %all-to-all-start.4 = ((bf16[16,8,1024]{2,1,0:T(8,128)(2,1)}), bf16[16,8,1024]{2,1,0:T(8,128)(2,1)S(1)}, u32[]{:S(2)}, u32[]{:S(2)}) async-start(bf16[16,8,1024]{2,1,0:T(8,128)(2,1)} %broadcast_in_dim.23), calls=%async_computation.4 | async-start | bytes 524288 | tf_op jit(solution)/shard_map/all_to_all | solution.py:49
  109.0 46.7 %copy-start.3 = (bf16[64,512]{1,0:T(8,128)(2,1)S(1)}, bf16[64,512]{1,0:T(8,128)(2,1)}, u32[]{:S(2)}) copy-start(bf16[64,512]{1,0:T(8,128)(2,1)} %param.9) | copy-start | bytes 196612
  122.5 34.0 %all-to-all-start.5 = ((f32[64,8,128]{2,1,0:T(8,128)}), f32[64,8,128]{2,1,0:T(8,128)S(1)}, u32[]{:S(2)}, u32[]{:S(2)}) async-start(f32[64,8,128]{2,1,0:T(8,128)} %bitcast.96), calls=%async_computation.5 | async-start | bytes 524288 | tf_op jit(solution)/shard_map/all_to_all | solution.py:49
  133.4 15.2 %collective-permute-start.4 = (bf16[64,512]{1,0:T(8,128)(2,1)}, bf16[64,512]{1,0:T(8,128)(2,1)S(1)}, u32[]{:S(2)}, u32[]{:S(2)}) collective-permute-start(bf16[64,512]{1,0:T(8,128)(2,1)} %convolution_convert_fusion.3), channel_id=1, source_target_pairs={{0,1008},{8,1016},{16,0},{24,8},{32,16},{40,24},{48,32},{56,40},{6... | collective-permute-start | bytes 196616 | tf_op jit(solution)/shard_map/ppermute | solution.py:45
  141.1 7.5 %collective-permute-start.5 = (bf16[64,512]{1,0:T(8,128)(2,1)}, bf16[64,512]{1,0:T(8,128)(2,1)S(1)}, u32[]{:S(2)}, u32[]{:S(2)}) collective-permute-start(bf16[64,512]{1,0:T(8,128)(2,1)} %convolution_convert_fusion.2), channel_id=1, source_target_pairs={{0,1016},{8,0},{16,8},{24,16},{32,24},{40,32},{48,40},{56,48},{64,... | collective-permute-start | bytes 196616 | tf_op jit(solution)/shard_map/ppermute | solution.py:45
  144.2 8.5 %collective-permute-start.6 = (bf16[64,512]{1,0:T(8,128)(2,1)}, bf16[64,512]{1,0:T(8,128)(2,1)S(1)}, u32[]{:S(2)}, u32[]{:S(2)}) collective-permute-start(bf16[64,512]{1,0:T(8,128)(2,1)} %convolution_convert_fusion.1), channel_id=1, source_target_pairs={{0,8},{8,16},{16,24},{24,32},{32,40},{40,48},{48,56},{56,64},{64,7... | collective-permute-start | bytes 196616 | tf_op jit(solution)/shard_map/ppermute | solution.py:45
  146.4 9.2 %collective-permute-start.7 = (bf16[64,512]{1,0:T(8,128)(2,1)S(1)}, bf16[64,512]{1,0:T(8,128)(2,1)S(1)}, u32[]{:S(2)}, u32[]{:S(2)}) collective-permute-start(bf16[64,512]{1,0:T(8,128)(2,1)S(1)} %convolution_convert_fusion), channel_id=1, source_target_pairs={{0,16},{8,24},{16,32},{24,40},{32,48},{40,56},{48,64},{56,72},{64,... | collective-permute-start | bytes 196616 | tf_op jit(solution)/shard_map/ppermute | solution.py:45

commit v2 on v1

v2 whole, which is shorter than its diff:
```python
import math

import jax
import jax.numpy as jnp
from jax import lax
from jax.experimental import pallas as pl
from jax.experimental.pallas import tpu as pltpu
from jax.sharding import Mesh
from jax.sharding import PartitionSpec as P

ROW = ("z", "y")
COL = ("x", "core")
TILE = 128
LAST = (((1,), (1,)), ((), ()))
FIRST = (((0,), (0,)), ((), ()))
PLAIN = (((1,), (0,)), ((), ()))
VMEM = pl.BlockSpec(memory_space=pltpu.VMEM)
SMEM = pl.BlockSpec(memory_space=pltpu.SMEM)
ANY = pl.BlockSpec(memory_space=pl.ANY)
BF16 = jnp.bfloat16
F32 = jnp.float32


def fetch(sources, buffer, arrived):
    copies = [
        pltpu.make_async_copy(source, buffer.at[slot], arrived.at[slot])
        for slot, source in enumerate(sources)
    ]
    for copy in copies:
        copy.start()
    return copies


def slots(count, shape):
    return [pltpu.VMEM((count, *shape), BF16), pltpu.SemaphoreType.DMA((count,))]


def dot(a, b, dims):
    return lax.dot_general(a, b, dims, preferred_element_type=F32)


def local_call(kernel, out_shape, in_specs, args, flops, scratch=()):
    outs = jax.tree.leaves(out_shape)
    moved = sum(a.size * a.dtype.itemsize for a in (*args, *outs))
    return pl.pallas_call(
        kernel,
        out_shape=out_shape,
        in_specs=in_specs,
        out_specs=jax.tree.map(lambda _: VMEM, out_shape),
        scratch_shapes=list(scratch),
        compiler_params=pltpu.CompilerParams(vmem_limit_bytes=24 * 1024 * 1024),
        cost_estimate=pl.CostEstimate(flops=flops, bytes_accessed=moved, transcendentals=0),
    )(*args)


def prep_kernel(own_ref, wself_ref, wneigh_ref, out_ref, buffer, arrived):
    groups, width, _ = out_ref.shape
    nodes = own_ref.shape[1]
    for copy in fetch((own_ref, wself_ref, wneigh_ref), buffer, arrived):
        copy.wait()
    own, wself, wneigh = buffer[0], buffer[1], buffer[2]
    for group in range(groups):
        out_ref[group, :, :nodes] = own
        columns = slice(group * width, (group + 1) * width)
        out_ref[group, :, nodes:] = jnp.concatenate([wself[:, columns], wneigh[:, columns]], axis=1)


def mask_kernel(
    mask_ref, own_ref, adj_ref, _, weighted_ref, base_ref, inverse_ref, buffer, arrived, near, here
):
    bands, nodes, _ = adj_ref.shape
    reach = (bands - 1) // 2
    width = own_ref.shape[0]
    (own_copy,) = fetch([own_ref], near, here)
    copies = fetch([adj_ref.at[band] for band in range(bands)], buffer, arrived)
    ones = jnp.ones((16, nodes), BF16)
    degree = jnp.zeros((16, nodes), F32)
    for band in range(bands):
        copies[band].wait()
        for row in range(nodes // TILE):
            for column in range(nodes // TILE):
                keep = mask_ref[row, column, band].astype(F32).astype(BF16)
                rows, columns = pl.ds(row * TILE, TILE), pl.ds(column * TILE, TILE)
                weighted_ref[band, rows, columns] = buffer[band, rows, columns] * keep
        if band == reach:
            own_copy.wait()
            both = dot(jnp.concatenate([near[0], ones], axis=0), weighted_ref[band], LAST)
            base_ref[...] = both[:width]
            degree = degree + both[width:]
        else:
            degree = degree + dot(ones, weighted_ref[band], LAST)
    inverse_ref[...] = 1.0 / jnp.maximum(degree[:8], 1.0)


def mean_kernel(*refs):
    *near_refs, weighted_ref, base_ref, inverse_ref, out_ref, buffer, arrived = refs
    copies = fetch(near_refs, buffer, arrived)
    bands = weighted_ref.shape[0]
    reach = (bands - 1) // 2
    total = base_ref[...]
    for slot, band in enumerate([b for b in range(bands) if b != reach]):
        copies[slot].wait()
        total = total + dot(buffer[slot], weighted_ref[band], LAST)
    mean = (total * inverse_ref[0:1, :]).astype(BF16)
    for copy in range(out_ref.shape[0]):
        out_ref[copy] = mean


def act_kernel(scale, early_ref, means_ref, cot_ref, act_ref, grad_ref, partial_ref):
    groups, width, nodes = means_ref.shape
    total = groups * width
    feats = early_ref[:, :, :nodes].reshape(total, nodes)
    columns = early_ref[:, :, nodes:].reshape(total, 2 * width)
    means = means_ref[...].reshape(total, nodes)
    preact = dot(columns, feats, FIRST)[:width] + dot(columns, means, FIRST)[width:]
    sigmoid_z = 1.0 / (1.0 + jnp.exp(-preact))
    act_ref[...] = (preact * sigmoid_z).astype(BF16)
    slope = sigmoid_z * (1.0 + preact * (1.0 - sigmoid_z))
    grad = (cot_ref[...].astype(F32) * slope).astype(BF16)
    grad_ref[...] = grad
    stacked = jnp.concatenate(
        [feats.reshape(groups, width, nodes), means.reshape(groups, width, nodes)], axis=1
    ).reshape(2 * total, nodes)
    partial = dot(grad, stacked, LAST) * scale
    rows = width // partial_ref.shape[0]
    for piece in range(partial_ref.shape[0]):
        part = partial[piece * rows : (piece + 1) * rows]
        partial_ref[piece] = jnp.concatenate([part[:, :total], part[:, total:]], axis=0).astype(BF16)


def sum_y_kernel(in_ref, *refs):
    out_ref = refs[-1]
    total = in_ref[0].astype(F32)
    for part in range(1, in_ref.shape[0]):
        total = total + in_ref[part].astype(F32)
    total = total.astype(BF16)
    for copy in range(out_ref.shape[0]):
        out_ref[copy] = total


def sum_z_kernel(groups, lines, in_ref, *refs):
    out_ref = refs[-1]
    total = in_ref[0].astype(F32)
    for part in range(1, in_ref.shape[0]):
        total = total + in_ref[part].astype(F32)
    rows, lanes = out_ref.shape[1:]
    per_row = total.shape[1] // lanes
    for group in range(groups):
        up, across = group // per_row, group % per_row
        share = total[up * rows : (up + 1) * rows, across * lanes : (across + 1) * lanes]
        for line in range(lines):
            out_ref[group * lines + line] = share.astype(BF16)


def final_kernel(in_ref, self_ref, neigh_ref):
    sources, rows, lanes = in_ref.shape
    turned = in_ref[...].astype(F32).reshape(sources * rows, lanes).T
    half = lanes // 2
    self_ref[...] = turned[:half]
    neigh_ref[...] = turned[half:]


def back_kernel(place_ref, wself_ref, wneigh_ref, *refs):
    parts = place_ref.shape[0]
    grad_refs, (weighted_ref, inverse_ref), outs = refs[:parts], refs[parts : parts + 2], refs[parts + 2 : -2]
    buffer, arrived = refs[-2:]
    copies = fetch(grad_refs, buffer, arrived)
    bands = weighted_ref.shape[0]
    reach = (bands - 1) // 2
    depth = grad_refs[0].shape[0]
    for part, grad_ref in enumerate(grad_refs):
        lanes = pl.ds(pl.multiple_of(place_ref[part] * depth, depth), depth)
        copies[part].wait()
        neigh_part = dot(wneigh_ref[:, lanes], buffer[part], PLAIN)
        self_part = dot(wself_ref[:, lanes], buffer[part], PLAIN)
        neigh = neigh_part if part == 0 else neigh + neigh_part
        stays = self_part if part == 0 else stays + self_part
    spread = (neigh * inverse_ref[0:1, :]).astype(BF16)
    term_refs, base_ref = outs[:-1], outs[-1]
    others = [b for b in range(bands) if b != reach]
    for term_ref, band in zip(term_refs, others):
        term_ref[...] = dot(spread, weighted_ref[band], PLAIN).astype(BF16)
    base_ref[...] = stays + dot(spread, weighted_ref[reach], PLAIN)


def from_behind(value, steps):
    count = lax.axis_size(ROW)
    pairs = [(source, (source + steps) % count) for source in range(count)]
    return lax.ppermute(value, ROW, pairs)


def around(value, steps):
    count = lax.axis_size("x")
    pairs = [(source, (source + steps) % count) for source in range(count)]
    return lax.ppermute(value, "x", pairs)


def exchange(chunks, axes):
    return lax.all_to_all(chunks, axes, 0, 0, tiled=True)


def body(features, adjacency, tile_mask, w_self, w_neigh, cotangent):
    own = features.T
    width, nodes = own.shape
    groups = lax.axis_size(COL)
    lines = lax.axis_size("y")
    planes = lax.axis_size("z")
    total = groups * width
    bands = tile_mask.shape[1]
    reach = (bands - 1) // 2
    offsets = [k for k in range(-reach, reach + 1) if k != 0]
    shape = jax.ShapeDtypeStruct

    out_columns = local_call(
        prep_kernel,
        shape((groups, width, nodes + 2 * width), BF16),
        [ANY] * 3,
        (own, w_self, w_neigh),
        adjacency.size // 8,
        slots(3, (width, nodes)),
    )
    early = exchange(out_columns, COL)
    neighbours = [from_behind(own, -k) for k in offsets]

    panel = (width, nodes)
    adj = adjacency.transpose(1, 0, 2)
    weighted, base, inverse = local_call(
        mask_kernel,
        (shape(adj.shape, BF16), shape(panel, F32), shape((8, nodes), F32)),
        [SMEM, ANY, ANY, ANY],
        (tile_mask.transpose(0, 2, 1), own, adj, early),
        2 * adj.size,
        slots(bands, (nodes, nodes)) + slots(1, panel),
    )
    copies = local_call(
        mean_kernel,
        shape((groups, *panel), BF16),
        [ANY] * len(offsets) + [VMEM] * 3,
        (*neighbours, weighted, base, inverse),
        2 * adj.size,
        slots(len(offsets), panel),
    )
    means = exchange(copies, COL)

    grad_scale = 1.0 / math.sqrt(lax.axis_size(ROW) * nodes)

    def act(*refs):
        act_kernel(grad_scale, *refs)

    activated, grad_preact, partial = local_call(
        act,
        (shape(panel, BF16), shape(panel, BF16), shape((lines, 2 * (width // lines), total), BF16)),
        [VMEM] * 3,
        (early, means, cotangent.T),
        2 * adj.size,
    )

    over_y = exchange(partial, "y")

    pair = lax.all_gather(grad_preact, "core", axis=0, tiled=True)
    sides = [pair] + [around(pair, k) for k in range(1, lax.axis_size("x"))]

    folded = local_call(
        sum_y_kernel,
        shape((planes, 2 * (width // lines), total), BF16),
        [VMEM] + [ANY] * len(sides),
        (over_y, *sides),
        adj.size,
    )
    over_z = exchange(folded, "z")

    places = lax.rem(
        lax.axis_index("x") - jnp.arange(len(sides), dtype=jnp.int32) + len(sides), len(sides)
    ).astype(jnp.int32)
    *terms, stays = local_call(
        back_kernel,
        (*[shape(panel, BF16)] * len(offsets), shape(panel, F32)),
        [SMEM, VMEM, VMEM] + [ANY] * len(sides) + [VMEM] * 2,
        (places, w_self, w_neigh, *sides, weighted, inverse),
        2 * adj.size,
        slots(len(sides), pair.shape),
    )
    arrived = [from_behind(term, k) for term, k in zip(terms, offsets)]

    def sum_z(*refs):
        sum_z_kernel(groups, lines, *refs)

    shares = local_call(
        sum_z,
        shape((groups * lines, width // lines, 2 * width), BF16),
        [VMEM] + [ANY] * len(arrived),
        (over_z, *arrived),
        adj.size,
    )
    gathered = exchange(shares, COL + ("y",))
    grad_self, grad_neigh = local_call(
        final_kernel,
        (shape((width, total), F32), shape((width, total), F32)),
        [VMEM],
        (gathered,),
        adj.size,
    )
    for term in arrived:
        stays = stays + term.astype(F32)
    return (activated.T, stays.astype(BF16).T, grad_self, grad_neigh)


def solution(mesh):
    rows, columns = mesh.devices.shape
    lines = math.gcd(rows, 8)
    cores = math.gcd(columns, 2)
    fine = Mesh(
        mesh.devices.reshape(rows // lines, lines, columns // cores, cores), ROW + COL
    )
    return jax.shard_map(
        body,
        mesh=fine,
        in_specs=(
            P(ROW, COL),
            P(ROW, None, None),
            P(ROW, None, None),
            P(COL, None),
            P(COL, None),
            P(ROW, COL),
        ),
        out_specs=(P(ROW, COL), P(ROW, COL), P(COL, None), P(COL, None)),
        check_vma=False,
    )
```

time: 160 us -> 134 us (0.84)
  waiting for transfers between devices: 34.9 us -> 19.4 us
  matrix products: 8.2 us -> 0 us
  blocking collectives: 25.4 us -> 17.5 us
  Pallas kernels: 4.96 us -> 10.4 us
  starting transfers between devices: 73.8 us -> 76.3 us
  other arithmetic: 3.33 us -> 1.59 us
    all_to_all x4, waiting for transfers between devices: 27.8 us -> 8.38 us  [exchange(): return lax.all_to_all(chunks, axes, 0, 0, tiled=True)]
    ppermute x8, starting transfers between devices: 44.8 us -> 32.4 us  [from_behind(): return lax.ppermute(value, ROW, pairs)]
    all_to_all x2 -> x1, blocking collectives: 25.4 us -> 14.9 us  [exchange(): return lax.all_to_all(chunks, axes, 0, 0, tiled=True)]
    ppermute x0 -> x3, starting transfers between devices: none -> 8.4 us  [around(): return lax.ppermute(value, 'x', pairs)]
    dot_general x15 -> x0, matrix products: 8.2 us -> none  [the longest x4 2.71 us: body(): jnp.dot(spread, weighted[band_reach + k], **DOT).astype(jnp.bfloat16)]
    all_to_all x4, starting transfers between devices: 29.1 us -> 35.5 us  [exchange(): return lax.all_to_all(chunks, axes, 0, 0, tiled=True)]
    pallas_call x1 -> x8, Pallas kernels: 4.96 us -> 10.4 us  [local_call(): pl.pallas_call(kernel, out_shape=out_shape, in_specs=in_specs, out_specs=...]
    ppermute x0 -> x3, waiting for transfers between devices: none -> 4.67 us  [around(): return lax.ppermute(value, 'x', pairs)]
  transfers between devices with their start and end apart: 12 -> 15, of which waited for: 5 -> 5; matrix products, arithmetic and copies ran while one was open for 7% -> 1% of each run, Pallas kernels for 3% -> 3%
where the time goes in v2:
time: 134 us; the launch traced here: 133 us
  starting transfers between devices  76.3 us (57%)
  waiting for transfers between devices  19.4 us (14%)
  blocking collectives  17.5 us (13%)
  Pallas kernels  10.4 us (8%)
  local copies, waits for them, and re-layouts  6.45 us (5%)
  other arithmetic  1.59 us (1%)
    all_to_all x4, starting transfers between devices, exchange(): return lax.all_to_all(chunks, axes, 0, 0, tiled=True)  35.5 us
    ppermute x8, starting transfers between devices, from_behind(): return lax.ppermute(value, ROW, pairs)  32.4 us
    all_to_all x1, blocking collectives, exchange(): return lax.all_to_all(chunks, axes, 0, 0, tiled=True)  14.9 us
    pallas_call x8, Pallas kernels, local_call(): pl.pallas_call(kernel, out_shape=out_shape, in_specs=in_specs, out_specs=...  10.4 us
    ppermute x3, starting transfers between devices, around(): return lax.ppermute(value, 'x', pairs)  8.4 us
    all_to_all x4, waiting for transfers between devices, exchange(): return lax.all_to_all(chunks, axes, 0, 0, tiled=True)  8.38 us
    unnamed x20, local copies, waits for them, and re-layouts  6.45 us
    ppermute x8, waiting for transfers between devices, from_behind(): return lax.ppermute(value, ROW, pairs)  6.39 us
  transfers between devices with their start and end apart: 15, of which 5 were waited for; matrix products, arithmetic and copies ran while one was open for 1% of the time, Pallas kernels for 3%

profile of v2, /device:TPU:1, one launch (start us, length us, event | category | flops | bytes accessed | tf_op | source)
XLA Modules:
  0.0 132.7 jit_solution(6181639170896214517)
XLA Ops:
  0.6 0.8 copy-done.1
  1.5 0.8 copy-done.3
  2.3 0.8 copy-done.5
  3.2 1.2 shard_map.93
  4.4 17.6 %all-to-all-start = ((bf16[8,64,640]{2,1,0:T(8,128)(2,1)}), bf16[8,64,640]{2,1,0:T(8,128)(2,1)S(1)}, u32[]{:S(2)}, u32[]{:S(2)}) async-start(bf16[8,64,640]{2,1,0:T(8,128)(2,1)} %shard_map.93), calls=%async_computation | async-start | bytes 1310720 | tf_op jit(solution)/shard_map/all_to_all | solution.py:199
  22.0 1.9 %collective-permute-start = (bf16[64,512]{1,0:T(8,128)(2,1)}, bf16[64,512]{1,0:T(8,128)(2,1)S(1)}, u32[]{:S(2)}, u32[]{:S(2)}) collective-permute-start(bf16[64,512]{1,0:T(8,128)(2,1)} %bitcast.8), channel_id=1, source_target_pairs={{0,16},{8,24},{16,32},{24,40},{32,48},{40,56},{48,64},{56,72},{64,... | collective-permute-start | bytes 196616 | tf_op jit(solution)/shard_map/ppermute | solution.py:189
  23.9 1.9 %collective-permute-start.1 = (bf16[64,512]{1,0:T(8,128)(2,1)}, bf16[64,512]{1,0:T(8,128)(2,1)S(1)}, u32[]{:S(2)}, u32[]{:S(2)}) collective-permute-start(bf16[64,512]{1,0:T(8,128)(2,1)} %bitcast.9), channel_id=1, source_target_pairs={{0,8},{8,16},{16,24},{24,32},{32,40},{40,48},{48,56},{56,64},{64,7... | collective-permute-start | bytes 196616 | tf_op jit(solution)/shard_map/ppermute | solution.py:189
  25.8 9.1 %collective-permute-start.2 = (bf16[64,512]{1,0:T(8,128)(2,1)}, bf16[64,512]{1,0:T(8,128)(2,1)S(1)}, u32[]{:S(2)}, u32[]{:S(2)}) collective-permute-start(bf16[64,512]{1,0:T(8,128)(2,1)} %bitcast.10), channel_id=1, source_target_pairs={{0,1016},{8,0},{16,8},{24,16},{32,24},{40,32},{48,40},{56,48},{64,... | collective-permute-start | bytes 196616 | tf_op jit(solution)/shard_map/ppermute | solution.py:189
  34.9 4.3 %collective-permute-start.3 = (bf16[64,512]{1,0:T(8,128)(2,1)}, bf16[64,512]{1,0:T(8,128)(2,1)S(1)}, u32[]{:S(2)}, u32[]{:S(2)}) collective-permute-start(bf16[64,512]{1,0:T(8,128)(2,1)} %bitcast.11), channel_id=1, source_target_pairs={{0,1008},{8,1016},{16,0},{24,8},{32,16},{40,24},{48,32},{56,40},{6... | collective-permute-start | bytes 196616 | tf_op jit(solution)/shard_map/ppermute | solution.py:189
  39.2 1.7 %copy-done = bf16[512,5,512]{2,0,1:T(8,128)(2,1)S(1)} copy-done((bf16[512,5,512]{2,0,1:T(8,128)(2,1)S(1)}, bf16[512,5,512]{2,0,1:T(8,128)(2,1)}, u32[]{:S(2)}) %copy-start) | copy-done | bytes 2621464
  40.9 0.8 copy-done.2
  42.4 2.3 %shard_map.94 = (bf16[5,512,512]{2,1,0:T(8,128)(2,1)S(1)}, f32[64,512]{1,0:T(8,128)S(1)}, f32[8,512]{1,0:T(8,128)S(1)}) custom-call(s32[4,4,5]{2,1,0:T(4,128)S(1)} %bitcast.15, bf16[64,512]{1,0:T(8,128)(2,1)S(1)} %bitcast.13, bf16[5,512,512]{2,1,0:T(8,128)(2,1)S(1)} %bitcast.7, bf16[8,64,640]{2,1,0:T(8,128)(2,1)S(1)} %all-to-all-done._.refs_0_), custom_call_target="tpu_custom_call" | custom-call | flops 2621440 | bytes 6111552 | tf_op jit(solution)/shard_map/pallas_call | solution.py:45
  44.8 1.2 shard_map.95
  46.0 14.9 %all_to_all.25.refs_1_ = bf16[8,64,512]{2,1,0:T(8,128)(2,1)S(1)} all-to-all(bf16[8,64,512]{2,1,0:T(8,128)(2,1)S(1)} %shard_map.95), channel_id=1, replica_groups=mesh['z'=16,'y'=8,'x'=4,'core'=2] {'x','core'}, dimensions={0} | all-to-all | bytes 1048576 | tf_op jit(solution)/shard_map/all_to_all | solution.py:199
  61.0 1.4 %shard_map.96 = (bf16[64,512]{1,0:T(8,128)(2,1)}, bf16[64,512]{1,0:T(8,128)(2,1)S(1)}, bf16[8,16,512]{2,1,0:T(8,128)(2,1)}) custom-call(bf16[8,64,640]{2,1,0:T(8,128)(2,1)S(1)} %all-to-all-done._.refs_0_, bf16[8,64,512]{2,1,0:T(8,128)(2,1)S(1)} %all_to_all.25.refs_1_, bf16[64,512]{1,0:T(8,128)(2,1)S(1)} %bitcast.14), custom_call_target="tpu_custom_call" | custom-call | flops 2621440 | bytes 1507328 | tf_op jit(solution)/shard_map/pallas_call | solution.py:45
  62.3 3.4 %all-to-all-start.2 = ((bf16[8,16,512]{2,1,0:T(8,128)(2,1)}), bf16[8,16,512]{2,1,0:T(8,128)(2,1)S(1)}, u32[]{:S(2)}, u32[]{:S(2)}) async-start(bf16[8,16,512]{2,1,0:T(8,128)(2,1)} %get-tuple-element.27), calls=%async_computation.2 | async-start | bytes 262144 | tf_op jit(solution)/shard_map/all_to_all | solution.py:199
  65.7 2.6 %all_gather.3.refs_0_ = bf16[128,512]{1,0:T(8,128)(2,1)S(1)} all-gather(bf16[64,512]{1,0:T(8,128)(2,1)S(1)} %get-tuple-element.21), channel_id=1, replica_groups=mesh['z'=16,'y'=8,'x'=4,'core'=2] {'core'}, dimensions={0}, use_global_device_ids=true | all-gather | bytes 196608 | tf_op jit(solution)/shard_map/all_gather | solution.py:260
  68.3 2.2 %collective-permute-start.4 = (bf16[128,512]{1,0:T(8,128)(2,1)S(1)}, bf16[128,512]{1,0:T(8,128)(2,1)S(1)}, u32[]{:S(2)}, u32[]{:S(2)}) collective-permute-start(bf16[128,512]{1,0:T(8,128)(2,1)S(1)} %all_gather.3.refs_0_), channel_id=1, source_target_pairs={{0,2},{2,4},{4,6},{6,0},{1,3},{3,5},{5,7},{7,1},{8,10},{10,12},{12... | collective-permute-start | bytes 393224 | tf_op jit(solution)/shard_map/ppermute | solution.py:195
  70.5 3.7 %collective-permute-start.5 = (bf16[128,512]{1,0:T(8,128)(2,1)S(1)}, bf16[128,512]{1,0:T(8,128)(2,1)S(1)}, u32[]{:S(2)}, u32[]{:S(2)}) collective-permute-start(bf16[128,512]{1,0:T(8,128)(2,1)S(1)} %all_gather.3.refs_0_), channel_id=1, source_target_pairs={{0,4},{2,6},{4,0},{6,2},{1,5},{3,7},{5,1},{7,3},{8,12},{10,14},{12... | collective-permute-start | bytes 393224 | tf_op jit(solution)/shard_map/ppermute | solution.py:195
  74.2 2.5 %collective-permute-start.6 = (bf16[128,512]{1,0:T(8,128)(2,1)S(1)}, bf16[128,512]{1,0:T(8,128)(2,1)S(1)}, u32[]{:S(2)}, u32[]{:S(2)}) collective-permute-start(bf16[128,512]{1,0:T(8,128)(2,1)S(1)} %all_gather.3.refs_0_), channel_id=1, source_target_pairs={{0,6},{2,0},{4,2},{6,4},{1,7},{3,1},{5,3},{7,5},{8,14},{10,8},{12,... | collective-permute-start | bytes 393224 | tf_op jit(solution)/shard_map/ppermute | solution.py:195
  76.8 1.7 %collective-permute-done.5.refs_2_ = bf16[128,512]{1,0:T(8,128)(2,1)S(1)} collective-permute-done((bf16[128,512]{1,0:T(8,128)(2,1)S(1)}, bf16[128,512]{1,0:T(8,128)(2,1)S(1)}, u32[]{:S(2)}, u32[]{:S(2)}) %collective-permute-start.5) | collective-permute-done | bytes 131104 | tf_op jit(solution)/shard_map/ppermute | solution.py:195
  78.4 3.0 %collective-permute-done.6.refs_3_ = bf16[128,512]{1,0:T(8,128)(2,1)S(1)} collective-permute-done((bf16[128,512]{1,0:T(8,128)(2,1)S(1)}, bf16[128,512]{1,0:T(8,128)(2,1)S(1)}, u32[]{:S(2)}, u32[]{:S(2)}) %collective-permute-start.6) | collective-permute-done | bytes 131104 | tf_op jit(solution)/shard_map/ppermute | solution.py:195
  82.2 6.3 %all-to-all-start.3 = ((bf16[16,16,512]{2,1,0:T(8,128)(2,1)}), bf16[16,16,512]{2,1,0:T(8,128)(2,1)S(1)}, u32[]{:S(2)}, u32[]{:S(2)}) async-start(bf16[16,16,512]{2,1,0:T(8,128)(2,1)} %shard_map.98), calls=%async_computation.3 | async-start | bytes 524288 | tf_op jit(solution)/shard_map/all_to_all | solution.py:199
  88.5 2.1 %shard_map.97 = (bf16[64,512]{1,0:T(8,128)(2,1)S(1)}, bf16[64,512]{1,0:T(8,128)(2,1)S(1)}, bf16[64,512]{1,0:T(8,128)(2,1)S(1)}, bf16[64,512]{1,0:T(8,128)(2,1)S(1)}, f32[64,512]{1,0:T(8,128)S(1)}) custom-call(s32[4]{0:T(128)S(1)} %compare_select_fusion.place_ref, bf16[64,512]{1,0:T(8,128)(2,1)S(1)} %copy-done.4, bf16[64,512]{1,0:T(8,128)(2,1)S(1)} %copy-done.6, ...), custom_call_target="tpu_custom_call" | custom-call | flops 2621440 | bytes 3686416 | tf_op jit(solution)/shard_map/pallas_call | solution.py:45
  91.3 4.5 %collective-permute-start.10 = (bf16[64,512]{1,0:T(8,128)(2,1)S(1)}, bf16[64,512]{1,0:T(8,128)(2,1)S(1)}, u32[]{:S(2)}, u32[]{:S(2)}) collective-permute-start(bf16[64,512]{1,0:T(8,128)(2,1)S(1)} %get-tuple-element.26), channel_id=1, source_target_pairs={{0,16},{8,24},{16,32},{24,40},{32,48},{40,56},{48,64},{56,72},{64,... | collective-permute-start | bytes 196616 | tf_op jit(solution)/shard_map/ppermute | solution.py:189
  95.8 5.4 %collective-permute-start.7 = (bf16[64,512]{1,0:T(8,128)(2,1)S(1)}, bf16[64,512]{1,0:T(8,128)(2,1)S(1)}, u32[]{:S(2)}, u32[]{:S(2)}) collective-permute-start(bf16[64,512]{1,0:T(8,128)(2,1)S(1)} %get-tuple-element.23), channel_id=1, source_target_pairs={{0,1008},{8,1016},{16,0},{24,8},{32,16},{40,24},{48,32},{56,40},{6... | collective-permute-start | bytes 196616 | tf_op jit(solution)/shard_map/ppermute | solution.py:189
  101.2 3.4 %collective-permute-start.8 = (bf16[64,512]{1,0:T(8,128)(2,1)S(1)}, bf16[64,512]{1,0:T(8,128)(2,1)S(1)}, u32[]{:S(2)}, u32[]{:S(2)}) collective-permute-start(bf16[64,512]{1,0:T(8,128)(2,1)S(1)} %get-tuple-element.24), channel_id=1, source_target_pairs={{0,1016},{8,0},{16,8},{24,16},{32,24},{40,32},{48,40},{56,48},{64,... | collective-permute-start | bytes 196616 | tf_op jit(solution)/shard_map/ppermute | solution.py:189
  104.6 1.9 %collective-permute-start.9 = (bf16[64,512]{1,0:T(8,128)(2,1)S(1)}, bf16[64,512]{1,0:T(8,128)(2,1)S(1)}, u32[]{:S(2)}, u32[]{:S(2)}) collective-permute-start(bf16[64,512]{1,0:T(8,128)(2,1)S(1)} %get-tuple-element.25), channel_id=1, source_target_pairs={{0,8},{8,16},{16,24},{24,32},{32,40},{40,48},{48,56},{56,64},{64,7... | collective-permute-start | bytes 196616 | tf_op jit(solution)/shard_map/ppermute | solution.py:189
  107.3 5.7 %collective-permute-done.9.refs_3_ = bf16[64,512]{1,0:T(8,128)(2,1)S(1)} collective-permute-done((bf16[64,512]{1,0:T(8,128)(2,1)S(1)}, bf16[64,512]{1,0:T(8,128)(2,1)S(1)}, u32[]{:S(2)}, u32[]{:S(2)}) %collective-permute-start.9) | collective-permute-done | bytes 65568 | tf_op jit(solution)/shard_map/ppermute | solution.py:189
  113.6 8.3 %all-to-all-start.4 = ((bf16[64,8,128]{2,1,0:T(8,128)(2,1)}), bf16[64,8,128]{2,1,0:T(8,128)(2,1)S(1)}, u32[]{:S(2)}, u32[]{:S(2)}) async-start(bf16[64,8,128]{2,1,0:T(8,128)(2,1)} %shard_map.99), calls=%async_computation.4 | async-start | bytes 262144 | tf_op jit(solution)/shard_map/all_to_all | solution.py:199
  121.9 1.6 %fusion = bf16[512,64]{0,1:T(8,128)(2,1)} fusion(bf16[64,512]{1,0:T(8,128)(2,1)S(1)} %collective-permute-done.10.refs_4_, bf16[64,512]{1,0:T(8,128)(2,1)S(1)} %collective-permute-done.9.refs_3_, bf16[64,512]{1,0:T(8,128)(2,1)S(1)} %collective-permute-done.8.refs_2_, f32[64,512]{1,0:T(8,128)} %copy-done.7, bf16[64,512]{1,0:T(8,128)(2,1)S(1)} %collective-permute-done.7.refs_1_), kind=kLoop, calls=%fused_computation.1 | loop fusion | flops 294912 | bytes 458752 | tf_op jit(solution)/shard_map/transpose | solution.py:305
  123.5 8.4 %all-to-all-done.4.in_ref = bf16[64,8,128]{2,1,0:T(8,128)(2,1)S(1)} async-done(((bf16[64,8,128]{2,1,0:T(8,128)(2,1)}), bf16[64,8,128]{2,1,0:T(8,128)(2,1)S(1)}, u32[]{:S(2)}, u32[]{:S(2)}) %all-to-all-start.4) | async-done | bytes 131104 | tf_op jit(solution)/shard_map/all_to_all | solution.py:199
  (30 shorter events, 4.3 us)
Async XLA Ops:
  0.6 0.8 copy-start.1
  1.5 0.8 copy-start.3
  2.3 0.8 copy-start.5
  4.4 34.8 %all-to-all-start = ((bf16[8,64,640]{2,1,0:T(8,128)(2,1)}), bf16[8,64,640]{2,1,0:T(8,128)(2,1)S(1)}, u32[]{:S(2)}, u32[]{:S(2)}) async-start(bf16[8,64,640]{2,1,0:T(8,128)(2,1)} %shard_map.93), calls=%async_computation | async-start | bytes 1310720 | tf_op jit(solution)/shard_map/all_to_all | solution.py:199
  22.0 22.8 %collective-permute-start = (bf16[64,512]{1,0:T(8,128)(2,1)}, bf16[64,512]{1,0:T(8,128)(2,1)S(1)}, u32[]{:S(2)}, u32[]{:S(2)}) collective-permute-start(bf16[64,512]{1,0:T(8,128)(2,1)} %bitcast.8), channel_id=1, source_target_pairs={{0,16},{8,24},{16,32},{24,40},{32,48},{40,56},{48,64},{56,72},{64,... | collective-permute-start | bytes 196616 | tf_op jit(solution)/shard_map/ppermute | solution.py:189
  23.9 20.9 %collective-permute-start.1 = (bf16[64,512]{1,0:T(8,128)(2,1)}, bf16[64,512]{1,0:T(8,128)(2,1)S(1)}, u32[]{:S(2)}, u32[]{:S(2)}) collective-permute-start(bf16[64,512]{1,0:T(8,128)(2,1)} %bitcast.9), channel_id=1, source_target_pairs={{0,8},{8,16},{16,24},{24,32},{32,40},{40,48},{48,56},{56,64},{64,7... | collective-permute-start | bytes 196616 | tf_op jit(solution)/shard_map/ppermute | solution.py:189
  25.8 19.0 %collective-permute-start.2 = (bf16[64,512]{1,0:T(8,128)(2,1)}, bf16[64,512]{1,0:T(8,128)(2,1)S(1)}, u32[]{:S(2)}, u32[]{:S(2)}) collective-permute-start(bf16[64,512]{1,0:T(8,128)(2,1)} %bitcast.10), channel_id=1, source_target_pairs={{0,1016},{8,0},{16,8},{24,16},{32,24},{40,32},{48,40},{56,48},{64,... | collective-permute-start | bytes 196616 | tf_op jit(solution)/shard_map/ppermute | solution.py:189
  34.9 9.9 %collective-permute-start.3 = (bf16[64,512]{1,0:T(8,128)(2,1)}, bf16[64,512]{1,0:T(8,128)(2,1)S(1)}, u32[]{:S(2)}, u32[]{:S(2)}) collective-permute-start(bf16[64,512]{1,0:T(8,128)(2,1)} %bitcast.11), channel_id=1, source_target_pairs={{0,1008},{8,1016},{16,0},{24,8},{32,16},{40,24},{48,32},{56,40},{6... | collective-permute-start | bytes 196616 | tf_op jit(solution)/shard_map/ppermute | solution.py:189
  39.2 1.7 %copy-start = (bf16[512,5,512]{2,0,1:T(8,128)(2,1)S(1)}, bf16[512,5,512]{2,0,1:T(8,128)(2,1)}, u32[]{:S(2)}) copy-start(bf16[512,5,512]{2,0,1:T(8,128)(2,1)} %param.7) | copy-start | bytes 7864324
  40.9 0.8 copy-start.2
  41.7 0.7 copy-start.9
  44.8 16.2 %copy-start.8 = (bf16[512,64]{0,1:T(8,128)(2,1)S(1)}, bf16[512,64]{0,1:T(8,128)(2,1)}, u32[]{:S(2)}) copy-start(bf16[512,64]{0,1:T(8,128)(2,1)} %param.11) | copy-start | bytes 196612
  46.0 42.5 %copy-start.4 = (bf16[64,512]{1,0:T(8,128)(2,1)S(1)}, bf16[64,512]{1,0:T(8,128)(2,1)}, u32[]{:S(2)}) copy-start(bf16[64,512]{1,0:T(8,128)(2,1)} %wself_ref.3) | copy-start | bytes 196612
  46.0 42.5 %copy-start.6 = (bf16[64,512]{1,0:T(8,128)(2,1)S(1)}, bf16[64,512]{1,0:T(8,128)(2,1)}, u32[]{:S(2)}) copy-start(bf16[64,512]{1,0:T(8,128)(2,1)} %wneigh_ref.3) | copy-start | bytes 196612
  62.3 19.1 %all-to-all-start.2 = ((bf16[8,16,512]{2,1,0:T(8,128)(2,1)}), bf16[8,16,512]{2,1,0:T(8,128)(2,1)S(1)}, u32[]{:S(2)}, u32[]{:S(2)}) async-start(bf16[8,16,512]{2,1,0:T(8,128)(2,1)} %get-tuple-element.27), calls=%async_computation.2 | async-start | bytes 262144 | tf_op jit(solution)/shard_map/all_to_all | solution.py:199
  68.3 8.4 %collective-permute-start.4 = (bf16[128,512]{1,0:T(8,128)(2,1)S(1)}, bf16[128,512]{1,0:T(8,128)(2,1)S(1)}, u32[]{:S(2)}, u32[]{:S(2)}) collective-permute-start(bf16[128,512]{1,0:T(8,128)(2,1)S(1)} %all_gather.3.refs_0_), channel_id=1, source_target_pairs={{0,2},{2,4},{4,6},{6,0},{1,3},{3,5},{5,7},{7,1},{8,10},{10,12},{12... | collective-permute-start | bytes 393224 | tf_op jit(solution)/shard_map/ppermute | solution.py:195
  70.5 7.9 %collective-permute-start.5 = (bf16[128,512]{1,0:T(8,128)(2,1)S(1)}, bf16[128,512]{1,0:T(8,128)(2,1)S(1)}, u32[]{:S(2)}, u32[]{:S(2)}) collective-permute-start(bf16[128,512]{1,0:T(8,128)(2,1)S(1)} %all_gather.3.refs_0_), channel_id=1, source_target_pairs={{0,4},{2,6},{4,0},{6,2},{1,5},{3,7},{5,1},{7,3},{8,12},{10,14},{12... | collective-permute-start | bytes 393224 | tf_op jit(solution)/shard_map/ppermute | solution.py:195
  74.2 7.2 %collective-permute-start.6 = (bf16[128,512]{1,0:T(8,128)(2,1)S(1)}, bf16[128,512]{1,0:T(8,128)(2,1)S(1)}, u32[]{:S(2)}, u32[]{:S(2)}) collective-permute-start(bf16[128,512]{1,0:T(8,128)(2,1)S(1)} %all_gather.3.refs_0_), channel_id=1, source_target_pairs={{0,6},{2,0},{4,2},{6,4},{1,7},{3,1},{5,3},{7,5},{8,14},{10,8},{12,... | collective-permute-start | bytes 393224 | tf_op jit(solution)/shard_map/ppermute | solution.py:195
  82.2 30.8 %all-to-all-start.3 = ((bf16[16,16,512]{2,1,0:T(8,128)(2,1)}), bf16[16,16,512]{2,1,0:T(8,128)(2,1)S(1)}, u32[]{:S(2)}, u32[]{:S(2)}) async-start(bf16[16,16,512]{2,1,0:T(8,128)(2,1)} %shard_map.98), calls=%async_computation.3 | async-start | bytes 524288 | tf_op jit(solution)/shard_map/all_to_all | solution.py:199
  90.6 0.7 copy-start.7
  91.3 15.3 %collective-permute-start.10 = (bf16[64,512]{1,0:T(8,128)(2,1)S(1)}, bf16[64,512]{1,0:T(8,128)(2,1)S(1)}, u32[]{:S(2)}, u32[]{:S(2)}) collective-permute-start(bf16[64,512]{1,0:T(8,128)(2,1)S(1)} %get-tuple-element.26), channel_id=1, source_target_pairs={{0,16},{8,24},{16,32},{24,40},{32,48},{40,56},{48,64},{56,72},{64,... | collective-permute-start | bytes 196616 | tf_op jit(solution)/shard_map/ppermute | solution.py:189
  95.8 10.7 %collective-permute-start.7 = (bf16[64,512]{1,0:T(8,128)(2,1)S(1)}, bf16[64,512]{1,0:T(8,128)(2,1)S(1)}, u32[]{:S(2)}, u32[]{:S(2)}) collective-permute-start(bf16[64,512]{1,0:T(8,128)(2,1)S(1)} %get-tuple-element.23), channel_id=1, source_target_pairs={{0,1008},{8,1016},{16,0},{24,8},{32,16},{40,24},{48,32},{56,40},{6... | collective-permute-start | bytes 196616 | tf_op jit(solution)/shard_map/ppermute | solution.py:189
  101.2 6.0 %collective-permute-start.8 = (bf16[64,512]{1,0:T(8,128)(2,1)S(1)}, bf16[64,512]{1,0:T(8,128)(2,1)S(1)}, u32[]{:S(2)}, u32[]{:S(2)}) collective-permute-start(bf16[64,512]{1,0:T(8,128)(2,1)S(1)} %get-tuple-element.24), channel_id=1, source_target_pairs={{0,1016},{8,0},{16,8},{24,16},{32,24},{40,32},{48,40},{56,48},{64,... | collective-permute-start | bytes 196616 | tf_op jit(solution)/shard_map/ppermute | solution.py:189
  104.6 8.3 %collective-permute-start.9 = (bf16[64,512]{1,0:T(8,128)(2,1)S(1)}, bf16[64,512]{1,0:T(8,128)(2,1)S(1)}, u32[]{:S(2)}, u32[]{:S(2)}) collective-permute-start(bf16[64,512]{1,0:T(8,128)(2,1)S(1)} %get-tuple-element.25), channel_id=1, source_target_pairs={{0,8},{8,16},{16,24},{24,32},{32,40},{40,48},{48,56},{56,64},{64,7... | collective-permute-start | bytes 196616 | tf_op jit(solution)/shard_map/ppermute | solution.py:189
  113.6 18.2 %all-to-all-start.4 = ((bf16[64,8,128]{2,1,0:T(8,128)(2,1)}), bf16[64,8,128]{2,1,0:T(8,128)(2,1)S(1)}, u32[]{:S(2)}, u32[]{:S(2)}) async-start(bf16[64,8,128]{2,1,0:T(8,128)(2,1)} %shard_map.99), calls=%async_computation.4 | async-start | bytes 262144 | tf_op jit(solution)/shard_map/all_to_all | solution.py:199

commit v3 on v2

v3 whole, which is shorter than its diff:
```python
import math

import jax
import jax.numpy as jnp
from jax import lax
from jax.experimental import pallas as pl
from jax.experimental.pallas import tpu as pltpu
from jax.sharding import Mesh
from jax.sharding import PartitionSpec as P

ROW = ("z", "y")
COL = ("x", "core")
TILE = 128
SPLIT = 1
LAST = (((1,), (1,)), ((), ()))
FIRST = (((0,), (0,)), ((), ()))
PLAIN = (((1,), (0,)), ((), ()))
VMEM = pl.BlockSpec(memory_space=pltpu.VMEM)
SMEM = pl.BlockSpec(memory_space=pltpu.SMEM)
ANY = pl.BlockSpec(memory_space=pl.ANY)
BF16 = jnp.bfloat16
F32 = jnp.float32


def local_call(kernel, out_shape, in_specs, args, flops):
    outs = jax.tree.leaves(out_shape)
    moved = sum(a.size * a.dtype.itemsize for a in (*args, *outs))
    return pl.pallas_call(
        kernel,
        out_shape=out_shape,
        in_specs=in_specs,
        out_specs=jax.tree.map(lambda _: VMEM, out_shape),
        compiler_params=pltpu.CompilerParams(vmem_limit_bytes=24 * 1024 * 1024),
        cost_estimate=pl.CostEstimate(flops=flops, bytes_accessed=moved, transcendentals=0),
    )(*args)


def dot(a, b, dims):
    return lax.dot_general(a, b, dims, preferred_element_type=F32)


def mask_kernel(mask_ref, own_ref, adj_ref, weighted_ref, base_ref, inverse_ref):
    bands, nodes, _ = adj_ref.shape
    reach = (bands - 1) // 2
    width = own_ref.shape[0]
    ones = jnp.ones((16, nodes), BF16)
    degree = jnp.zeros((16, nodes), F32)
    for band in range(bands):
        for row in range(nodes // TILE):
            for column in range(nodes // TILE):
                keep = mask_ref[row, column, band].astype(F32).astype(BF16)
                rows, columns = pl.ds(row * TILE, TILE), pl.ds(column * TILE, TILE)
                weighted_ref[band, rows, columns] = adj_ref[band, rows, columns] * keep
        if band == reach:
            both = dot(jnp.concatenate([own_ref[...], ones], axis=0), weighted_ref[band], LAST)
            base_ref[...] = both[:width]
            degree = degree + both[width:]
        else:
            degree = degree + dot(ones, weighted_ref[band], LAST)
    inverse_ref[...] = 1.0 / jnp.maximum(degree[:8], 1.0)


def mean_kernel(*refs):
    *near_refs, weighted_ref, base_ref, inverse_ref, own_ref, wself_ref, wneigh_ref = refs[:-2]
    mean_ref, partial_ref = refs[-2:]
    bands = weighted_ref.shape[0]
    reach = (bands - 1) // 2
    total = base_ref[...]
    for near_ref, band in zip(near_refs, [b for b in range(bands) if b != reach]):
        total = total + dot(near_ref[...], weighted_ref[band], LAST)
    mean = (total * inverse_ref[0:1, :]).astype(BF16)
    mean_ref[...] = mean
    weights = jnp.concatenate([wself_ref[...], wneigh_ref[...]], axis=0)
    values = jnp.concatenate([own_ref[...], mean], axis=0)
    partial_ref[...] = dot(weights, values, FIRST).astype(BF16).reshape(partial_ref.shape)


def act_kernel(parts_ref, cot_ref, act_ref, grad_ref):
    preact = parts_ref[0].astype(F32)
    for part in range(1, parts_ref.shape[0]):
        preact = preact + parts_ref[part].astype(F32)
    sigmoid_z = 1.0 / (1.0 + jnp.exp(-preact))
    act_ref[...] = (preact * sigmoid_z).astype(BF16)
    slope = sigmoid_z * (1.0 + preact * (1.0 - sigmoid_z))
    grad = (cot_ref[...].astype(F32) * slope).astype(BF16)
    for copy in range(grad_ref.shape[0]):
        grad_ref[copy] = grad


def weight_kernel(scale, grads_ref, own_ref, mean_ref, pieces_ref):
    groups, width, nodes = grads_ref.shape
    values = jnp.concatenate([own_ref[...], mean_ref[...]], axis=0)
    term = dot(values, grads_ref[...].reshape(groups * width, nodes), LAST) * scale
    pieces_ref[...] = term.astype(BF16).reshape(pieces_ref.shape)


def sum_kernel(in_ref, *refs):
    out_ref = refs[-1]
    total = in_ref[0].astype(F32)
    for part in range(1, in_ref.shape[0]):
        total = total + in_ref[part].astype(F32)
    total = total.astype(BF16)
    for copy in range(out_ref.shape[0]):
        out_ref[copy] = total


def final_kernel(in_ref, self_ref, neigh_ref):
    total = in_ref[...].astype(F32).reshape(in_ref.shape[0] * in_ref.shape[1], in_ref.shape[2])
    half = self_ref.shape[0]
    self_ref[...] = total[:half]
    neigh_ref[...] = total[half:]


def back_kernel(grads_ref, wself_ref, wneigh_ref, weighted_ref, inverse_ref, *outs):
    groups, width, nodes = grads_ref.shape
    bands = weighted_ref.shape[0]
    reach = (bands - 1) // 2
    grads = grads_ref[...].reshape(groups * width, nodes)
    spread = (dot(wneigh_ref[...], grads, PLAIN) * inverse_ref[0:1, :]).astype(BF16)
    term_refs, stays_ref = outs[:-1], outs[-1]
    for term_ref, band in zip(term_refs, [b for b in range(bands) if b != reach]):
        term_ref[...] = dot(spread, weighted_ref[band], PLAIN).astype(BF16)
    stays_ref[...] = dot(wself_ref[...], grads, PLAIN) + dot(spread, weighted_ref[reach], PLAIN)


def from_behind(value, steps):
    count = lax.axis_size(ROW)
    pairs = [(source, (source + steps) % count) for source in range(count)]
    return lax.ppermute(value, ROW, pairs)


def exchange(chunks, axes):
    return lax.all_to_all(chunks, axes, 0, 0, tiled=True)


def body(features, adjacency, tile_mask, w_self, w_neigh, cotangent):
    own = features.T
    panel = width, nodes = own.shape
    groups = lax.axis_size(COL)
    lines = lax.axis_size("y")
    planes = lax.axis_size("z")
    total = groups * width
    bands = tile_mask.shape[1]
    reach = (bands - 1) // 2
    offsets = [k for k in range(-reach, reach + 1) if k != 0]
    shape = jax.ShapeDtypeStruct
    everyone = shape((groups, *panel), BF16)

    neighbours = [from_behind(own, -k) for k in offsets]
    adj = adjacency.transpose(1, 0, 2)
    weighted, base, inverse = local_call(
        mask_kernel,
        (shape(adj.shape, BF16), shape(panel, F32), shape((8, nodes), F32)),
        [SMEM, VMEM, VMEM],
        (tile_mask.transpose(0, 2, 1), own, adj),
        2 * adj.size,
    )
    mean, shares = local_call(
        mean_kernel,
        (shape(panel, BF16), everyone),
        [VMEM] * (len(offsets) + 6),
        (*neighbours, weighted, base, inverse, own, w_self, w_neigh),
        2 * adj.size,
    )
    activated, copies = local_call(
        act_kernel,
        (shape(panel, BF16), everyone),
        [VMEM] * 2,
        (exchange(shares, COL), cotangent.T),
        adj.size,
    )
    grads = exchange(copies, COL)

    grad_scale = 1.0 / math.sqrt(lax.axis_size(ROW) * nodes)

    def weight_terms(*refs):
        weight_kernel(grad_scale, *refs)

    height = 2 * width // lines
    pieces = local_call(
        weight_terms,
        shape((lines, height, total), BF16),
        [VMEM] * 3,
        (grads, own, mean),
        adj.size,
    )
    over_y = exchange(pieces, "y")

    *terms, stays = local_call(
        back_kernel,
        (*[shape(panel, BF16)] * len(offsets), shape(panel, F32)),
        [VMEM] * 5,
        (grads, w_self, w_neigh, weighted, inverse),
        2 * adj.size,
    )
    arrived = [from_behind(term, k) for term, k in zip(terms, offsets)]
    early, late = arrived[:SPLIT], arrived[SPLIT:]

    folded = local_call(
        sum_kernel,
        shape((planes, height, total), BF16),
        [VMEM] + [ANY] * len(early),
        (over_y, *early),
        adj.size,
    )
    over_z = exchange(folded, "z")
    summed = local_call(
        sum_kernel,
        shape((lines, height, total), BF16),
        [VMEM] + [ANY] * len(late),
        (over_z, *late),
        adj.size,
    )
    gathered = exchange(summed, "y")
    grad_self, grad_neigh = local_call(
        final_kernel,
        (shape((width, total), F32), shape((width, total), F32)),
        [VMEM],
        (gathered,),
        adj.size,
    )
    for term in arrived:
        stays = stays + term.astype(F32)
    return (activated.T, stays.astype(BF16).T, grad_self, grad_neigh)


def solution(mesh):
    rows, columns = mesh.devices.shape
    lines = math.gcd(rows, 8)
    cores = math.gcd(columns, 2)
    fine = Mesh(
        mesh.devices.reshape(rows // lines, lines, columns // cores, cores), ROW + COL
    )
    return jax.shard_map(
        body,
        mesh=fine,
        in_specs=(
            P(ROW, COL),
            P(ROW, None, None),
            P(ROW, None, None),
            P(COL, None),
            P(COL, None),
            P(ROW, COL),
        ),
        out_specs=(P(ROW, COL), P(ROW, COL), P(COL, None), P(COL, None)),
        check_vma=False,
    )
```

time: 134 us -> 125 us (0.933)
  the two profiles are of different devices: /device:TPU:1 before, /device:TPU:2 now
where the time goes in v3:
time: 125 us
  starting transfers between devices  61.5 us (49%)
  blocking collectives  26.4 us (21%)
  waiting for transfers between devices  22.9 us (18%)
  Pallas kernels  7.24 us (6%)
  local copies, waits for them, and re-layouts  5.17 us (4%)
    ppermute x8, starting transfers between devices, from_behind(): return lax.ppermute(value, ROW, pairs)  51.2 us
    all_to_all x2, blocking collectives, exchange(): return lax.all_to_all(chunks, axes, 0, 0, tiled=True)  26.4 us
    ppermute x8, waiting for transfers between devices, from_behind(): return lax.ppermute(value, ROW, pairs)  14.5 us
    all_to_all x3, starting transfers between devices, exchange(): return lax.all_to_all(chunks, axes, 0, 0, tiled=True)  10.3 us
    all_to_all x3, waiting for transfers between devices, exchange(): return lax.all_to_all(chunks, axes, 0, 0, tiled=True)  8.33 us
    pallas_call x8, Pallas kernels, local_call(): pl.pallas_call(kernel, out_shape=out_shape, in_specs=in_specs, out_specs=...  7.24 us
    unnamed x20, local copies, waits for them, and re-layouts  5.17 us
  transfers between devices with their start and end apart: 11, of which 6 were waited for; matrix products, arithmetic and copies ran while one was open for 1% of the time, Pallas kernels for 2%

profile of v3, /device:TPU:2, one launch (start us, length us, event | category | flops | bytes accessed | tf_op | source)
XLA Modules:
  0.0 124.6 jit_solution(7857753097558882054)
XLA Ops:
  0.6 21.9 %collective-permute-start.3 = (bf16[64,512]{1,0:T(8,128)(2,1)}, bf16[64,512]{1,0:T(8,128)(2,1)S(1)}, u32[]{:S(2)}, u32[]{:S(2)}) collective-permute-start(bf16[64,512]{1,0:T(8,128)(2,1)} %bitcast.8), channel_id=1, source_target_pairs={{0,1008},{8,1016},{16,0},{24,8},{32,16},{40,24},{48,32},{56,40},{6... | collective-permute-start | bytes 196616 | tf_op jit(solution)/shard_map/ppermute | solution.py:129
  22.6 3.3 %collective-permute-start.2 = (bf16[64,512]{1,0:T(8,128)(2,1)}, bf16[64,512]{1,0:T(8,128)(2,1)S(1)}, u32[]{:S(2)}, u32[]{:S(2)}) collective-permute-start(bf16[64,512]{1,0:T(8,128)(2,1)} %bitcast.9), channel_id=1, source_target_pairs={{0,1016},{8,0},{16,8},{24,16},{32,24},{40,32},{48,40},{56,48},{64,... | collective-permute-start | bytes 196616 | tf_op jit(solution)/shard_map/ppermute | solution.py:129
  25.8 2.6 %collective-permute-start.1 = (bf16[64,512]{1,0:T(8,128)(2,1)}, bf16[64,512]{1,0:T(8,128)(2,1)S(1)}, u32[]{:S(2)}, u32[]{:S(2)}) collective-permute-start(bf16[64,512]{1,0:T(8,128)(2,1)} %bitcast.10), channel_id=1, source_target_pairs={{0,8},{8,16},{16,24},{24,32},{32,40},{40,48},{48,56},{56,64},{64,7... | collective-permute-start | bytes 196616 | tf_op jit(solution)/shard_map/ppermute | solution.py:129
  28.4 2.0 %collective-permute-start = (bf16[64,512]{1,0:T(8,128)(2,1)}, bf16[64,512]{1,0:T(8,128)(2,1)S(1)}, u32[]{:S(2)}, u32[]{:S(2)}) collective-permute-start(bf16[64,512]{1,0:T(8,128)(2,1)} %bitcast.11), channel_id=1, source_target_pairs={{0,16},{8,24},{16,32},{24,40},{32,48},{40,56},{48,64},{56,72},{64,... | collective-permute-start | bytes 196616 | tf_op jit(solution)/shard_map/ppermute | solution.py:129
  30.5 1.7 %copy-done = bf16[512,5,512]{2,0,1:T(8,128)(2,1)S(1)} copy-done((bf16[512,5,512]{2,0,1:T(8,128)(2,1)S(1)}, bf16[512,5,512]{2,0,1:T(8,128)(2,1)}, u32[]{:S(2)}) %copy-start) | copy-done | bytes 2621464
  32.2 0.8 copy-done.1
  33.0 0.7 copy-done.6
  33.7 1.5 %shard_map.93 = (bf16[5,512,512]{2,1,0:T(8,128)(2,1)S(1)}, f32[64,512]{1,0:T(8,128)S(1)}, f32[8,512]{1,0:T(8,128)S(1)}) custom-call(s32[4,4,5]{2,1,0:T(4,128)S(1)} %bitcast.16, bf16[64,512]{1,0:T(8,128)(2,1)S(1)} %bitcast.12, bf16[5,512,512]{2,1,0:T(8,128)(2,1)S(1)} %bitcast.7), custom_call_target="tpu_custom_call" | custom-call | flops 2621440 | bytes 5456192 | tf_op jit(solution)/shard_map/pallas_call | solution.py:28
  35.5 3.5 %collective-permute-done.refs_0_ = bf16[64,512]{1,0:T(8,128)(2,1)S(1)} collective-permute-done((bf16[64,512]{1,0:T(8,128)(2,1)}, bf16[64,512]{1,0:T(8,128)(2,1)S(1)}, u32[]{:S(2)}, u32[]{:S(2)}) %collective-permute-start) | collective-permute-done | bytes 65568 | tf_op jit(solution)/shard_map/ppermute | solution.py:129
  39.0 1.0 shard_map.94
  40.0 13.6 %all_to_all.25.parts_ref = bf16[8,64,512]{2,1,0:T(8,128)(2,1)S(1)} all-to-all(bf16[8,64,512]{2,1,0:T(8,128)(2,1)S(1)} %get-tuple-element.21), channel_id=1, replica_groups=mesh['z'=16,'y'=8,'x'=4,'core'=2] {'x','core'}, dimensions={0} | all-to-all | bytes 1048576 | tf_op jit(solution)/shard_map/all_to_all | solution.py:133
  53.6 0.8 shard_map.95
  54.4 12.8 %all_to_all.26.grads_ref.refs_0_ = bf16[8,64,512]{2,1,0:T(8,128)(2,1)S(1)} all-to-all(bf16[8,64,512]{2,1,0:T(8,128)(2,1)S(1)} %get-tuple-element.23), channel_id=1, replica_groups=mesh['z'=16,'y'=8,'x'=4,'core'=2] {'x','core'}, dimensions={0} | all-to-all | bytes 1048576 | tf_op jit(solution)/shard_map/all_to_all | solution.py:133
  67.2 1.0 shard_map.97
  68.1 3.4 %all-to-all-start.2 = ((bf16[8,16,512]{2,1,0:T(8,128)(2,1)}), bf16[8,16,512]{2,1,0:T(8,128)(2,1)S(1)}, u32[]{:S(2)}, u32[]{:S(2)}) async-start(bf16[8,16,512]{2,1,0:T(8,128)(2,1)} %shard_map.97), calls=%async_computation.2 | async-start | bytes 262144 | tf_op jit(solution)/shard_map/all_to_all | solution.py:133
  71.5 0.8 shard_map.96
  73.0 0.6 copy-done.8
  73.6 0.6 copy-done.9
  74.2 7.2 %collective-permute-start.4 = (bf16[64,512]{1,0:T(8,128)(2,1)S(1)}, bf16[64,512]{1,0:T(8,128)(2,1)S(1)}, u32[]{:S(2)}, u32[]{:S(2)}) collective-permute-start(bf16[64,512]{1,0:T(8,128)(2,1)S(1)} %get-tuple-element.25), channel_id=1, source_target_pairs={{0,1008},{8,1016},{16,0},{24,8},{32,16},{40,24},{48,32},{56,40},{6... | collective-permute-start | bytes 196616 | tf_op jit(solution)/shard_map/ppermute | solution.py:129
  81.4 1.9 %collective-permute-done.4.refs_0_ = bf16[64,512]{1,0:T(8,128)(2,1)S(1)} collective-permute-done((bf16[64,512]{1,0:T(8,128)(2,1)S(1)}, bf16[64,512]{1,0:T(8,128)(2,1)S(1)}, u32[]{:S(2)}, u32[]{:S(2)}) %collective-permute-start.4) | collective-permute-done | bytes 65568 | tf_op jit(solution)/shard_map/ppermute | solution.py:129
  83.3 0.8 shard_map.98
  84.1 3.5 %all-to-all-start.3 = ((bf16[16,16,512]{2,1,0:T(8,128)(2,1)}), bf16[16,16,512]{2,1,0:T(8,128)(2,1)S(1)}, u32[]{:S(2)}, u32[]{:S(2)}) async-start(bf16[16,16,512]{2,1,0:T(8,128)(2,1)} %shard_map.98), calls=%async_computation.3 | async-start | bytes 524288 | tf_op jit(solution)/shard_map/all_to_all | solution.py:133
  87.6 10.4 %collective-permute-start.5 = (bf16[64,512]{1,0:T(8,128)(2,1)}, bf16[64,512]{1,0:T(8,128)(2,1)S(1)}, u32[]{:S(2)}, u32[]{:S(2)}) collective-permute-start(bf16[64,512]{1,0:T(8,128)(2,1)} %copy-done.9), channel_id=1, source_target_pairs={{0,1016},{8,0},{16,8},{24,16},{32,24},{40,32},{48,40},{56,48},{64,... | collective-permute-start | bytes 196616 | tf_op jit(solution)/shard_map/ppermute | solution.py:129
  98.0 1.9 %collective-permute-start.6 = (bf16[64,512]{1,0:T(8,128)(2,1)}, bf16[64,512]{1,0:T(8,128)(2,1)S(1)}, u32[]{:S(2)}, u32[]{:S(2)}) collective-permute-start(bf16[64,512]{1,0:T(8,128)(2,1)} %copy-done.8), channel_id=1, source_target_pairs={{0,8},{8,16},{16,24},{24,32},{32,40},{40,48},{48,56},{56,64},{64,7... | collective-permute-start | bytes 196616 | tf_op jit(solution)/shard_map/ppermute | solution.py:129
  100.0 1.9 %collective-permute-start.7 = (bf16[64,512]{1,0:T(8,128)(2,1)}, bf16[64,512]{1,0:T(8,128)(2,1)S(1)}, u32[]{:S(2)}, u32[]{:S(2)}) collective-permute-start(bf16[64,512]{1,0:T(8,128)(2,1)} %copy-done.7), channel_id=1, source_target_pairs={{0,16},{8,24},{16,32},{24,40},{32,48},{40,56},{48,64},{56,72},{64,... | collective-permute-start | bytes 196616 | tf_op jit(solution)/shard_map/ppermute | solution.py:129
  101.9 6.1 %collective-permute-done.6.refs_1_ = bf16[64,512]{1,0:T(8,128)(2,1)S(1)} collective-permute-done((bf16[64,512]{1,0:T(8,128)(2,1)}, bf16[64,512]{1,0:T(8,128)(2,1)S(1)}, u32[]{:S(2)}, u32[]{:S(2)}) %collective-permute-start.6) | collective-permute-done | bytes 65568 | tf_op jit(solution)/shard_map/ppermute | solution.py:129
  108.0 2.9 %collective-permute-done.7.refs_2_ = bf16[64,512]{1,0:T(8,128)(2,1)S(1)} collective-permute-done((bf16[64,512]{1,0:T(8,128)(2,1)}, bf16[64,512]{1,0:T(8,128)(2,1)S(1)}, u32[]{:S(2)}, u32[]{:S(2)}) %collective-permute-start.7) | collective-permute-done | bytes 65568 | tf_op jit(solution)/shard_map/ppermute | solution.py:129
  110.9 0.7 shard_map.99
  111.6 3.4 %all-to-all-start.4 = ((bf16[8,16,512]{2,1,0:T(8,128)(2,1)}), bf16[8,16,512]{2,1,0:T(8,128)(2,1)S(1)}, u32[]{:S(2)}, u32[]{:S(2)}) async-start(bf16[8,16,512]{2,1,0:T(8,128)(2,1)} %shard_map.99), calls=%async_computation.4 | async-start | bytes 262144 | tf_op jit(solution)/shard_map/all_to_all | solution.py:133
  114.9 0.7 fusion
  115.6 8.3 %all-to-all-done.4.in_ref = bf16[8,16,512]{2,1,0:T(8,128)(2,1)S(1)} async-done(((bf16[8,16,512]{2,1,0:T(8,128)(2,1)}), bf16[8,16,512]{2,1,0:T(8,128)(2,1)S(1)}, u32[]{:S(2)}, u32[]{:S(2)}) %all-to-all-start.4) | async-done | bytes 131104 | tf_op jit(solution)/shard_map/all_to_all | solution.py:133
  123.9 0.7 shard_map.100
  (21 shorter events, 0.9 us)
Async XLA Ops:
  0.6 34.7 %collective-permute-start.3 = (bf16[64,512]{1,0:T(8,128)(2,1)}, bf16[64,512]{1,0:T(8,128)(2,1)S(1)}, u32[]{:S(2)}, u32[]{:S(2)}) collective-permute-start(bf16[64,512]{1,0:T(8,128)(2,1)} %bitcast.8), channel_id=1, source_target_pairs={{0,1008},{8,1016},{16,0},{24,8},{32,16},{40,24},{48,32},{56,40},{6... | collective-permute-start | bytes 196616 | tf_op jit(solution)/shard_map/ppermute | solution.py:129
  22.6 12.7 %collective-permute-start.2 = (bf16[64,512]{1,0:T(8,128)(2,1)}, bf16[64,512]{1,0:T(8,128)(2,1)S(1)}, u32[]{:S(2)}, u32[]{:S(2)}) collective-permute-start(bf16[64,512]{1,0:T(8,128)(2,1)} %bitcast.9), channel_id=1, source_target_pairs={{0,1016},{8,0},{16,8},{24,16},{32,24},{40,32},{48,40},{56,48},{64,... | collective-permute-start | bytes 196616 | tf_op jit(solution)/shard_map/ppermute | solution.py:129
  25.8 9.7 %collective-permute-start.1 = (bf16[64,512]{1,0:T(8,128)(2,1)}, bf16[64,512]{1,0:T(8,128)(2,1)S(1)}, u32[]{:S(2)}, u32[]{:S(2)}) collective-permute-start(bf16[64,512]{1,0:T(8,128)(2,1)} %bitcast.10), channel_id=1, source_target_pairs={{0,8},{8,16},{16,24},{24,32},{32,40},{40,48},{48,56},{56,64},{64,7... | collective-permute-start | bytes 196616 | tf_op jit(solution)/shard_map/ppermute | solution.py:129
  28.4 10.6 %collective-permute-start = (bf16[64,512]{1,0:T(8,128)(2,1)}, bf16[64,512]{1,0:T(8,128)(2,1)S(1)}, u32[]{:S(2)}, u32[]{:S(2)}) collective-permute-start(bf16[64,512]{1,0:T(8,128)(2,1)} %bitcast.11), channel_id=1, source_target_pairs={{0,16},{8,24},{16,32},{24,40},{32,48},{40,56},{48,64},{56,72},{64,... | collective-permute-start | bytes 196616 | tf_op jit(solution)/shard_map/ppermute | solution.py:129
  30.5 1.7 %copy-start = (bf16[512,5,512]{2,0,1:T(8,128)(2,1)S(1)}, bf16[512,5,512]{2,0,1:T(8,128)(2,1)}, u32[]{:S(2)}) copy-start(bf16[512,5,512]{2,0,1:T(8,128)(2,1)} %param.7) | copy-start | bytes 7864324
  32.2 0.8 copy-start.1
  33.0 0.7 copy-start.6
  33.7 5.3 %copy-start.3 = (bf16[64,512]{1,0:T(8,128)(2,1)S(1)}, bf16[64,512]{1,0:T(8,128)(2,1)}, u32[]{:S(2)}) copy-start(bf16[64,512]{1,0:T(8,128)(2,1)} %wself_ref.1) | copy-start | bytes 196612
  33.7 5.3 %copy-start.4 = (bf16[64,512]{1,0:T(8,128)(2,1)S(1)}, bf16[64,512]{1,0:T(8,128)(2,1)}, u32[]{:S(2)}) copy-start(bf16[64,512]{1,0:T(8,128)(2,1)} %wneigh_ref.1) | copy-start | bytes 196612
  35.3 18.4 %copy-start.5 = (bf16[512,64]{0,1:T(8,128)(2,1)S(1)}, bf16[512,64]{0,1:T(8,128)(2,1)}, u32[]{:S(2)}) copy-start(bf16[512,64]{0,1:T(8,128)(2,1)} %param.11) | copy-start | bytes 196612
  39.0 28.2 %copy-start.2 = (bf16[512,64]{0,1:T(8,128)(2,1)S(1)}, bf16[512,64]{0,1:T(8,128)(2,1)}, u32[]{:S(2)}) copy-start(bf16[512,64]{0,1:T(8,128)(2,1)} %param.6) | copy-start | bytes 196612
  68.1 15.2 %all-to-all-start.2 = ((bf16[8,16,512]{2,1,0:T(8,128)(2,1)}), bf16[8,16,512]{2,1,0:T(8,128)(2,1)S(1)}, u32[]{:S(2)}, u32[]{:S(2)}) async-start(bf16[8,16,512]{2,1,0:T(8,128)(2,1)} %shard_map.97), calls=%async_computation.2 | async-start | bytes 262144 | tf_op jit(solution)/shard_map/all_to_all | solution.py:133
  72.4 0.6 copy-start.7
  73.0 0.6 copy-start.8
  73.6 0.6 copy-start.9
  74.2 9.1 %collective-permute-start.4 = (bf16[64,512]{1,0:T(8,128)(2,1)S(1)}, bf16[64,512]{1,0:T(8,128)(2,1)S(1)}, u32[]{:S(2)}, u32[]{:S(2)}) collective-permute-start(bf16[64,512]{1,0:T(8,128)(2,1)S(1)} %get-tuple-element.25), channel_id=1, source_target_pairs={{0,1008},{8,1016},{16,0},{24,8},{32,16},{40,24},{48,32},{56,40},{6... | collective-permute-start | bytes 196616 | tf_op jit(solution)/shard_map/ppermute | solution.py:129
  84.1 26.8 %all-to-all-start.3 = ((bf16[16,16,512]{2,1,0:T(8,128)(2,1)}), bf16[16,16,512]{2,1,0:T(8,128)(2,1)S(1)}, u32[]{:S(2)}, u32[]{:S(2)}) async-start(bf16[16,16,512]{2,1,0:T(8,128)(2,1)} %shard_map.98), calls=%async_computation.3 | async-start | bytes 524288 | tf_op jit(solution)/shard_map/all_to_all | solution.py:133
  87.6 14.3 %collective-permute-start.5 = (bf16[64,512]{1,0:T(8,128)(2,1)}, bf16[64,512]{1,0:T(8,128)(2,1)S(1)}, u32[]{:S(2)}, u32[]{:S(2)}) collective-permute-start(bf16[64,512]{1,0:T(8,128)(2,1)} %copy-done.9), channel_id=1, source_target_pairs={{0,1016},{8,0},{16,8},{24,16},{32,24},{40,32},{48,40},{56,48},{64,... | collective-permute-start | bytes 196616 | tf_op jit(solution)/shard_map/ppermute | solution.py:129
  98.0 9.9 %collective-permute-start.6 = (bf16[64,512]{1,0:T(8,128)(2,1)}, bf16[64,512]{1,0:T(8,128)(2,1)S(1)}, u32[]{:S(2)}, u32[]{:S(2)}) collective-permute-start(bf16[64,512]{1,0:T(8,128)(2,1)} %copy-done.8), channel_id=1, source_target_pairs={{0,8},{8,16},{16,24},{24,32},{32,40},{40,48},{48,56},{56,64},{64,7... | collective-permute-start | bytes 196616 | tf_op jit(solution)/shard_map/ppermute | solution.py:129
  100.0 10.9 %collective-permute-start.7 = (bf16[64,512]{1,0:T(8,128)(2,1)}, bf16[64,512]{1,0:T(8,128)(2,1)S(1)}, u32[]{:S(2)}, u32[]{:S(2)}) collective-permute-start(bf16[64,512]{1,0:T(8,128)(2,1)} %copy-done.7), channel_id=1, source_target_pairs={{0,16},{8,24},{16,32},{24,40},{32,48},{40,56},{48,64},{56,72},{64,... | collective-permute-start | bytes 196616 | tf_op jit(solution)/shard_map/ppermute | solution.py:129
  111.6 12.4 %all-to-all-start.4 = ((bf16[8,16,512]{2,1,0:T(8,128)(2,1)}), bf16[8,16,512]{2,1,0:T(8,128)(2,1)S(1)}, u32[]{:S(2)}, u32[]{:S(2)}) async-start(bf16[8,16,512]{2,1,0:T(8,128)(2,1)} %shard_map.99), calls=%async_computation.4 | async-start | bytes 262144 | tf_op jit(solution)/shard_map/all_to_all | solution.py:133

commit v4 on v3

v4 whole, which is shorter than its diff:
```python
import math

import jax
import jax.numpy as jnp
from jax import lax
from jax.experimental import pallas as pl
from jax.experimental.pallas import tpu as pltpu
from jax.sharding import Mesh
from jax.sharding import PartitionSpec as P

ROW = ("z", "y")
COL = ("x", "core")
TILE = 128
LAST = (((1,), (1,)), ((), ()))
FIRST = (((0,), (0,)), ((), ()))
PLAIN = (((1,), (0,)), ((), ()))
VMEM = pl.BlockSpec(memory_space=pltpu.VMEM)
SMEM = pl.BlockSpec(memory_space=pltpu.SMEM)
ANY = pl.BlockSpec(memory_space=pl.ANY)
BF16 = jnp.bfloat16
F32 = jnp.float32


def local_call(kernel, out_shape, in_specs, args, flops, scratch=()):
    outs = jax.tree.leaves(out_shape)
    moved = sum(a.size * a.dtype.itemsize for a in (*args, *outs))
    return pl.pallas_call(
        kernel,
        out_shape=out_shape,
        in_specs=in_specs,
        out_specs=jax.tree.map(lambda _: VMEM, out_shape),
        scratch_shapes=[pltpu.VMEM(size, F32) for size in scratch],
        compiler_params=pltpu.CompilerParams(vmem_limit_bytes=24 * 1024 * 1024),
        cost_estimate=pl.CostEstimate(flops=flops, bytes_accessed=moved, transcendentals=0),
    )(*args)


def dot(a, b, dims):
    return lax.dot_general(a, b, dims, preferred_element_type=F32)


def mask_kernel(mask_ref, pair_ref, adj_ref, weighted_ref, base_ref, inverse_ref):
    bands, nodes, _ = adj_ref.shape
    reach = (bands - 1) // 2
    depth = base_ref.shape[0]
    ones = jnp.ones((16, nodes), BF16)
    degree = jnp.zeros((16, nodes), F32)
    for band in range(bands):
        for row in range(nodes // TILE):
            for column in range(nodes // TILE):
                keep = mask_ref[row, column, band].astype(F32).astype(BF16)
                rows, columns = pl.ds(row * TILE, TILE), pl.ds(column * TILE, TILE)
                weighted_ref[band, rows, columns] = adj_ref[band, rows, columns] * keep
        if band == reach:
            pair = pair_ref[...].reshape(depth, nodes)
            both = dot(jnp.concatenate([pair, ones], axis=0), weighted_ref[band], LAST)
            base_ref[...] = both[:depth]
            degree = degree + both[depth:]
        else:
            degree = degree + dot(ones, weighted_ref[band], LAST)
    inverse_ref[...] = 1.0 / jnp.maximum(degree[:8], 1.0)


def near_kernel(core_ref, behind_ref, ahead_ref, weighted_ref, out_ref):
    reach = (weighted_ref.shape[0] - 1) // 2
    steps = core_ref[0] + 1
    total = dot(behind_ref[...], weighted_ref[reach - steps], LAST)
    out_ref[...] = total + dot(ahead_ref[...], weighted_ref[reach + steps], LAST)


def mean_kernel(
    core_ref, near_ref, base_ref, inverse_ref, pair_ref, wself_ref, wneigh_ref, mean_ref, out_ref, scratch
):
    cores, width, nodes = pair_ref.shape
    depth = cores * width
    core = core_ref[0]
    total = base_ref[...]
    for part in range(cores):
        total = total + near_ref[part]
    mean = (total * inverse_ref[0:1, :]).astype(BF16)
    scratch[:depth] = total * inverse_ref[0:1, :]
    mean_ref[...] = scratch[pl.ds(pl.multiple_of(core * width, width), width), :].astype(BF16)
    weights = jnp.concatenate(
        [w[...].reshape(depth, w.shape[2]) for w in (wself_ref, wneigh_ref)], axis=0
    )
    values = jnp.concatenate([pair_ref[...].reshape(depth, nodes), mean], axis=0)
    scratch[...] = dot(weights, values, FIRST)
    for chip in range(out_ref.shape[0]):
        first = pl.multiple_of((chip * cores + core) * width, width)
        out_ref[chip] = scratch[pl.ds(first, width), :].astype(BF16)


def act_kernel(parts_ref, cot_ref, act_ref, grad_ref):
    preact = parts_ref[0].astype(F32)
    for part in range(1, parts_ref.shape[0]):
        preact = preact + parts_ref[part].astype(F32)
    sigmoid_z = 1.0 / (1.0 + jnp.exp(-preact))
    act_ref[...] = (preact * sigmoid_z).astype(BF16)
    slope = sigmoid_z * (1.0 + preact * (1.0 - sigmoid_z))
    grad = (cot_ref[...].astype(F32) * slope).astype(BF16)
    for copy in range(grad_ref.shape[0]):
        grad_ref[copy] = grad


def weight_kernel(scale, grads_ref, own_ref, mean_ref, pieces_ref):
    groups, width, nodes = grads_ref.shape
    values = jnp.concatenate([own_ref[...], mean_ref[...]], axis=0)
    term = dot(values, grads_ref[...].reshape(groups * width, nodes), LAST) * scale
    pieces_ref[...] = term.astype(BF16).reshape(pieces_ref.shape)


def sum_kernel(in_ref, *refs):
    out_ref = refs[-1]
    total = in_ref[0].astype(F32)
    for part in range(1, in_ref.shape[0]):
        total = total + in_ref[part].astype(F32)
    total = total.astype(BF16)
    for copy in range(out_ref.shape[0]):
        out_ref[copy] = total


def final_kernel(in_ref, self_ref, neigh_ref):
    total = in_ref[...].astype(F32).reshape(in_ref.shape[0] * in_ref.shape[1], in_ref.shape[2])
    half = self_ref.shape[0]
    self_ref[...] = total[:half]
    neigh_ref[...] = total[half:]


def back_kernel(
    core_ref, grads_ref, wself_ref, wneigh_ref, weighted_ref, inverse_ref, behind_ref, ahead_ref, stays_ref, scratch
):
    groups, width, nodes = grads_ref.shape
    reach = (weighted_ref.shape[0] - 1) // 2
    depth = scratch.shape[0]
    core = core_ref[0]
    steps = core + 1
    grads = grads_ref[...].reshape(groups * width, nodes)
    wneigh = wneigh_ref[...].reshape(depth, groups * width)
    spread = (dot(wneigh, grads, PLAIN) * inverse_ref[0:1, :]).astype(BF16)
    behind_ref[...] = dot(spread, weighted_ref[reach - steps], PLAIN).astype(BF16)
    ahead_ref[...] = dot(spread, weighted_ref[reach + steps], PLAIN).astype(BF16)
    scratch[...] = dot(spread, weighted_ref[reach], PLAIN)
    own = scratch[pl.ds(pl.multiple_of(core * width, width), width), :]
    stays_ref[...] = dot(wself_ref[...], grads, PLAIN) + own


def out_kernel(core_ref, stays_ref, *refs):
    *term_refs, out_ref = refs
    width = out_ref.shape[0]
    total = stays_ref[...]
    rows = pl.ds(pl.multiple_of(core_ref[0] * width, width), width)
    for term_ref in term_refs:
        for part in range(term_ref.shape[0]):
            total = total + term_ref[part, rows, :].astype(F32)
    out_ref[...] = total.astype(BF16)


def shift(value, sign):
    axes = ROW + ("core",)
    cores = lax.axis_size("core")
    count = lax.axis_size(ROW)
    pairs = [
        (source * cores + core, (source + sign * (core + 1)) % count * cores + core)
        for source in range(count)
        for core in range(cores)
    ]
    return lax.ppermute(value, axes, pairs)


def of_chip(value):
    return lax.all_gather(value, "core", axis=0, tiled=False)


def exchange(chunks, axes):
    return lax.all_to_all(chunks, axes, 0, 0, tiled=True)


def body(features, adjacency, tile_mask, w_self, w_neigh, cotangent):
    own = features.T
    panel = width, nodes = own.shape
    groups = lax.axis_size(COL)
    lines = lax.axis_size("y")
    planes = lax.axis_size("z")
    total = groups * width
    cores = lax.axis_size("core")
    chips = lax.axis_size("x")
    depth = cores * width
    shape = jax.ShapeDtypeStruct
    wide = (depth, nodes)
    core = lax.axis_index("core").astype(jnp.int32).reshape(1)

    pair = of_chip(own)
    behind = shift(pair.reshape(wide), 1)
    ahead = shift(pair.reshape(wide), -1)
    wself_pair, wneigh_pair = of_chip(w_self), of_chip(w_neigh)
    adj = adjacency.transpose(1, 0, 2)
    weighted, base, inverse = local_call(
        mask_kernel,
        (shape(adj.shape, BF16), shape(wide, F32), shape((8, nodes), F32)),
        [SMEM, VMEM, VMEM],
        (tile_mask.transpose(0, 2, 1), pair, adj),
        2 * adj.size,
    )
    near = local_call(
        near_kernel,
        shape(wide, F32),
        [SMEM] + [VMEM] * 3,
        (core, behind, ahead, weighted),
        2 * adj.size,
    )
    mean, shares = local_call(
        mean_kernel,
        (shape(panel, BF16), shape((chips, *panel), BF16)),
        [SMEM] + [VMEM] * 6,
        (core, of_chip(near), base, inverse, pair, wself_pair, wneigh_pair),
        2 * adj.size,
        [(total, nodes)],
    )
    activated, copies = local_call(
        act_kernel,
        (shape(panel, BF16), shape((groups, *panel), BF16)),
        [VMEM] * 2,
        (exchange(shares, "x"), cotangent.T),
        adj.size,
    )
    grads = exchange(copies, COL)

    grad_scale = 1.0 / math.sqrt(lax.axis_size(ROW) * nodes)

    def weight_terms(*refs):
        weight_kernel(grad_scale, *refs)

    height = 2 * width // lines
    pieces = local_call(
        weight_terms,
        shape((lines, height, total), BF16),
        [VMEM] * 3,
        (grads, own, mean),
        adj.size,
    )
    over_y = exchange(pieces, "y")

    to_behind, to_ahead, stays = local_call(
        back_kernel,
        (shape(wide, BF16), shape(wide, BF16), shape(panel, F32)),
        [SMEM] + [VMEM] * 5,
        (core, grads, w_self, wneigh_pair, weighted, inverse),
        2 * adj.size,
        [wide],
    )
    arrived = [shift(to_behind, -1), shift(to_ahead, 1)]

    folded = local_call(
        sum_kernel,
        shape((planes, height, total), BF16),
        [VMEM],
        (over_y,),
        adj.size,
    )
    over_z = exchange(folded, "z")
    summed = local_call(
        sum_kernel,
        shape((lines, height, total), BF16),
        [VMEM] + [ANY] * len(arrived),
        (over_z, *arrived),
        adj.size,
    )
    gathered = exchange(summed, "y")
    grad_self, grad_neigh = local_call(
        final_kernel,
        (shape((width, total), F32), shape((width, total), F32)),
        [VMEM],
        (gathered,),
        adj.size,
    )
    grad_features = local_call(
        out_kernel,
        shape(panel, BF16),
        [SMEM] + [VMEM] * (1 + len(arrived)),
        (core, stays, *[of_chip(term) for term in arrived]),
        adj.size,
    )
    return (activated.T, grad_features.T, grad_self, grad_neigh)


def solution(mesh):
    rows, columns = mesh.devices.shape
    lines = math.gcd(rows, 8)
    cores = math.gcd(columns, 2)
    fine = Mesh(
        mesh.devices.reshape(rows // lines, lines, columns // cores, cores), ROW + COL
    )
    return jax.shard_map(
        body,
        mesh=fine,
        in_specs=(
            P(ROW, COL),
            P(ROW, None, None),
            P(ROW, None, None),
            P(COL, None),
            P(COL, None),
            P(ROW, COL),
        ),
        out_specs=(P(ROW, COL), P(ROW, COL), P(COL, None), P(COL, None)),
        check_vma=False,
    )
```

time: 125 us -> 113 us (0.904)
  the two profiles are of different devices: /device:TPU:2 before, /device:TPU:1 now
where the time goes in v4:
time: 113 us; the launch traced here: 111 us
  blocking collectives  61.8 us (55%)
  starting transfers between devices  27.4 us (24%)
  waiting for transfers between devices  8.99 us (8%)
  Pallas kernels  6.07 us (5%)
  local copies, waits for them, and re-layouts  5.54 us (5%)
    all_to_all x3, blocking collectives, exchange(): return lax.all_to_all(chunks, axes, 0, 0, tiled=True)  33.3 us
    all_gather x6, blocking collectives, of_chip(): return lax.all_gather(value, 'core', axis=0, tiled=False)  28.5 us
    ppermute x4, starting transfers between devices, shift(): return lax.ppermute(value, axes, pairs)  17.1 us
    all_to_all x2, starting transfers between devices, exchange(): return lax.all_to_all(chunks, axes, 0, 0, tiled=True)  10.3 us
    ppermute x4, waiting for transfers between devices, shift(): return lax.ppermute(value, axes, pairs)  8.98 us
    pallas_call x10, Pallas kernels, local_call(): pl.pallas_call(kernel, out_shape=out_shape, in_specs=in_specs, out_specs=...  6.07 us
    unnamed x20, local copies, waits for them, and re-layouts  5.54 us
  transfers between devices with their start and end apart: 6, of which 2 were waited for; matrix products, arithmetic and copies ran while one was open for 0% of the time, Pallas kernels for 3%

profile of v4, /device:TPU:1, one launch (start us, length us, event | category | flops | bytes accessed | tf_op | source)
XLA Modules:
  0.0 110.6 jit_solution(12333655514098747899)
XLA Ops:
  0.7 16.0 %all-gather = bf16[128,512]{1,0:T(8,128)(2,1)S(1)} all-gather(bf16[64,512]{1,0:T(8,128)(2,1)} %bitcast.22), channel_id=2, replica_groups=mesh['z'=16,'y'=8,'x'=4,'core'=2] {'core'}, dimensions={0}, use_global_device_ids=true | all-gather | bytes 196608 | tf_op jit(solution)/shard_map/all_gather | solution.py:171
  16.7 1.9 %collective-permute-start = (bf16[128,512]{1,0:T(8,128)(2,1)S(1)}, bf16[128,512]{1,0:T(8,128)(2,1)S(1)}, u32[]{:S(2)}, u32[]{:S(2)}) collective-permute-start(bf16[128,512]{1,0:T(8,128)(2,1)S(1)} %all-gather), channel_id=1, source_target_pairs={{0,8},{1,17},{8,16},{9,25},{16,24},{17,33},{24,32},{25,41},{32,40}... | collective-permute-start | bytes 393224 | tf_op jit(solution)/shard_map/ppermute | solution.py:167
  18.6 9.0 %collective-permute-start.1 = (bf16[128,512]{1,0:T(8,128)(2,1)S(1)}, bf16[128,512]{1,0:T(8,128)(2,1)S(1)}, u32[]{:S(2)}, u32[]{:S(2)}) collective-permute-start(bf16[128,512]{1,0:T(8,128)(2,1)S(1)} %all-gather), channel_id=1, source_target_pairs={{0,1016},{1,1009},{8,0},{9,1017},{16,8},{17,1},{24,16},{25,9},{32,... | collective-permute-start | bytes 393224 | tf_op jit(solution)/shard_map/ppermute | solution.py:167
  27.6 1.7 %copy-done = bf16[512,5,512]{2,0,1:T(8,128)(2,1)S(1)} copy-done((bf16[512,5,512]{2,0,1:T(8,128)(2,1)S(1)}, bf16[512,5,512]{2,0,1:T(8,128)(2,1)}, u32[]{:S(2)}) %copy-start) | copy-done | bytes 2621464
  29.4 0.7 copy-done.8
  30.1 1.5 %shard_map.93 = (bf16[5,512,512]{2,1,0:T(8,128)(2,1)S(1)}, f32[128,512]{1,0:T(8,128)S(1)}, f32[8,512]{1,0:T(8,128)S(1)}) custom-call(s32[4,4,5]{2,1,0:T(4,128)S(1)} %bitcast.25, bf16[2,64,512]{2,1,0:T(8,128)(2,1)S(1)} %bitcast.17, bf16[5,512,512]{2,1,0:T(8,128)(2,1)S(1)} %bitcast.13), custom_call_target="tpu_custom_call" | custom-call | flops 2621440 | bytes 5652800 | tf_op jit(solution)/shard_map/pallas_call | solution.py:27
  31.6 1.9 %all-gather.3 = bf16[128,512]{1,0:T(8,128)(2,1)S(1)} all-gather(bf16[64,512]{1,0:T(8,128)(2,1)S(1)} %copy-done.9), channel_id=5, replica_groups=mesh['z'=16,'y'=8,'x'=4,'core'=2] {'core'}, dimensions={0}, use_global_device_ids=true | all-gather | bytes 196608 | tf_op jit(solution)/shard_map/all_gather | solution.py:171
  33.5 1.9 %all-gather.2 = bf16[128,512]{1,0:T(8,128)(2,1)S(1)} all-gather(bf16[64,512]{1,0:T(8,128)(2,1)S(1)} %copy-done.3), channel_id=4, replica_groups=mesh['z'=16,'y'=8,'x'=4,'core'=2] {'core'}, dimensions={0}, use_global_device_ids=true | all-gather | bytes 196608 | tf_op jit(solution)/shard_map/all_gather | solution.py:171
  35.4 0.5 shard_map.94
  35.9 2.3 %all-gather.1 = f32[256,512]{1,0:T(8,128)S(1)} all-gather(f32[128,512]{1,0:T(8,128)S(1)} %shard_map.94), channel_id=3, replica_groups=mesh['z'=16,'y'=8,'x'=4,'core'=2] {'core'}, dimensions={0}, use_global_device_ids=true | all-gather | bytes 786432 | tf_op jit(solution)/shard_map/all_gather | solution.py:171
  38.2 0.3 shard_map.95
  38.6 10.1 %all_to_all.25.parts_ref = bf16[4,64,512]{2,1,0:T(8,128)(2,1)S(1)} all-to-all(bf16[4,64,512]{2,1,0:T(8,128)(2,1)S(1)} %get-tuple-element.19), channel_id=1, replica_groups=mesh['z'=16,'y'=8,'x'=4,'core'=2] {'x'}, dimensions={0} | all-to-all | bytes 524288 | tf_op jit(solution)/shard_map/all_to_all | solution.py:175
  48.7 0.7 shard_map.96
  49.4 13.0 %all_to_all.26.grads_ref.refs_0_ = bf16[8,64,512]{2,1,0:T(8,128)(2,1)S(1)} all-to-all(bf16[8,64,512]{2,1,0:T(8,128)(2,1)S(1)} %get-tuple-element.21), channel_id=1, replica_groups=mesh['z'=16,'y'=8,'x'=4,'core'=2] {'x','core'}, dimensions={0} | all-to-all | bytes 1048576 | tf_op jit(solution)/shard_map/all_to_all | solution.py:175
  62.5 0.3 shard_map.99
  62.8 10.1 %all_to_all.27.in_ref = bf16[8,16,512]{2,1,0:T(8,128)(2,1)S(1)} all-to-all(bf16[8,16,512]{2,1,0:T(8,128)(2,1)S(1)} %shard_map.99), channel_id=1, replica_groups=mesh['z'=16,'y'=8,'x'=4,'core'=2] {'y'}, dimensions={0} | all-to-all | bytes 262144 | tf_op jit(solution)/shard_map/all_to_all | solution.py:175
  73.0 0.7 copy-done.1
  73.7 6.9 %all-to-all-start.3 = ((bf16[16,16,512]{2,1,0:T(8,128)(2,1)}), bf16[16,16,512]{2,1,0:T(8,128)(2,1)S(1)}, u32[]{:S(2)}, u32[]{:S(2)}) async-start(bf16[16,16,512]{2,1,0:T(8,128)(2,1)} %copy-done.1), calls=%async_computation.3 | async-start | bytes 524288 | tf_op jit(solution)/shard_map/all_to_all | solution.py:175
  80.6 0.8 copy-done.4
  81.5 0.6 shard_map.97
  82.1 0.6 copy-done.5
  82.7 4.3 %collective-permute-start.2 = (bf16[128,512]{1,0:T(8,128)(2,1)S(1)}, bf16[128,512]{1,0:T(8,128)(2,1)S(1)}, u32[]{:S(2)}, u32[]{:S(2)}) collective-permute-start(bf16[128,512]{1,0:T(8,128)(2,1)S(1)} %get-tuple-element.23), channel_id=1, source_target_pairs={{0,1016},{1,1009},{8,0},{9,1017},{16,8},{17,1},{24,16},{25,9},{32,... | collective-permute-start | bytes 393224 | tf_op jit(solution)/shard_map/ppermute | solution.py:167
  87.0 1.9 %collective-permute-start.3 = (bf16[128,512]{1,0:T(8,128)(2,1)S(1)}, bf16[128,512]{1,0:T(8,128)(2,1)S(1)}, u32[]{:S(2)}, u32[]{:S(2)}) collective-permute-start(bf16[128,512]{1,0:T(8,128)(2,1)S(1)} %get-tuple-element.24), channel_id=1, source_target_pairs={{0,8},{1,17},{8,16},{9,25},{16,24},{17,33},{24,32},{25,41},{32,40}... | collective-permute-start | bytes 393224 | tf_op jit(solution)/shard_map/ppermute | solution.py:167
  89.0 4.8 %collective-permute-done.2.refs_0_ = bf16[128,512]{1,0:T(8,128)(2,1)S(1)} collective-permute-done((bf16[128,512]{1,0:T(8,128)(2,1)S(1)}, bf16[128,512]{1,0:T(8,128)(2,1)S(1)}, u32[]{:S(2)}, u32[]{:S(2)}) %collective-permute-start.2) | collective-permute-done | bytes 131104 | tf_op jit(solution)/shard_map/ppermute | solution.py:167
  93.8 4.2 %collective-permute-done.3.refs_1_ = bf16[128,512]{1,0:T(8,128)(2,1)S(1)} collective-permute-done((bf16[128,512]{1,0:T(8,128)(2,1)S(1)}, bf16[128,512]{1,0:T(8,128)(2,1)S(1)}, u32[]{:S(2)}, u32[]{:S(2)}) %collective-permute-start.3) | collective-permute-done | bytes 131104 | tf_op jit(solution)/shard_map/ppermute | solution.py:167
  98.0 0.7 shard_map.101
  98.7 3.4 %all-to-all-start.4 = ((bf16[8,16,512]{2,1,0:T(8,128)(2,1)}), bf16[8,16,512]{2,1,0:T(8,128)(2,1)S(1)}, u32[]{:S(2)}, u32[]{:S(2)}) async-start(bf16[8,16,512]{2,1,0:T(8,128)(2,1)} %shard_map.101), calls=%async_computation.4 | async-start | bytes 262144 | tf_op jit(solution)/shard_map/all_to_all | solution.py:175
  102.0 4.3 %all-gather.5 = bf16[256,512]{1,0:T(8,128)(2,1)S(1)} all-gather(bf16[128,512]{1,0:T(8,128)(2,1)S(1)} %collective-permute-done.3.refs_1_), channel_id=7, replica_groups=mesh['z'=16,'y'=8,'x'=4,'core'=2] {'core'}, dimensions={0}, use_global_device_ids=true | all-gather | bytes 393216 | tf_op jit(solution)/shard_map/all_gather | solution.py:171
  106.4 2.0 %all-gather.4 = bf16[256,512]{1,0:T(8,128)(2,1)S(1)} all-gather(bf16[128,512]{1,0:T(8,128)(2,1)S(1)} %collective-permute-done.2.refs_0_), channel_id=6, replica_groups=mesh['z'=16,'y'=8,'x'=4,'core'=2] {'core'}, dimensions={0}, use_global_device_ids=true | all-gather | bytes 393216 | tf_op jit(solution)/shard_map/all_gather | solution.py:171
  108.3 0.9 copy-done.6
  109.2 0.7 shard_map.98
  109.9 0.7 shard_map.102
  (19 shorter events, 0.1 us)
Async XLA Ops:
  0.6 31.0 %copy-start.9 = (bf16[64,512]{1,0:T(8,128)(2,1)S(1)}, bf16[64,512]{1,0:T(8,128)(2,1)}, u32[]{:S(2)}) copy-start(bf16[64,512]{1,0:T(8,128)(2,1)} %param.10) | copy-start | bytes 196612
  0.6 32.9 %copy-start.3 = (bf16[64,512]{1,0:T(8,128)(2,1)S(1)}, bf16[64,512]{1,0:T(8,128)(2,1)}, u32[]{:S(2)}) copy-start(bf16[64,512]{1,0:T(8,128)(2,1)} %wself_ref.1) | copy-start | bytes 196612
  16.7 18.7 %collective-permute-start = (bf16[128,512]{1,0:T(8,128)(2,1)S(1)}, bf16[128,512]{1,0:T(8,128)(2,1)S(1)}, u32[]{:S(2)}, u32[]{:S(2)}) collective-permute-start(bf16[128,512]{1,0:T(8,128)(2,1)S(1)} %all-gather), channel_id=1, source_target_pairs={{0,8},{1,17},{8,16},{9,25},{16,24},{17,33},{24,32},{25,41},{32,40}... | collective-permute-start | bytes 393224 | tf_op jit(solution)/shard_map/ppermute | solution.py:167
  18.6 16.8 %collective-permute-start.1 = (bf16[128,512]{1,0:T(8,128)(2,1)S(1)}, bf16[128,512]{1,0:T(8,128)(2,1)S(1)}, u32[]{:S(2)}, u32[]{:S(2)}) collective-permute-start(bf16[128,512]{1,0:T(8,128)(2,1)S(1)} %all-gather), channel_id=1, source_target_pairs={{0,1016},{1,1009},{8,0},{9,1017},{16,8},{17,1},{24,16},{25,9},{32,... | collective-permute-start | bytes 393224 | tf_op jit(solution)/shard_map/ppermute | solution.py:167
  27.6 1.7 %copy-start = (bf16[512,5,512]{2,0,1:T(8,128)(2,1)S(1)}, bf16[512,5,512]{2,0,1:T(8,128)(2,1)}, u32[]{:S(2)}) copy-start(bf16[512,5,512]{2,0,1:T(8,128)(2,1)} %param.7) | copy-start | bytes 7864324
  29.4 0.7 copy-start.8
  35.4 13.3 %copy-start.7 = (bf16[512,64]{0,1:T(8,128)(2,1)S(1)}, bf16[512,64]{0,1:T(8,128)(2,1)}, u32[]{:S(2)}) copy-start(bf16[512,64]{0,1:T(8,128)(2,1)} %param.11) | copy-start | bytes 196612
  35.9 26.6 %copy-start.2 = (bf16[512,64]{0,1:T(8,128)(2,1)S(1)}, bf16[512,64]{0,1:T(8,128)(2,1)}, u32[]{:S(2)}) copy-start(bf16[512,64]{0,1:T(8,128)(2,1)} %param.6) | copy-start | bytes 196612
  73.0 0.7 copy-start.1
  73.7 24.3 %all-to-all-start.3 = ((bf16[16,16,512]{2,1,0:T(8,128)(2,1)}), bf16[16,16,512]{2,1,0:T(8,128)(2,1)S(1)}, u32[]{:S(2)}, u32[]{:S(2)}) async-start(bf16[16,16,512]{2,1,0:T(8,128)(2,1)} %copy-done.1), calls=%async_computation.3 | async-start | bytes 524288 | tf_op jit(solution)/shard_map/all_to_all | solution.py:175
  80.6 0.8 copy-start.4
  82.1 0.7 copy-start.5
  82.7 11.0 %collective-permute-start.2 = (bf16[128,512]{1,0:T(8,128)(2,1)S(1)}, bf16[128,512]{1,0:T(8,128)(2,1)S(1)}, u32[]{:S(2)}, u32[]{:S(2)}) collective-permute-start(bf16[128,512]{1,0:T(8,128)(2,1)S(1)} %get-tuple-element.23), channel_id=1, source_target_pairs={{0,1016},{1,1009},{8,0},{9,1017},{16,8},{17,1},{24,16},{25,9},{32,... | collective-permute-start | bytes 393224 | tf_op jit(solution)/shard_map/ppermute | solution.py:167
  87.0 10.9 %collective-permute-start.3 = (bf16[128,512]{1,0:T(8,128)(2,1)S(1)}, bf16[128,512]{1,0:T(8,128)(2,1)S(1)}, u32[]{:S(2)}, u32[]{:S(2)}) collective-permute-start(bf16[128,512]{1,0:T(8,128)(2,1)S(1)} %get-tuple-element.24), channel_id=1, source_target_pairs={{0,8},{1,17},{8,16},{9,25},{16,24},{17,33},{24,32},{25,41},{32,40}... | collective-permute-start | bytes 393224 | tf_op jit(solution)/shard_map/ppermute | solution.py:167
  98.7 11.3 %all-to-all-start.4 = ((bf16[8,16,512]{2,1,0:T(8,128)(2,1)}), bf16[8,16,512]{2,1,0:T(8,128)(2,1)S(1)}, u32[]{:S(2)}, u32[]{:S(2)}) async-start(bf16[8,16,512]{2,1,0:T(8,128)(2,1)} %shard_map.101), calls=%async_computation.4 | async-start | bytes 262144 | tf_op jit(solution)/shard_map/all_to_all | solution.py:175
  108.3 0.9 copy-start.6

commit v5 on v4

--- a/solution.py
+++ b/solution.py
@@ -39,7 +39,8 @@
     return lax.dot_general(a, b, dims, preferred_element_type=F32)
 
 
-def mask_kernel(mask_ref, pair_ref, adj_ref, weighted_ref, base_ref, inverse_ref):
+def mask_kernel(mask_ref, pair_ref, adj_ref, *refs):
+    weighted_ref, base_ref, inverse_ref = refs[-3:]
     bands, nodes, _ = adj_ref.shape
     reach = (bands - 1) // 2
     depth = base_ref.shape[0]
@@ -78,8 +79,7 @@
     for part in range(cores):
         total = total + near_ref[part]
     mean = (total * inverse_ref[0:1, :]).astype(BF16)
-    scratch[:depth] = total * inverse_ref[0:1, :]
-    mean_ref[...] = scratch[pl.ds(pl.multiple_of(core * width, width), width), :].astype(BF16)
+    mean_ref[...] = mean
     weights = jnp.concatenate(
         [w[...].reshape(depth, w.shape[2]) for w in (wself_ref, wneigh_ref)], axis=0
     )
@@ -102,11 +102,20 @@
         grad_ref[copy] = grad
 
 
-def weight_kernel(scale, grads_ref, own_ref, mean_ref, pieces_ref):
-    groups, width, nodes = grads_ref.shape
-    values = jnp.concatenate([own_ref[...], mean_ref[...]], axis=0)
-    term = dot(values, grads_ref[...].reshape(groups * width, nodes), LAST) * scale
-    pieces_ref[...] = term.astype(BF16).reshape(pieces_ref.shape)
+def weight_kernel(scale, grads_ref, pair_ref, mean_ref, pieces_ref):
+    chips, width, nodes = grads_ref.shape
+    lines, cores, height, columns = pieces_ref.shape
+    values = [
+        ref[core * width : (core + 1) * width]
+        for core in range(cores)
+        for ref in (pair_ref[...].reshape(cores * width, nodes), mean_ref[...])
+    ]
+    grads = grads_ref[...].reshape(columns, nodes)
+    term = dot(jnp.concatenate(values, axis=0), grads, LAST) * scale
+    for line in range(lines):
+        for core in range(cores):
+            first = core * lines * height + line * height
+            pieces_ref[line, core] = term[first : first + height].astype(BF16)
 
 
 def sum_kernel(in_ref, *refs):
@@ -114,27 +123,36 @@
     total = in_ref[0].astype(F32)
     for part in range(1, in_ref.shape[0]):
         total = total + in_ref[part].astype(F32)
-    total = total.astype(BF16)
+    total = total.astype(BF16).reshape(out_ref.shape[1:])
     for copy in range(out_ref.shape[0]):
         out_ref[copy] = total
 
 
-def final_kernel(in_ref, self_ref, neigh_ref):
-    total = in_ref[...].astype(F32).reshape(in_ref.shape[0] * in_ref.shape[1], in_ref.shape[2])
+def final_kernel(width, in_ref, self_ref, neigh_ref):
+    lines, cores, height, columns = in_ref.shape
+    parts = [in_ref[:, core].reshape(lines * height, columns).astype(F32) for core in range(cores)]
     half = self_ref.shape[0]
-    self_ref[...] = total[:half]
-    neigh_ref[...] = total[half:]
+    for chip in range(columns // width):
+        both = jnp.concatenate(
+            [part[:, chip * width : (chip + 1) * width] for part in parts], axis=1
+        )
+        lanes = slice(chip * cores * width, (chip + 1) * cores * width)
+        self_ref[:, lanes] = both[:half]
+        neigh_ref[:, lanes] = both[half:]
 
 
 def back_kernel(
     core_ref, grads_ref, wself_ref, wneigh_ref, weighted_ref, inverse_ref, behind_ref, ahead_ref, stays_ref, scratch
 ):
-    groups, width, nodes = grads_ref.shape
+    cores, chips, width, nodes = grads_ref.shape
+    groups = cores * chips
     reach = (weighted_ref.shape[0] - 1) // 2
     depth = scratch.shape[0]
     core = core_ref[0]
     steps = core + 1
-    grads = grads_ref[...].reshape(groups * width, nodes)
+    grads = jnp.concatenate(
+        [grads_ref[part, chip] for chip in range(chips) for part in range(cores)], axis=0
+    )
     wneigh = wneigh_ref[...].reshape(depth, groups * width)
     spread = (dot(wneigh, grads, PLAIN) * inverse_ref[0:1, :]).astype(BF16)
     behind_ref[...] = dot(spread, weighted_ref[reach - steps], PLAIN).astype(BF16)
@@ -197,8 +215,8 @@
     weighted, base, inverse = local_call(
         mask_kernel,
         (shape(adj.shape, BF16), shape(wide, F32), shape((8, nodes), F32)),
-        [SMEM, VMEM, VMEM],
-        (tile_mask.transpose(0, 2, 1), pair, adj),
+        [SMEM, VMEM, VMEM, ANY, ANY],
+        (tile_mask.transpose(0, 2, 1), pair, adj, wself_pair, wneigh_pair),
         2 * adj.size,
     )
     near = local_call(
@@ -210,7 +228,7 @@
     )
     mean, shares = local_call(
         mean_kernel,
-        (shape(panel, BF16), shape((chips, *panel), BF16)),
+        (shape(wide, BF16), shape((chips, *panel), BF16)),
         [SMEM] + [VMEM] * 6,
         (core, of_chip(near), base, inverse, pair, wself_pair, wneigh_pair),
         2 * adj.size,
@@ -218,12 +236,12 @@
     )
     activated, copies = local_call(
         act_kernel,
-        (shape(panel, BF16), shape((groups, *panel), BF16)),
+        (shape(panel, BF16), shape((chips, *panel), BF16)),
         [VMEM] * 2,
         (exchange(shares, "x"), cotangent.T),
         adj.size,
     )
-    grads = exchange(copies, COL)
+    grads = exchange(copies, "x")
 
     grad_scale = 1.0 / math.sqrt(lax.axis_size(ROW) * nodes)
 
@@ -231,11 +249,12 @@
         weight_kernel(grad_scale, *refs)
 
     height = 2 * width // lines
+    piece = (cores, height, chips * width)
     pieces = local_call(
         weight_terms,
-        shape((lines, height, total), BF16),
+        shape((lines, *piece), BF16),
         [VMEM] * 3,
-        (grads, own, mean),
+        (grads, pair, mean),
         adj.size,
     )
     over_y = exchange(pieces, "y")
@@ -244,7 +263,7 @@
         back_kernel,
         (shape(wide, BF16), shape(wide, BF16), shape(panel, F32)),
         [SMEM] + [VMEM] * 5,
-        (core, grads, w_self, wneigh_pair, weighted, inverse),
+        (core, of_chip(grads), w_self, wneigh_pair, weighted, inverse),
         2 * adj.size,
         [wide],
     )
@@ -252,32 +271,37 @@
 
     folded = local_call(
         sum_kernel,
-        shape((planes, height, total), BF16),
-        [VMEM],
-        (over_y,),
+        shape((planes, *piece), BF16),
+        [VMEM, ANY],
+        (over_y, stays),
         adj.size,
     )
     over_z = exchange(folded, "z")
+    first, second = of_chip(arrived[0]), arrived[1]
     summed = local_call(
         sum_kernel,
-        shape((lines, height, total), BF16),
-        [VMEM] + [ANY] * len(arrived),
-        (over_z, *arrived),
-        adj.size,
-    )
-    gathered = exchange(summed, "y")
+        shape((lines, *piece), BF16),
+        [VMEM, ANY, ANY],
+        (over_z, first, second),
+        adj.size,
+    )
+    gathered = exchange(summed.reshape(lines * cores, *piece[1:]), ("y", "core"))
+
+    def final(*refs):
+        final_kernel(width, *refs)
+
     grad_self, grad_neigh = local_call(
-        final_kernel,
+        final,
         (shape((width, total), F32), shape((width, total), F32)),
         [VMEM],
-        (gathered,),
+        (gathered.reshape(lines, *piece),),
         adj.size,
     )
     grad_features = local_call(
         out_kernel,
         shape(panel, BF16),
         [SMEM] + [VMEM] * (1 + len(arrived)),
-        (core, stays, *[of_chip(term) for term in arrived]),
+        (core, stays, first, of_chip(second)),
         adj.size,
     )
     return (activated.T, grad_features.T, grad_self, grad_neigh)

time: 113 us -> 112 us (level); the launches traced: 111 us -> 111 us
  blocking collectives: 61.8 us -> 50.1 us
  starting transfers between devices: 27.4 us -> 34.5 us
  waiting for transfers between devices: 8.99 us -> 15.9 us
  local copies, waits for them, and re-layouts: 5.54 us -> 2.45 us
  Pallas kernels: 6.07 us -> 7.52 us
    all_to_all x3 -> x2, blocking collectives: 33.3 us -> 18.1 us  [exchange(): return lax.all_to_all(chunks, axes, 0, 0, tiled=True)]
    all_to_all x2 -> x3, waiting for transfers between devices: 0.01 us -> 9.59 us  [exchange(): return lax.all_to_all(chunks, axes, 0, 0, tiled=True)]
    all_to_all x2 -> x3, starting transfers between devices: 10.3 us -> 16.4 us  [exchange(): return lax.all_to_all(chunks, axes, 0, 0, tiled=True)]
    all_gather x6 -> x7, blocking collectives: 28.5 us -> 32.1 us  [of_chip(): return lax.all_gather(value, 'core', axis=0, tiled=False)]
    unnamed x20 -> x8, local copies, waits for them, and re-layouts: 5.54 us -> 2.45 us
    ppermute x4, waiting for transfers between devices: 8.98 us -> 6.34 us  [shift(): return lax.ppermute(value, axes, pairs)]
    pallas_call x10, Pallas kernels: 6.07 us -> 7.52 us  [local_call(): pl.pallas_call(kernel, out_shape=out_shape, in_specs=in_specs, out_specs=...]
  transfers between devices with their start and end apart: 6 -> 7, of which waited for: 2 -> 4; matrix products, arithmetic and copies ran while one was open for 0% -> 0% of each run, Pallas kernels for 3% -> 3%
where the time goes in v5:
time: 112 us; the launch traced here: 111 us
  blocking collectives  50.1 us (45%)
  starting transfers between devices  34.5 us (31%)
  waiting for transfers between devices  15.9 us (14%)
  Pallas kernels  7.52 us (7%)
  local copies, waits for them, and re-layouts  2.45 us (2%)
    all_gather x7, blocking collectives, of_chip(): return lax.all_gather(value, 'core', axis=0, tiled=False)  32.1 us
    ppermute x4, starting transfers between devices, shift(): return lax.ppermute(value, axes, pairs)  18.1 us
    all_to_all x2, blocking collectives, exchange(): return lax.all_to_all(chunks, axes, 0, 0, tiled=True)  18.1 us
    all_to_all x3, starting transfers between devices, exchange(): return lax.all_to_all(chunks, axes, 0, 0, tiled=True)  16.4 us
    all_to_all x3, waiting for transfers between devices, exchange(): return lax.all_to_all(chunks, axes, 0, 0, tiled=True)  9.59 us
    pallas_call x10, Pallas kernels, local_call(): pl.pallas_call(kernel, out_shape=out_shape, in_specs=in_specs, out_specs=...  7.52 us
    ppermute x4, waiting for transfers between devices, shift(): return lax.ppermute(value, axes, pairs)  6.34 us
    unnamed x8, local copies, waits for them, and re-layouts  2.45 us
  transfers between devices with their start and end apart: 7, of which 4 were waited for; matrix products, arithmetic and copies ran while one was open for 0% of the time, Pallas kernels for 3%

profile of v5, /device:TPU:1, one launch (start us, length us, event | category | flops | bytes accessed | tf_op | source)
XLA Modules:
  0.0 111.2 jit_solution(2393423569812594609)
XLA Ops:
  0.6 15.9 %all-gather = bf16[128,512]{1,0:T(8,128)(2,1)S(1)} all-gather(bf16[64,512]{1,0:T(8,128)(2,1)} %bitcast.33), channel_id=2, replica_groups=mesh['z'=16,'y'=8,'x'=4,'core'=2] {'core'}, dimensions={0}, use_global_device_ids=true | all-gather | bytes 196608 | tf_op jit(solution)/shard_map/all_gather | solution.py:189
  16.5 1.9 %collective-permute-start = (bf16[128,512]{1,0:T(8,128)(2,1)S(1)}, bf16[128,512]{1,0:T(8,128)(2,1)S(1)}, u32[]{:S(2)}, u32[]{:S(2)}) collective-permute-start(bf16[128,512]{1,0:T(8,128)(2,1)S(1)} %all-gather), channel_id=1, source_target_pairs={{0,8},{1,17},{8,16},{9,25},{16,24},{17,33},{24,32},{25,41},{32,40}... | collective-permute-start | bytes 393224 | tf_op jit(solution)/shard_map/ppermute | solution.py:185
  18.5 9.0 %collective-permute-start.1 = (bf16[128,512]{1,0:T(8,128)(2,1)S(1)}, bf16[128,512]{1,0:T(8,128)(2,1)S(1)}, u32[]{:S(2)}, u32[]{:S(2)}) collective-permute-start(bf16[128,512]{1,0:T(8,128)(2,1)S(1)} %all-gather), channel_id=1, source_target_pairs={{0,1016},{1,1009},{8,0},{9,1017},{16,8},{17,1},{24,16},{25,9},{32,... | collective-permute-start | bytes 393224 | tf_op jit(solution)/shard_map/ppermute | solution.py:185
  27.5 2.1 %all-gather.2 = bf16[128,512]{1,0:T(8,128)(2,1)S(1)} all-gather(bf16[64,512]{1,0:T(8,128)(2,1)} %param.10), channel_id=4, replica_groups=mesh['z'=16,'y'=8,'x'=4,'core'=2] {'core'}, dimensions={0}, use_global_device_ids=true | all-gather | bytes 196608 | tf_op jit(solution)/shard_map/all_gather | solution.py:189
  29.6 2.1 %all-gather.1 = bf16[128,512]{1,0:T(8,128)(2,1)S(1)} all-gather(bf16[64,512]{1,0:T(8,128)(2,1)} %wself_ref.1), channel_id=3, replica_groups=mesh['z'=16,'y'=8,'x'=4,'core'=2] {'core'}, dimensions={0}, use_global_device_ids=true | all-gather | bytes 196608 | tf_op jit(solution)/shard_map/all_gather | solution.py:189
  31.7 1.7 %copy-done = bf16[512,5,512]{2,0,1:T(8,128)(2,1)S(1)} copy-done((bf16[512,5,512]{2,0,1:T(8,128)(2,1)S(1)}, bf16[512,5,512]{2,0,1:T(8,128)(2,1)}, u32[]{:S(2)}) %copy-start) | copy-done | bytes 2621464
  33.4 0.7 copy-done.3
  34.1 1.5 %shard_map.93 = (bf16[5,512,512]{2,1,0:T(8,128)(2,1)S(1)}, f32[128,512]{1,0:T(8,128)S(1)}, f32[8,512]{1,0:T(8,128)S(1)}) custom-call(s32[4,4,5]{2,1,0:T(4,128)S(1)} %bitcast.32, bf16[2,64,512]{2,1,0:T(8,128)(2,1)S(1)} %bitcast.19, bf16[5,512,512]{2,1,0:T(8,128)(2,1)S(1)} %bitcast.16, bf16[2,64,512]{2,1,0:T(8,128)(2,1)S(1)} %bitcast.27, ...), custom_call_target="tpu_custom_call" | custom-call | flops 2621440 | bytes 5914944 | tf_op jit(solution)/shard_map/pallas_call | solution.py:27
  35.7 0.5 shard_map.94
  36.2 2.3 %all-gather.3 = f32[256,512]{1,0:T(8,128)S(1)} all-gather(f32[128,512]{1,0:T(8,128)S(1)} %shard_map.94), channel_id=5, replica_groups=mesh['z'=16,'y'=8,'x'=4,'core'=2] {'core'}, dimensions={0}, use_global_device_ids=true | all-gather | bytes 786432 | tf_op jit(solution)/shard_map/all_gather | solution.py:189
  38.5 0.4 shard_map.95
  38.9 10.2 %all_to_all.25.parts_ref = bf16[4,64,512]{2,1,0:T(8,128)(2,1)S(1)} all-to-all(bf16[4,64,512]{2,1,0:T(8,128)(2,1)S(1)} %get-tuple-element.19), channel_id=1, replica_groups=mesh['z'=16,'y'=8,'x'=4,'core'=2] {'x'}, dimensions={0} | all-to-all | bytes 524288 | tf_op jit(solution)/shard_map/all_to_all | solution.py:193
  49.0 0.7 shard_map.96
  49.7 7.9 %all_to_all.26.refs_0_ = bf16[4,64,512]{2,1,0:T(8,128)(2,1)S(1)} all-to-all(bf16[4,64,512]{2,1,0:T(8,128)(2,1)S(1)} %get-tuple-element.21), channel_id=1, replica_groups=mesh['z'=16,'y'=8,'x'=4,'core'=2] {'x'}, dimensions={0} | all-to-all | bytes 524288 | tf_op jit(solution)/shard_map/all_to_all | solution.py:193
  57.6 0.9 shard_map.99
  58.6 3.4 %all-to-all-start.2 = ((bf16[8,2,16,256]{3,2,1,0:T(8,128)(2,1)}), bf16[8,2,16,256]{3,2,1,0:T(8,128)(2,1)S(1)}, u32[]{:S(2)}, u32[]{:S(2)}) async-start(bf16[8,2,16,256]{3,2,1,0:T(8,128)(2,1)} %shard_map.99), calls=%async_computation.2 | async-start | bytes 262144 | tf_op jit(solution)/shard_map/all_to_all | solution.py:193
  61.9 4.2 %all-gather.4 = bf16[8,64,512]{2,1,0:T(8,128)(2,1)S(1)} all-gather(bf16[4,64,512]{2,1,0:T(8,128)(2,1)S(1)} %all_to_all.26.refs_0_), channel_id=6, replica_groups=mesh['z'=16,'y'=8,'x'=4,'core'=2] {'core'}, dimensions={0}, use_global_device_ids=true | all-gather | bytes 786432 | tf_op jit(solution)/shard_map/all_gather | solution.py:189
  66.2 0.6 shard_map.97
  66.8 3.1 %all-to-all-done.2.in_ref = bf16[8,2,16,256]{3,2,1,0:T(8,128)(2,1)S(1)} async-done(((bf16[8,2,16,256]{3,2,1,0:T(8,128)(2,1)}), bf16[8,2,16,256]{3,2,1,0:T(8,128)(2,1)S(1)}, u32[]{:S(2)}, u32[]{:S(2)}) %all-to-all-start.2) | async-done | bytes 131104 | tf_op jit(solution)/shard_map/all_to_all | solution.py:193
  69.9 0.7 shard_map.100
  70.6 5.9 %all-to-all-start.3 = ((bf16[16,2,16,256]{3,2,1,0:T(8,128)(2,1)}), bf16[16,2,16,256]{3,2,1,0:T(8,128)(2,1)S(1)}, u32[]{:S(2)}, u32[]{:S(2)}) async-start(bf16[16,2,16,256]{3,2,1,0:T(8,128)(2,1)} %shard_map.100), calls=%async_computation.3 | async-start | bytes 524288 | tf_op jit(solution)/shard_map/all_to_all | solution.py:193
  76.5 5.3 %collective-permute-start.2 = (bf16[128,512]{1,0:T(8,128)(2,1)S(1)}, bf16[128,512]{1,0:T(8,128)(2,1)S(1)}, u32[]{:S(2)}, u32[]{:S(2)}) collective-permute-start(bf16[128,512]{1,0:T(8,128)(2,1)S(1)} %get-tuple-element.23), channel_id=1, source_target_pairs={{0,1016},{1,1009},{8,0},{9,1017},{16,8},{17,1},{24,16},{25,9},{32,... | collective-permute-start | bytes 393224 | tf_op jit(solution)/shard_map/ppermute | solution.py:185
  81.7 1.9 %collective-permute-start.3 = (bf16[128,512]{1,0:T(8,128)(2,1)S(1)}, bf16[128,512]{1,0:T(8,128)(2,1)S(1)}, u32[]{:S(2)}, u32[]{:S(2)}) collective-permute-start(bf16[128,512]{1,0:T(8,128)(2,1)S(1)} %get-tuple-element.24), channel_id=1, source_target_pairs={{0,8},{1,17},{8,16},{9,25},{16,24},{17,33},{24,32},{25,41},{32,40}... | collective-permute-start | bytes 393224 | tf_op jit(solution)/shard_map/ppermute | solution.py:185
  83.7 6.0 %collective-permute-done.2 = bf16[128,512]{1,0:T(8,128)(2,1)S(1)} collective-permute-done((bf16[128,512]{1,0:T(8,128)(2,1)S(1)}, bf16[128,512]{1,0:T(8,128)(2,1)S(1)}, u32[]{:S(2)}, u32[]{:S(2)}) %collective-permute-start.2) | collective-permute-done | bytes 131104 | tf_op jit(solution)/shard_map/ppermute | solution.py:185
  89.7 3.4 %all-gather.5 = bf16[256,512]{1,0:T(8,128)(2,1)S(1)} all-gather(bf16[128,512]{1,0:T(8,128)(2,1)S(1)} %collective-permute-done.2), channel_id=7, replica_groups=mesh['z'=16,'y'=8,'x'=4,'core'=2] {'core'}, dimensions={0}, use_global_device_ids=true | all-gather | bytes 393216 | tf_op jit(solution)/shard_map/all_gather | solution.py:189
  93.1 0.3 collective-permute-done.3.refs_1_
  93.4 0.7 shard_map.101
  94.1 7.2 %all-to-all-start.4 = ((bf16[16,16,256]{2,1,0:T(8,128)(2,1)}), bf16[16,16,256]{2,1,0:T(8,128)(2,1)S(1)}, u32[]{:S(2)}, u32[]{:S(2)}) async-start(bf16[16,16,256]{2,1,0:T(8,128)(2,1)} %bitcast.14), calls=%async_computation.4 | async-start | bytes 262144 | tf_op jit(solution)/shard_map/all_to_all | solution.py:193
  101.3 2.0 %all-gather.6 = bf16[256,512]{1,0:T(8,128)(2,1)S(1)} all-gather(bf16[128,512]{1,0:T(8,128)(2,1)S(1)} %collective-permute-done.3.refs_1_), channel_id=8, replica_groups=mesh['z'=16,'y'=8,'x'=4,'core'=2] {'core'}, dimensions={0}, use_global_device_ids=true | all-gather | bytes 393216 | tf_op jit(solution)/shard_map/all_gather | solution.py:189
  103.2 0.7 shard_map.98
  103.9 6.5 %all-to-all-done.4 = bf16[16,16,256]{2,1,0:T(8,128)(2,1)S(1)} async-done(((bf16[16,16,256]{2,1,0:T(8,128)(2,1)}), bf16[16,16,256]{2,1,0:T(8,128)(2,1)S(1)}, u32[]{:S(2)}, u32[]{:S(2)}) %all-to-all-start.4) | async-done | bytes 131104 | tf_op jit(solution)/shard_map/all_to_all | solution.py:193
  110.4 0.8 shard_map.102
  (9 shorter events, 0.0 us)
Async XLA Ops:
  16.5 19.1 %collective-permute-start = (bf16[128,512]{1,0:T(8,128)(2,1)S(1)}, bf16[128,512]{1,0:T(8,128)(2,1)S(1)}, u32[]{:S(2)}, u32[]{:S(2)}) collective-permute-start(bf16[128,512]{1,0:T(8,128)(2,1)S(1)} %all-gather), channel_id=1, source_target_pairs={{0,8},{1,17},{8,16},{9,25},{16,24},{17,33},{24,32},{25,41},{32,40}... | collective-permute-start | bytes 393224 | tf_op jit(solution)/shard_map/ppermute | solution.py:185
  18.5 17.2 %collective-permute-start.1 = (bf16[128,512]{1,0:T(8,128)(2,1)S(1)}, bf16[128,512]{1,0:T(8,128)(2,1)S(1)}, u32[]{:S(2)}, u32[]{:S(2)}) collective-permute-start(bf16[128,512]{1,0:T(8,128)(2,1)S(1)} %all-gather), channel_id=1, source_target_pairs={{0,1016},{1,1009},{8,0},{9,1017},{16,8},{17,1},{24,16},{25,9},{32,... | collective-permute-start | bytes 393224 | tf_op jit(solution)/shard_map/ppermute | solution.py:185
  31.7 1.7 %copy-start = (bf16[512,5,512]{2,0,1:T(8,128)(2,1)S(1)}, bf16[512,5,512]{2,0,1:T(8,128)(2,1)}, u32[]{:S(2)}) copy-start(bf16[512,5,512]{2,0,1:T(8,128)(2,1)} %param.7) | copy-start | bytes 7864324
  33.4 0.7 copy-start.3
  35.7 13.3 %copy-start.2 = (bf16[512,64]{0,1:T(8,128)(2,1)S(1)}, bf16[512,64]{0,1:T(8,128)(2,1)}, u32[]{:S(2)}) copy-start(bf16[512,64]{0,1:T(8,128)(2,1)} %param.11) | copy-start | bytes 196612
  36.2 30.0 %copy-start.1 = (bf16[64,512]{1,0:T(8,128)(2,1)S(1)}, bf16[64,512]{1,0:T(8,128)(2,1)}, u32[]{:S(2)}) copy-start(bf16[64,512]{1,0:T(8,128)(2,1)} %wself_ref.1) | copy-start | bytes 196612
  58.6 11.3 %all-to-all-start.2 = ((bf16[8,2,16,256]{3,2,1,0:T(8,128)(2,1)}), bf16[8,2,16,256]{3,2,1,0:T(8,128)(2,1)S(1)}, u32[]{:S(2)}, u32[]{:S(2)}) async-start(bf16[8,2,16,256]{3,2,1,0:T(8,128)(2,1)} %shard_map.99), calls=%async_computation.2 | async-start | bytes 262144 | tf_op jit(solution)/shard_map/all_to_all | solution.py:193
  70.6 22.8 %all-to-all-start.3 = ((bf16[16,2,16,256]{3,2,1,0:T(8,128)(2,1)}), bf16[16,2,16,256]{3,2,1,0:T(8,128)(2,1)S(1)}, u32[]{:S(2)}, u32[]{:S(2)}) async-start(bf16[16,2,16,256]{3,2,1,0:T(8,128)(2,1)} %shard_map.100), calls=%async_computation.3 | async-start | bytes 524288 | tf_op jit(solution)/shard_map/all_to_all | solution.py:193
  76.5 13.2 %collective-permute-start.2 = (bf16[128,512]{1,0:T(8,128)(2,1)S(1)}, bf16[128,512]{1,0:T(8,128)(2,1)S(1)}, u32[]{:S(2)}, u32[]{:S(2)}) collective-permute-start(bf16[128,512]{1,0:T(8,128)(2,1)S(1)} %get-tuple-element.23), channel_id=1, source_target_pairs={{0,1016},{1,1009},{8,0},{9,1017},{16,8},{17,1},{24,16},{25,9},{32,... | collective-permute-start | bytes 393224 | tf_op jit(solution)/shard_map/ppermute | solution.py:185
  81.7 11.7 %collective-permute-start.3 = (bf16[128,512]{1,0:T(8,128)(2,1)S(1)}, bf16[128,512]{1,0:T(8,128)(2,1)S(1)}, u32[]{:S(2)}, u32[]{:S(2)}) collective-permute-start(bf16[128,512]{1,0:T(8,128)(2,1)S(1)} %get-tuple-element.24), channel_id=1, source_target_pairs={{0,8},{1,17},{8,16},{9,25},{16,24},{17,33},{24,32},{25,41},{32,40}... | collective-permute-start | bytes 393224 | tf_op jit(solution)/shard_map/ppermute | solution.py:185
  94.1 16.3 %all-to-all-start.4 = ((bf16[16,16,256]{2,1,0:T(8,128)(2,1)}), bf16[16,16,256]{2,1,0:T(8,128)(2,1)S(1)}, u32[]{:S(2)}, u32[]{:S(2)}) async-start(bf16[16,16,256]{2,1,0:T(8,128)(2,1)} %bitcast.14), calls=%async_computation.4 | async-start | bytes 262144 | tf_op jit(solution)/shard_map/all_to_all | solution.py:193

commit v6 on v5

--- a/solution.py
+++ b/solution.py
@@ -8,7 +8,8 @@
 from jax.sharding import Mesh
 from jax.sharding import PartitionSpec as P
 
-ROW = ("z", "y")
+ROW = ("far", "near", "y")
+BLOCK = ("near", "y")
 COL = ("x", "core")
 TILE = 128
 LAST = (((1,), (1,)), ((), ()))
@@ -70,7 +71,7 @@
 
 
 def mean_kernel(
-    core_ref, near_ref, base_ref, inverse_ref, pair_ref, wself_ref, wneigh_ref, mean_ref, out_ref, scratch
+    core_ref, near_ref, base_ref, inverse_ref, pair_ref, weights_ref, mean_ref, out_ref, scratch
 ):
     cores, width, nodes = pair_ref.shape
     depth = cores * width
@@ -80,10 +81,15 @@
         total = total + near_ref[part]
     mean = (total * inverse_ref[0:1, :]).astype(BF16)
     mean_ref[...] = mean
-    weights = jnp.concatenate(
-        [w[...].reshape(depth, w.shape[2]) for w in (wself_ref, wneigh_ref)], axis=0
-    )
-    values = jnp.concatenate([pair_ref[...].reshape(depth, nodes), mean], axis=0)
+    values = jnp.concatenate(
+        [
+            part[first : first + width]
+            for first in range(0, depth, width)
+            for part in (pair_ref[...].reshape(depth, nodes), mean)
+        ],
+        axis=0,
+    )
+    weights = weights_ref[...].reshape(2 * depth, weights_ref.shape[2])
     scratch[...] = dot(weights, values, FIRST)
     for chip in range(out_ref.shape[0]):
         first = pl.multiple_of((chip * cores + core) * width, width)
@@ -104,7 +110,9 @@
 
 def weight_kernel(scale, grads_ref, pair_ref, mean_ref, pieces_ref):
     chips, width, nodes = grads_ref.shape
-    lines, cores, height, columns = pieces_ref.shape
+    lines, rows, columns = pieces_ref.shape
+    cores = pair_ref.shape[0]
+    height = rows // cores
     values = [
         ref[core * width : (core + 1) * width]
         for core in range(cores)
@@ -113,9 +121,11 @@
     grads = grads_ref[...].reshape(columns, nodes)
     term = dot(jnp.concatenate(values, axis=0), grads, LAST) * scale
     for line in range(lines):
-        for core in range(cores):
-            first = core * lines * height + line * height
-            pieces_ref[line, core] = term[first : first + height].astype(BF16)
+        parts = [
+            term[first : first + height]
+            for first in range(line * height, lines * rows, lines * height)
+        ]
+        pieces_ref[line] = jnp.concatenate(parts, axis=0).astype(BF16)
 
 
 def sum_kernel(in_ref, *refs):
@@ -123,26 +133,50 @@
     total = in_ref[0].astype(F32)
     for part in range(1, in_ref.shape[0]):
         total = total + in_ref[part].astype(F32)
-    total = total.astype(BF16).reshape(out_ref.shape[1:])
+    total = total.astype(BF16)
     for copy in range(out_ref.shape[0]):
         out_ref[copy] = total
 
 
+def share_kernel(in_ref, *refs):
+    out_ref = refs[-1]
+    lines, cores, rows, lanes = out_ref.shape
+    total = in_ref[0].astype(F32)
+    for part in range(1, in_ref.shape[0]):
+        total = total + in_ref[part].astype(F32)
+    height = total.shape[0] // cores
+    for core in range(cores):
+        mine = total[core * height : (core + 1) * height]
+        folded = [mine[:, first : first + lanes] for first in range(0, mine.shape[1], lanes)]
+        share = jnp.concatenate(folded, axis=0).astype(BF16)
+        for line in range(lines):
+            out_ref[line, core] = share
+
+
 def final_kernel(width, in_ref, self_ref, neigh_ref):
-    lines, cores, height, columns = in_ref.shape
-    parts = [in_ref[:, core].reshape(lines * height, columns).astype(F32) for core in range(cores)]
+    lines, cores, rows, lanes = in_ref.shape
+    total = in_ref[...].astype(F32)
     half = self_ref.shape[0]
-    for chip in range(columns // width):
+    height = 2 * half // lines
+    chips = self_ref.shape[1] // (cores * width)
+    for chip in range(chips):
+        fold, first = divmod(chip * width, lanes)
         both = jnp.concatenate(
-            [part[:, chip * width : (chip + 1) * width] for part in parts], axis=1
+            [
+                total[:, core, fold * height : (fold + 1) * height, first : first + width].reshape(
+                    2 * half, width
+                )
+                for core in range(cores)
+            ],
+            axis=1,
         )
-        lanes = slice(chip * cores * width, (chip + 1) * cores * width)
-        self_ref[:, lanes] = both[:half]
-        neigh_ref[:, lanes] = both[half:]
+        columns = slice(chip * cores * width, (chip + 1) * cores * width)
+        self_ref[:, columns] = both[:half]
+        neigh_ref[:, columns] = both[half:]
 
 
 def back_kernel(
-    core_ref, grads_ref, wself_ref, wneigh_ref, weighted_ref, inverse_ref, behind_ref, ahead_ref, stays_ref, scratch
+    core_ref, grads_ref, wself_ref, weights_ref, weighted_ref, inverse_ref, behind_ref, ahead_ref, stays_ref, scratch
 ):
     cores, chips, width, nodes = grads_ref.shape
     groups = cores * chips
@@ -153,7 +187,7 @@
     grads = jnp.concatenate(
         [grads_ref[part, chip] for chip in range(chips) for part in range(cores)], axis=0
     )
-    wneigh = wneigh_ref[...].reshape(depth, groups * width)
+    wneigh = weights_ref[:, width:].reshape(depth, groups * width)
     spread = (dot(wneigh, grads, PLAIN) * inverse_ref[0:1, :]).astype(BF16)
     behind_ref[...] = dot(spread, weighted_ref[reach - steps], PLAIN).astype(BF16)
     ahead_ref[...] = dot(spread, weighted_ref[reach + steps], PLAIN).astype(BF16)
@@ -197,8 +231,8 @@
     own = features.T
     panel = width, nodes = own.shape
     groups = lax.axis_size(COL)
-    lines = lax.axis_size("y")
-    planes = lax.axis_size("z")
+    lines = lax.axis_size(BLOCK)
+    planes = lax.axis_size("far")
     total = groups * width
     cores = lax.axis_size("core")
     chips = lax.axis_size("x")
@@ -210,13 +244,13 @@
     pair = of_chip(own)
     behind = shift(pair.reshape(wide), 1)
     ahead = shift(pair.reshape(wide), -1)
-    wself_pair, wneigh_pair = of_chip(w_self), of_chip(w_neigh)
+    weights = of_chip(jnp.concatenate([w_self, w_neigh], axis=0))
     adj = adjacency.transpose(1, 0, 2)
     weighted, base, inverse = local_call(
         mask_kernel,
         (shape(adj.shape, BF16), shape(wide, F32), shape((8, nodes), F32)),
-        [SMEM, VMEM, VMEM, ANY, ANY],
-        (tile_mask.transpose(0, 2, 1), pair, adj, wself_pair, wneigh_pair),
+        [SMEM, VMEM, VMEM, ANY],
+        (tile_mask.transpose(0, 2, 1), pair, adj, weights),
         2 * adj.size,
     )
     near = local_call(
@@ -229,8 +263,8 @@
     mean, shares = local_call(
         mean_kernel,
         (shape(wide, BF16), shape((chips, *panel), BF16)),
-        [SMEM] + [VMEM] * 6,
-        (core, of_chip(near), base, inverse, pair, wself_pair, wneigh_pair),
+        [SMEM] + [VMEM] * 5,
+        (core, of_chip(near), base, inverse, pair, weights),
         2 * adj.size,
         [(total, nodes)],
     )
@@ -249,7 +283,7 @@
         weight_kernel(grad_scale, *refs)
 
     height = 2 * width // lines
-    piece = (cores, height, chips * width)
+    piece = (cores * height, chips * width)
     pieces = local_call(
         weight_terms,
         shape((lines, *piece), BF16),
@@ -257,13 +291,13 @@
         (grads, pair, mean),
         adj.size,
     )
-    over_y = exchange(pieces, "y")
+    over_block = exchange(pieces, BLOCK)
 
     to_behind, to_ahead, stays = local_call(
         back_kernel,
         (shape(wide, BF16), shape(wide, BF16), shape(panel, F32)),
         [SMEM] + [VMEM] * 5,
-        (core, of_chip(grads), w_self, wneigh_pair, weighted, inverse),
+        (core, of_chip(grads), w_self, weights, weighted, inverse),
         2 * adj.size,
         [wide],
     )
@@ -273,19 +307,20 @@
         sum_kernel,
         shape((planes, *piece), BF16),
         [VMEM, ANY],
-        (over_y, stays),
-        adj.size,
-    )
-    over_z = exchange(folded, "z")
+        (over_block, stays),
+        adj.size,
+    )
+    over_far = exchange(folded, "far")
     first, second = of_chip(arrived[0]), arrived[1]
+    share = (lines, cores, height * chips * width // TILE, TILE)
     summed = local_call(
-        sum_kernel,
-        shape((lines, *piece), BF16),
+        share_kernel,
+        shape(share, BF16),
         [VMEM, ANY, ANY],
-        (over_z, first, second),
-        adj.size,
-    )
-    gathered = exchange(summed.reshape(lines * cores, *piece[1:]), ("y", "core"))
+        (over_far, first, second),
+        adj.size,
+    )
+    gathered = exchange(summed.reshape(lines * cores, *share[2:]), BLOCK + ("core",))
 
     def final(*refs):
         final_kernel(width, *refs)
@@ -294,7 +329,7 @@
         final,
         (shape((width, total), F32), shape((width, total), F32)),
         [VMEM],
-        (gathered.reshape(lines, *piece),),
+        (gathered.reshape(share),),
         adj.size,
     )
     grad_features = local_call(
@@ -310,10 +345,10 @@
 def solution(mesh):
     rows, columns = mesh.devices.shape
     lines = math.gcd(rows, 8)
+    near = math.gcd(rows // lines, 2)
     cores = math.gcd(columns, 2)
-    fine = Mesh(
-        mesh.devices.reshape(rows // lines, lines, columns // cores, cores), ROW + COL
-    )
+    sizes = (rows // lines // near, near, lines, columns // cores, cores)
+    fine = Mesh(mesh.devices.reshape(sizes), ROW + COL)
     return jax.shard_map(
         body,
         mesh=fine,

time: 112 us -> 110 us (0.982)
  waiting for transfers between devices: 15.9 us -> 11.5 us
  starting transfers between devices: 34.5 us -> 36.3 us
    ppermute x4, waiting for transfers between devices: 6.34 us -> 3.35 us  [shift(): return lax.ppermute(value, axes, pairs)]
    all_to_all x3, waiting for transfers between devices: 9.59 us -> 8.11 us  [exchange(): return lax.all_to_all(chunks, axes, 0, 0, tiled=True)]
    ppermute x4, starting transfers between devices: 18.1 us -> 19.5 us  [shift(): return lax.ppermute(value, axes, pairs)]
    all_gather x7 -> x6, blocking collectives: 32.1 us -> 32.1 us  [of_chip(): return lax.all_gather(value, 'core', axis=0, tiled=False)]
  transfers between devices with their start and end apart: 7 -> 7, of which waited for: 4 -> 4; matrix products, arithmetic and copies ran while one was open for 0% -> 1% of each run, Pallas kernels for 3% -> 3%
where the time goes in v6:
time: 110 us; the launch traced here: 109 us
  blocking collectives  50.2 us (46%)
  starting transfers between devices  36.3 us (33%)
  waiting for transfers between devices  11.5 us (10%)
  Pallas kernels  7.4 us (7%)
  local copies, waits for them, and re-layouts  2.45 us (2%)
    all_gather x6, blocking collectives, of_chip(): return lax.all_gather(value, 'core', axis=0, tiled=False)  32.1 us
    ppermute x4, starting transfers between devices, shift(): return lax.ppermute(value, axes, pairs)  19.5 us
    all_to_all x2, blocking collectives, exchange(): return lax.all_to_all(chunks, axes, 0, 0, tiled=True)  18 us
    all_to_all x3, starting transfers between devices, exchange(): return lax.all_to_all(chunks, axes, 0, 0, tiled=True)  16.8 us
    all_to_all x3, waiting for transfers between devices, exchange(): return lax.all_to_all(chunks, axes, 0, 0, tiled=True)  8.11 us
    pallas_call x10, Pallas kernels, local_call(): pl.pallas_call(kernel, out_shape=out_shape, in_specs=in_specs, out_specs=...  7.4 us
    ppermute x4, waiting for transfers between devices, shift(): return lax.ppermute(value, axes, pairs)  3.35 us
    unnamed x8, local copies, waits for them, and re-layouts  2.45 us
  transfers between devices with their start and end apart: 7, of which 4 were waited for; matrix products, arithmetic and copies ran while one was open for 1% of the time, Pallas kernels for 3%

profile of v6, /device:TPU:1, one launch (start us, length us, event | category | flops | bytes accessed | tf_op | source)
XLA Modules:
  0.0 109.4 jit_solution(11175645102563515498)
XLA Ops:
  0.6 15.9 %all-gather = bf16[128,512]{1,0:T(8,128)(2,1)S(1)} all-gather(bf16[64,512]{1,0:T(8,128)(2,1)} %bitcast.30), channel_id=2, replica_groups=mesh['far'=8,'near'=2,'y'=8,'x'=4,'core'=2] {'core'}, dimensions={0}, use_global_device_ids=true | all-gather | bytes 196608 | tf_op jit(solution)/shard_map/all_gather | solution.py:223
  16.5 1.9 %collective-permute-start = (bf16[128,512]{1,0:T(8,128)(2,1)S(1)}, bf16[128,512]{1,0:T(8,128)(2,1)S(1)}, u32[]{:S(2)}, u32[]{:S(2)}) collective-permute-start(bf16[128,512]{1,0:T(8,128)(2,1)S(1)} %all-gather), channel_id=1, source_target_pairs={{0,8},{1,17},{8,16},{9,25},{16,24},{17,33},{24,32},{25,41},{32,40}... | collective-permute-start | bytes 393224 | tf_op jit(solution)/shard_map/ppermute | solution.py:219
  18.5 9.0 %collective-permute-start.1 = (bf16[128,512]{1,0:T(8,128)(2,1)S(1)}, bf16[128,512]{1,0:T(8,128)(2,1)S(1)}, u32[]{:S(2)}, u32[]{:S(2)}) collective-permute-start(bf16[128,512]{1,0:T(8,128)(2,1)S(1)} %all-gather), channel_id=1, source_target_pairs={{0,1016},{1,1009},{8,0},{9,1017},{16,8},{17,1},{24,16},{25,9},{32,... | collective-permute-start | bytes 393224 | tf_op jit(solution)/shard_map/ppermute | solution.py:219
  27.5 0.9 pad_maximum_fusion
  28.3 2.0 %all-gather.1 = bf16[256,512]{1,0:T(8,128)(2,1)S(1)} all-gather(bf16[128,512]{1,0:T(8,128)(2,1)S(1)} %pad_maximum_fusion), channel_id=3, replica_groups=mesh['far'=8,'near'=2,'y'=8,'x'=4,'core'=2] {'core'}, dimensions={0}, use_global_device_ids=true | all-gather | bytes 393216 | tf_op jit(solution)/shard_map/all_gather | solution.py:223
  30.3 1.7 %copy-done = bf16[512,5,512]{2,0,1:T(8,128)(2,1)S(1)} copy-done((bf16[512,5,512]{2,0,1:T(8,128)(2,1)S(1)}, bf16[512,5,512]{2,0,1:T(8,128)(2,1)}, u32[]{:S(2)}) %copy-start) | copy-done | bytes 2621464
  32.1 0.7 copy-done.3
  32.8 1.5 %shard_map.93 = (bf16[5,512,512]{2,1,0:T(8,128)(2,1)S(1)}, f32[128,512]{1,0:T(8,128)S(1)}, f32[8,512]{1,0:T(8,128)S(1)}) custom-call(s32[4,4,5]{2,1,0:T(4,128)S(1)} %bitcast.29, bf16[2,64,512]{2,1,0:T(8,128)(2,1)S(1)} %bitcast.21, bf16[5,512,512]{2,1,0:T(8,128)(2,1)S(1)} %bitcast.18, bf16[2,128,512]{2,1,0:T(8,128)(2,1)S(1)} %bitcast.15), custom_call_target="tpu_custom_call" | custom-call | flops 2621440 | bytes 5914944 | tf_op jit(solution)/shard_map/pallas_call | solution.py:28
  34.4 0.5 shard_map.94
  34.8 2.3 %all-gather.2 = f32[256,512]{1,0:T(8,128)S(1)} all-gather(f32[128,512]{1,0:T(8,128)S(1)} %shard_map.94), channel_id=4, replica_groups=mesh['far'=8,'near'=2,'y'=8,'x'=4,'core'=2] {'core'}, dimensions={0}, use_global_device_ids=true | all-gather | bytes 786432 | tf_op jit(solution)/shard_map/all_gather | solution.py:223
  37.2 0.4 shard_map.95
  37.5 10.1 %all_to_all.25.parts_ref = bf16[4,64,512]{2,1,0:T(8,128)(2,1)S(1)} all-to-all(bf16[4,64,512]{2,1,0:T(8,128)(2,1)S(1)} %get-tuple-element.19), channel_id=1, replica_groups=mesh['far'=8,'near'=2,'y'=8,'x'=4,'core'=2] {'x'}, dimensions={0} | all-to-all | bytes 524288 | tf_op jit(solution)/shard_map/all_to_all | solution.py:227
  47.7 0.7 shard_map.96
  48.4 7.9 %all_to_all.26.refs_0_ = bf16[4,64,512]{2,1,0:T(8,128)(2,1)S(1)} all-to-all(bf16[4,64,512]{2,1,0:T(8,128)(2,1)S(1)} %get-tuple-element.21), channel_id=1, replica_groups=mesh['far'=8,'near'=2,'y'=8,'x'=4,'core'=2] {'x'}, dimensions={0} | all-to-all | bytes 524288 | tf_op jit(solution)/shard_map/all_to_all | solution.py:227
  56.3 0.9 shard_map.99
  57.2 3.5 %all-to-all-start.2 = ((bf16[16,16,256]{2,1,0:T(8,128)(2,1)}), bf16[16,16,256]{2,1,0:T(8,128)(2,1)S(1)}, u32[]{:S(2)}, u32[]{:S(2)}) async-start(bf16[16,16,256]{2,1,0:T(8,128)(2,1)} %shard_map.99), calls=%async_computation.2 | async-start | bytes 262144 | tf_op jit(solution)/shard_map/all_to_all | solution.py:227
  60.7 4.3 %all-gather.3 = bf16[8,64,512]{2,1,0:T(8,128)(2,1)S(1)} all-gather(bf16[4,64,512]{2,1,0:T(8,128)(2,1)S(1)} %all_to_all.26.refs_0_), channel_id=5, replica_groups=mesh['far'=8,'near'=2,'y'=8,'x'=4,'core'=2] {'core'}, dimensions={0}, use_global_device_ids=true | all-gather | bytes 786432 | tf_op jit(solution)/shard_map/all_gather | solution.py:223
  65.0 0.6 shard_map.97
  65.6 2.5 %all-to-all-done.2.in_ref = bf16[16,16,256]{2,1,0:T(8,128)(2,1)S(1)} async-done(((bf16[16,16,256]{2,1,0:T(8,128)(2,1)}), bf16[16,16,256]{2,1,0:T(8,128)(2,1)S(1)}, u32[]{:S(2)}, u32[]{:S(2)}) %all-to-all-start.2) | async-done | bytes 131104 | tf_op jit(solution)/shard_map/all_to_all | solution.py:227
  68.1 0.7 shard_map.100
  68.8 6.7 %all-to-all-start.3 = ((bf16[8,16,256]{2,1,0:T(8,128)(2,1)}), bf16[8,16,256]{2,1,0:T(8,128)(2,1)S(1)}, u32[]{:S(2)}, u32[]{:S(2)}) async-start(bf16[8,16,256]{2,1,0:T(8,128)(2,1)} %shard_map.100), calls=%async_computation.3 | async-start | bytes 131072 | tf_op jit(solution)/shard_map/all_to_all | solution.py:227
  75.5 6.7 %collective-permute-start.2 = (bf16[128,512]{1,0:T(8,128)(2,1)S(1)}, bf16[128,512]{1,0:T(8,128)(2,1)S(1)}, u32[]{:S(2)}, u32[]{:S(2)}) collective-permute-start(bf16[128,512]{1,0:T(8,128)(2,1)S(1)} %get-tuple-element.23), channel_id=1, source_target_pairs={{0,1016},{1,1009},{8,0},{9,1017},{16,8},{17,1},{24,16},{25,9},{32,... | collective-permute-start | bytes 393224 | tf_op jit(solution)/shard_map/ppermute | solution.py:219
  82.1 1.9 %collective-permute-start.3 = (bf16[128,512]{1,0:T(8,128)(2,1)S(1)}, bf16[128,512]{1,0:T(8,128)(2,1)S(1)}, u32[]{:S(2)}, u32[]{:S(2)}) collective-permute-start(bf16[128,512]{1,0:T(8,128)(2,1)S(1)} %get-tuple-element.24), channel_id=1, source_target_pairs={{0,8},{1,17},{8,16},{9,25},{16,24},{17,33},{24,32},{25,41},{32,40}... | collective-permute-start | bytes 393224 | tf_op jit(solution)/shard_map/ppermute | solution.py:219
  84.1 0.5 collective-permute-done.2
  84.6 5.7 %all-gather.4 = bf16[256,512]{1,0:T(8,128)(2,1)S(1)} all-gather(bf16[128,512]{1,0:T(8,128)(2,1)S(1)} %collective-permute-done.2), channel_id=6, replica_groups=mesh['far'=8,'near'=2,'y'=8,'x'=4,'core'=2] {'core'}, dimensions={0}, use_global_device_ids=true | all-gather | bytes 393216 | tf_op jit(solution)/shard_map/all_gather | solution.py:223
  90.2 2.8 %collective-permute-done.3.refs_1_ = bf16[128,512]{1,0:T(8,128)(2,1)S(1)} collective-permute-done((bf16[128,512]{1,0:T(8,128)(2,1)S(1)}, bf16[128,512]{1,0:T(8,128)(2,1)S(1)}, u32[]{:S(2)}, u32[]{:S(2)}) %collective-permute-start.3) | collective-permute-done | bytes 131104 | tf_op jit(solution)/shard_map/ppermute | solution.py:219
  93.1 0.7 shard_map.101
  93.7 6.6 %all-to-all-start.4 = ((bf16[32,16,128]{2,1,0:T(8,128)(2,1)}), bf16[32,16,128]{2,1,0:T(8,128)(2,1)S(1)}, u32[]{:S(2)}, u32[]{:S(2)}) async-start(bf16[32,16,128]{2,1,0:T(8,128)(2,1)} %bitcast.13), calls=%async_computation.4 | async-start | bytes 262144 | tf_op jit(solution)/shard_map/all_to_all | solution.py:227
  100.3 2.0 %all-gather.5 = bf16[256,512]{1,0:T(8,128)(2,1)S(1)} all-gather(bf16[128,512]{1,0:T(8,128)(2,1)S(1)} %collective-permute-done.3.refs_1_), channel_id=7, replica_groups=mesh['far'=8,'near'=2,'y'=8,'x'=4,'core'=2] {'core'}, dimensions={0}, use_global_device_ids=true | all-gather | bytes 393216 | tf_op jit(solution)/shard_map/all_gather | solution.py:223
  102.3 0.7 shard_map.98
  103.0 5.6 %all-to-all-done.4 = bf16[32,16,128]{2,1,0:T(8,128)(2,1)S(1)} async-done(((bf16[32,16,128]{2,1,0:T(8,128)(2,1)}), bf16[32,16,128]{2,1,0:T(8,128)(2,1)S(1)}, u32[]{:S(2)}, u32[]{:S(2)}) %all-to-all-start.4) | async-done | bytes 131104 | tf_op jit(solution)/shard_map/all_to_all | solution.py:227
  108.6 0.8 shard_map.102
  (9 shorter events, 0.0 us)
Async XLA Ops:
  16.5 17.8 %collective-permute-start = (bf16[128,512]{1,0:T(8,128)(2,1)S(1)}, bf16[128,512]{1,0:T(8,128)(2,1)S(1)}, u32[]{:S(2)}, u32[]{:S(2)}) collective-permute-start(bf16[128,512]{1,0:T(8,128)(2,1)S(1)} %all-gather), channel_id=1, source_target_pairs={{0,8},{1,17},{8,16},{9,25},{16,24},{17,33},{24,32},{25,41},{32,40}... | collective-permute-start | bytes 393224 | tf_op jit(solution)/shard_map/ppermute | solution.py:219
  18.5 15.9 %collective-permute-start.1 = (bf16[128,512]{1,0:T(8,128)(2,1)S(1)}, bf16[128,512]{1,0:T(8,128)(2,1)S(1)}, u32[]{:S(2)}, u32[]{:S(2)}) collective-permute-start(bf16[128,512]{1,0:T(8,128)(2,1)S(1)} %all-gather), channel_id=1, source_target_pairs={{0,1016},{1,1009},{8,0},{9,1017},{16,8},{17,1},{24,16},{25,9},{32,... | collective-permute-start | bytes 393224 | tf_op jit(solution)/shard_map/ppermute | solution.py:219
  30.3 1.7 %copy-start = (bf16[512,5,512]{2,0,1:T(8,128)(2,1)S(1)}, bf16[512,5,512]{2,0,1:T(8,128)(2,1)}, u32[]{:S(2)}) copy-start(bf16[512,5,512]{2,0,1:T(8,128)(2,1)} %param.7) | copy-start | bytes 7864324
  32.1 0.7 copy-start.3
  34.3 13.3 %copy-start.2 = (bf16[512,64]{0,1:T(8,128)(2,1)S(1)}, bf16[512,64]{0,1:T(8,128)(2,1)}, u32[]{:S(2)}) copy-start(bf16[512,64]{0,1:T(8,128)(2,1)} %param.11) | copy-start | bytes 196612
  34.8 30.2 %copy-start.1 = (bf16[64,512]{1,0:T(8,128)(2,1)S(1)}, bf16[64,512]{1,0:T(8,128)(2,1)}, u32[]{:S(2)}) copy-start(bf16[64,512]{1,0:T(8,128)(2,1)} %wself_ref.1) | copy-start | bytes 196612
  57.2 10.9 %all-to-all-start.2 = ((bf16[16,16,256]{2,1,0:T(8,128)(2,1)}), bf16[16,16,256]{2,1,0:T(8,128)(2,1)S(1)}, u32[]{:S(2)}, u32[]{:S(2)}) async-start(bf16[16,16,256]{2,1,0:T(8,128)(2,1)} %shard_map.99), calls=%async_computation.2 | async-start | bytes 262144 | tf_op jit(solution)/shard_map/all_to_all | solution.py:227
  68.8 24.3 %all-to-all-start.3 = ((bf16[8,16,256]{2,1,0:T(8,128)(2,1)}), bf16[8,16,256]{2,1,0:T(8,128)(2,1)S(1)}, u32[]{:S(2)}, u32[]{:S(2)}) async-start(bf16[8,16,256]{2,1,0:T(8,128)(2,1)} %shard_map.100), calls=%async_computation.3 | async-start | bytes 131072 | tf_op jit(solution)/shard_map/all_to_all | solution.py:227
  75.5 9.1 %collective-permute-start.2 = (bf16[128,512]{1,0:T(8,128)(2,1)S(1)}, bf16[128,512]{1,0:T(8,128)(2,1)S(1)}, u32[]{:S(2)}, u32[]{:S(2)}) collective-permute-start(bf16[128,512]{1,0:T(8,128)(2,1)S(1)} %get-tuple-element.23), channel_id=1, source_target_pairs={{0,1016},{1,1009},{8,0},{9,1017},{16,8},{17,1},{24,16},{25,9},{32,... | collective-permute-start | bytes 393224 | tf_op jit(solution)/shard_map/ppermute | solution.py:219
  82.1 10.9 %collective-permute-start.3 = (bf16[128,512]{1,0:T(8,128)(2,1)S(1)}, bf16[128,512]{1,0:T(8,128)(2,1)S(1)}, u32[]{:S(2)}, u32[]{:S(2)}) collective-permute-start(bf16[128,512]{1,0:T(8,128)(2,1)S(1)} %get-tuple-element.24), channel_id=1, source_target_pairs={{0,8},{1,17},{8,16},{9,25},{16,24},{17,33},{24,32},{25,41},{32,40}... | collective-permute-start | bytes 393224 | tf_op jit(solution)/shard_map/ppermute | solution.py:219
  93.7 14.8 %all-to-all-start.4 = ((bf16[32,16,128]{2,1,0:T(8,128)(2,1)}), bf16[32,16,128]{2,1,0:T(8,128)(2,1)S(1)}, u32[]{:S(2)}, u32[]{:S(2)}) async-start(bf16[32,16,128]{2,1,0:T(8,128)(2,1)} %bitcast.13), calls=%async_computation.4 | async-start | bytes 262144 | tf_op jit(solution)/shard_map/all_to_all | solution.py:227

commit v7 on v6

--- a/solution.py
+++ b/solution.py
@@ -196,14 +196,16 @@
     stays_ref[...] = dot(wself_ref[...], grads, PLAIN) + own
 
 
-def out_kernel(core_ref, stays_ref, *refs):
-    *term_refs, out_ref = refs
+def add_kernel(first_ref, second_ref, out_ref):
+    out_ref[...] = first_ref[...].astype(F32) + second_ref[...].astype(F32)
+
+
+def out_kernel(core_ref, stays_ref, terms_ref, out_ref):
     width = out_ref.shape[0]
     total = stays_ref[...]
     rows = pl.ds(pl.multiple_of(core_ref[0] * width, width), width)
-    for term_ref in term_refs:
-        for part in range(term_ref.shape[0]):
-            total = total + term_ref[part, rows, :].astype(F32)
+    for part in range(terms_ref.shape[0]):
+        total = total + terms_ref[part, rows, :]
     out_ref[...] = total.astype(BF16)
 
 
@@ -311,13 +313,12 @@
         adj.size,
     )
     over_far = exchange(folded, "far")
-    first, second = of_chip(arrived[0]), arrived[1]
     share = (lines, cores, height * chips * width // TILE, TILE)
     summed = local_call(
         share_kernel,
         shape(share, BF16),
         [VMEM, ANY, ANY],
-        (over_far, first, second),
+        (over_far, *arrived),
         adj.size,
     )
     gathered = exchange(summed.reshape(lines * cores, *share[2:]), BLOCK + ("core",))
@@ -332,11 +333,12 @@
         (gathered.reshape(share),),
         adj.size,
     )
+    returned = local_call(add_kernel, shape(wide, F32), [VMEM] * 2, arrived, nodes * depth)
     grad_features = local_call(
         out_kernel,
         shape(panel, BF16),
-        [SMEM] + [VMEM] * (1 + len(arrived)),
-        (core, stays, first, of_chip(second)),
+        [SMEM, VMEM, VMEM],
+        (core, stays, of_chip(returned)),
         adj.size,
     )
     return (activated.T, grad_features.T, grad_self, grad_neigh)

time: 110 us -> 110 us (level)
  blocking collectives: 50.2 us -> 44.7 us
  waiting for transfers between devices: 11.5 us -> 16.9 us
    ppermute x4, waiting for transfers between devices: 3.35 us -> 9.02 us  [shift(): return lax.ppermute(value, axes, pairs)]
    all_gather x6 -> x5, blocking collectives: 32.1 us -> 26.7 us  [of_chip(): return lax.all_gather(value, 'core', axis=0, tiled=False)]
    pallas_call x10 -> x11, Pallas kernels: 7.4 us -> 7.41 us  [local_call(): pl.pallas_call(kernel, out_shape=out_shape, in_specs=in_specs, out_specs=...]
where the time goes in v7:
time: 110 us; the launch traced here: 109 us
  blocking collectives  44.7 us (41%)
  starting transfers between devices  36.3 us (33%)
  waiting for transfers between devices  16.9 us (15%)
  Pallas kernels  7.41 us (7%)
  local copies, waits for them, and re-layouts  2.45 us (2%)
    all_gather x5, blocking collectives, of_chip(): return lax.all_gather(value, 'core', axis=0, tiled=False)  26.7 us
    ppermute x4, starting transfers between devices, shift(): return lax.ppermute(value, axes, pairs)  19.5 us
    all_to_all x2, blocking collectives, exchange(): return lax.all_to_all(chunks, axes, 0, 0, tiled=True)  18 us
    all_to_all x3, starting transfers between devices, exchange(): return lax.all_to_all(chunks, axes, 0, 0, tiled=True)  16.8 us
    ppermute x4, waiting for transfers between devices, shift(): return lax.ppermute(value, axes, pairs)  9.02 us
    all_to_all x3, waiting for transfers between devices, exchange(): return lax.all_to_all(chunks, axes, 0, 0, tiled=True)  7.9 us
    pallas_call x11, Pallas kernels, local_call(): pl.pallas_call(kernel, out_shape=out_shape, in_specs=in_specs, out_specs=...  7.41 us
    unnamed x8, local copies, waits for them, and re-layouts  2.45 us
  transfers between devices with their start and end apart: 7, of which 4 were waited for; matrix products, arithmetic and copies ran while one was open for 1% of the time, Pallas kernels for 3%

profile of v7, /device:TPU:1, one launch (start us, length us, event | category | flops | bytes accessed | tf_op | source)
XLA Modules:
  0.0 109.4 jit_solution(7101867930914928973)
XLA Ops:
  0.6 15.9 %all-gather = bf16[128,512]{1,0:T(8,128)(2,1)S(1)} all-gather(bf16[64,512]{1,0:T(8,128)(2,1)} %bitcast.27), channel_id=2, replica_groups=mesh['far'=8,'near'=2,'y'=8,'x'=4,'core'=2] {'core'}, dimensions={0}, use_global_device_ids=true | all-gather | bytes 196608 | tf_op jit(solution)/shard_map/all_gather | solution.py:225
  16.5 1.9 %collective-permute-start = (bf16[128,512]{1,0:T(8,128)(2,1)S(1)}, bf16[128,512]{1,0:T(8,128)(2,1)S(1)}, u32[]{:S(2)}, u32[]{:S(2)}) collective-permute-start(bf16[128,512]{1,0:T(8,128)(2,1)S(1)} %all-gather), channel_id=1, source_target_pairs={{0,8},{1,17},{8,16},{9,25},{16,24},{17,33},{24,32},{25,41},{32,40}... | collective-permute-start | bytes 393224 | tf_op jit(solution)/shard_map/ppermute | solution.py:221
  18.5 9.0 %collective-permute-start.1 = (bf16[128,512]{1,0:T(8,128)(2,1)S(1)}, bf16[128,512]{1,0:T(8,128)(2,1)S(1)}, u32[]{:S(2)}, u32[]{:S(2)}) collective-permute-start(bf16[128,512]{1,0:T(8,128)(2,1)S(1)} %all-gather), channel_id=1, source_target_pairs={{0,1016},{1,1009},{8,0},{9,1017},{16,8},{17,1},{24,16},{25,9},{32,... | collective-permute-start | bytes 393224 | tf_op jit(solution)/shard_map/ppermute | solution.py:221
  27.5 0.9 pad_maximum_fusion
  28.3 2.0 %all-gather.1 = bf16[256,512]{1,0:T(8,128)(2,1)S(1)} all-gather(bf16[128,512]{1,0:T(8,128)(2,1)S(1)} %pad_maximum_fusion), channel_id=3, replica_groups=mesh['far'=8,'near'=2,'y'=8,'x'=4,'core'=2] {'core'}, dimensions={0}, use_global_device_ids=true | all-gather | bytes 393216 | tf_op jit(solution)/shard_map/all_gather | solution.py:225
  30.3 1.7 %copy-done = bf16[512,5,512]{2,0,1:T(8,128)(2,1)S(1)} copy-done((bf16[512,5,512]{2,0,1:T(8,128)(2,1)S(1)}, bf16[512,5,512]{2,0,1:T(8,128)(2,1)}, u32[]{:S(2)}) %copy-start) | copy-done | bytes 2621464
  32.1 0.7 copy-done.3
  32.8 1.5 %shard_map.93 = (bf16[5,512,512]{2,1,0:T(8,128)(2,1)S(1)}, f32[128,512]{1,0:T(8,128)S(1)}, f32[8,512]{1,0:T(8,128)S(1)}) custom-call(s32[4,4,5]{2,1,0:T(4,128)S(1)} %bitcast.26, bf16[2,64,512]{2,1,0:T(8,128)(2,1)S(1)} %bitcast.18, bf16[5,512,512]{2,1,0:T(8,128)(2,1)S(1)} %bitcast.17, bf16[2,128,512]{2,1,0:T(8,128)(2,1)S(1)} %bitcast.14), custom_call_target="tpu_custom_call" | custom-call | flops 2621440 | bytes 5914944 | tf_op jit(solution)/shard_map/pallas_call | solution.py:28
  34.3 0.0 collective-permute-done.behind_ref
  34.4 0.5 shard_map.94
  34.8 2.3 %all-gather.2 = f32[256,512]{1,0:T(8,128)S(1)} all-gather(f32[128,512]{1,0:T(8,128)S(1)} %shard_map.94), channel_id=4, replica_groups=mesh['far'=8,'near'=2,'y'=8,'x'=4,'core'=2] {'core'}, dimensions={0}, use_global_device_ids=true | all-gather | bytes 786432 | tf_op jit(solution)/shard_map/all_gather | solution.py:225
  37.2 0.4 shard_map.95
  37.5 10.1 %all_to_all.25.parts_ref = bf16[4,64,512]{2,1,0:T(8,128)(2,1)S(1)} all-to-all(bf16[4,64,512]{2,1,0:T(8,128)(2,1)S(1)} %get-tuple-element.19), channel_id=1, replica_groups=mesh['far'=8,'near'=2,'y'=8,'x'=4,'core'=2] {'x'}, dimensions={0} | all-to-all | bytes 524288 | tf_op jit(solution)/shard_map/all_to_all | solution.py:229
  47.7 0.7 shard_map.96
  48.4 7.9 %all_to_all.26.refs_0_ = bf16[4,64,512]{2,1,0:T(8,128)(2,1)S(1)} all-to-all(bf16[4,64,512]{2,1,0:T(8,128)(2,1)S(1)} %get-tuple-element.21), channel_id=1, replica_groups=mesh['far'=8,'near'=2,'y'=8,'x'=4,'core'=2] {'x'}, dimensions={0} | all-to-all | bytes 524288 | tf_op jit(solution)/shard_map/all_to_all | solution.py:229
  56.3 0.9 shard_map.100
  57.2 3.5 %all-to-all-start.2 = ((bf16[16,16,256]{2,1,0:T(8,128)(2,1)}), bf16[16,16,256]{2,1,0:T(8,128)(2,1)S(1)}, u32[]{:S(2)}, u32[]{:S(2)}) async-start(bf16[16,16,256]{2,1,0:T(8,128)(2,1)} %shard_map.100), calls=%async_computation.2 | async-start | bytes 262144 | tf_op jit(solution)/shard_map/all_to_all | solution.py:229
  60.7 4.3 %all-gather.3 = bf16[8,64,512]{2,1,0:T(8,128)(2,1)S(1)} all-gather(bf16[4,64,512]{2,1,0:T(8,128)(2,1)S(1)} %all_to_all.26.refs_0_), channel_id=5, replica_groups=mesh['far'=8,'near'=2,'y'=8,'x'=4,'core'=2] {'core'}, dimensions={0}, use_global_device_ids=true | all-gather | bytes 786432 | tf_op jit(solution)/shard_map/all_gather | solution.py:225
  65.0 0.6 shard_map.97
  65.6 2.5 %all-to-all-done.2.in_ref = bf16[16,16,256]{2,1,0:T(8,128)(2,1)S(1)} async-done(((bf16[16,16,256]{2,1,0:T(8,128)(2,1)}), bf16[16,16,256]{2,1,0:T(8,128)(2,1)S(1)}, u32[]{:S(2)}, u32[]{:S(2)}) %all-to-all-start.2) | async-done | bytes 131104 | tf_op jit(solution)/shard_map/all_to_all | solution.py:229
  68.1 0.7 shard_map.101
  68.8 6.7 %all-to-all-start.3 = ((bf16[8,16,256]{2,1,0:T(8,128)(2,1)}), bf16[8,16,256]{2,1,0:T(8,128)(2,1)S(1)}, u32[]{:S(2)}, u32[]{:S(2)}) async-start(bf16[8,16,256]{2,1,0:T(8,128)(2,1)} %shard_map.101), calls=%async_computation.3 | async-start | bytes 131072 | tf_op jit(solution)/shard_map/all_to_all | solution.py:229
  75.5 6.7 %collective-permute-start.2 = (bf16[128,512]{1,0:T(8,128)(2,1)S(1)}, bf16[128,512]{1,0:T(8,128)(2,1)S(1)}, u32[]{:S(2)}, u32[]{:S(2)}) collective-permute-start(bf16[128,512]{1,0:T(8,128)(2,1)S(1)} %get-tuple-element.23), channel_id=1, source_target_pairs={{0,1016},{1,1009},{8,0},{9,1017},{16,8},{17,1},{24,16},{25,9},{32,... | collective-permute-start | bytes 393224 | tf_op jit(solution)/shard_map/ppermute | solution.py:221
  82.1 1.9 %collective-permute-start.3 = (bf16[128,512]{1,0:T(8,128)(2,1)S(1)}, bf16[128,512]{1,0:T(8,128)(2,1)S(1)}, u32[]{:S(2)}, u32[]{:S(2)}) collective-permute-start(bf16[128,512]{1,0:T(8,128)(2,1)S(1)} %get-tuple-element.24), channel_id=1, source_target_pairs={{0,8},{1,17},{8,16},{9,25},{16,24},{17,33},{24,32},{25,41},{32,40}... | collective-permute-start | bytes 393224 | tf_op jit(solution)/shard_map/ppermute | solution.py:221
  84.1 0.5 collective-permute-done.2.first_ref.refs_0_
  84.6 8.5 %collective-permute-done.3.second_ref.refs_1_ = bf16[128,512]{1,0:T(8,128)(2,1)S(1)} collective-permute-done((bf16[128,512]{1,0:T(8,128)(2,1)S(1)}, bf16[128,512]{1,0:T(8,128)(2,1)S(1)}, u32[]{:S(2)}, u32[]{:S(2)}) %collective-permute-start.3) | collective-permute-done | bytes 131104 | tf_op jit(solution)/shard_map/ppermute | solution.py:221
  93.1 0.7 shard_map.102
  93.7 6.6 %all-to-all-start.4 = ((bf16[32,16,128]{2,1,0:T(8,128)(2,1)}), bf16[32,16,128]{2,1,0:T(8,128)(2,1)S(1)}, u32[]{:S(2)}, u32[]{:S(2)}) async-start(bf16[32,16,128]{2,1,0:T(8,128)(2,1)} %bitcast.12), calls=%async_computation.4 | async-start | bytes 262144 | tf_op jit(solution)/shard_map/all_to_all | solution.py:229
  100.3 2.2 %all-gather.4 = f32[256,512]{1,0:T(8,128)S(1)} all-gather(f32[128,512]{1,0:T(8,128)S(1)} %shard_map.98), channel_id=6, replica_groups=mesh['far'=8,'near'=2,'y'=8,'x'=4,'core'=2] {'core'}, dimensions={0}, use_global_device_ids=true | all-gather | bytes 786432 | tf_op jit(solution)/shard_map/all_gather | solution.py:225
  102.5 0.7 shard_map.99
  103.2 5.4 %all-to-all-done.4 = bf16[32,16,128]{2,1,0:T(8,128)(2,1)S(1)} async-done(((bf16[32,16,128]{2,1,0:T(8,128)(2,1)}), bf16[32,16,128]{2,1,0:T(8,128)(2,1)S(1)}, u32[]{:S(2)}, u32[]{:S(2)}) %all-to-all-start.4) | async-done | bytes 131104 | tf_op jit(solution)/shard_map/all_to_all | solution.py:229
  108.6 0.8 shard_map.103
  (9 shorter events, 0.1 us)
Async XLA Ops:
  16.5 17.8 %collective-permute-start = (bf16[128,512]{1,0:T(8,128)(2,1)S(1)}, bf16[128,512]{1,0:T(8,128)(2,1)S(1)}, u32[]{:S(2)}, u32[]{:S(2)}) collective-permute-start(bf16[128,512]{1,0:T(8,128)(2,1)S(1)} %all-gather), channel_id=1, source_target_pairs={{0,8},{1,17},{8,16},{9,25},{16,24},{17,33},{24,32},{25,41},{32,40}... | collective-permute-start | bytes 393224 | tf_op jit(solution)/shard_map/ppermute | solution.py:221
  18.5 15.9 %collective-permute-start.1 = (bf16[128,512]{1,0:T(8,128)(2,1)S(1)}, bf16[128,512]{1,0:T(8,128)(2,1)S(1)}, u32[]{:S(2)}, u32[]{:S(2)}) collective-permute-start(bf16[128,512]{1,0:T(8,128)(2,1)S(1)} %all-gather), channel_id=1, source_target_pairs={{0,1016},{1,1009},{8,0},{9,1017},{16,8},{17,1},{24,16},{25,9},{32,... | collective-permute-start | bytes 393224 | tf_op jit(solution)/shard_map/ppermute | solution.py:221
  30.3 1.7 %copy-start = (bf16[512,5,512]{2,0,1:T(8,128)(2,1)S(1)}, bf16[512,5,512]{2,0,1:T(8,128)(2,1)}, u32[]{:S(2)}) copy-start(bf16[512,5,512]{2,0,1:T(8,128)(2,1)} %param.7) | copy-start | bytes 7864324
  32.1 0.7 copy-start.3
  34.3 13.3 %copy-start.2 = (bf16[512,64]{0,1:T(8,128)(2,1)S(1)}, bf16[512,64]{0,1:T(8,128)(2,1)}, u32[]{:S(2)}) copy-start(bf16[512,64]{0,1:T(8,128)(2,1)} %param.11) | copy-start | bytes 196612
  34.8 30.2 %copy-start.1 = (bf16[64,512]{1,0:T(8,128)(2,1)S(1)}, bf16[64,512]{1,0:T(8,128)(2,1)}, u32[]{:S(2)}) copy-start(bf16[64,512]{1,0:T(8,128)(2,1)} %wself_ref.1) | copy-start | bytes 196612
  57.2 10.9 %all-to-all-start.2 = ((bf16[16,16,256]{2,1,0:T(8,128)(2,1)}), bf16[16,16,256]{2,1,0:T(8,128)(2,1)S(1)}, u32[]{:S(2)}, u32[]{:S(2)}) async-start(bf16[16,16,256]{2,1,0:T(8,128)(2,1)} %shard_map.100), calls=%async_computation.2 | async-start | bytes 262144 | tf_op jit(solution)/shard_map/all_to_all | solution.py:229
  68.8 24.3 %all-to-all-start.3 = ((bf16[8,16,256]{2,1,0:T(8,128)(2,1)}), bf16[8,16,256]{2,1,0:T(8,128)(2,1)S(1)}, u32[]{:S(2)}, u32[]{:S(2)}) async-start(bf16[8,16,256]{2,1,0:T(8,128)(2,1)} %shard_map.101), calls=%async_computation.3 | async-start | bytes 131072 | tf_op jit(solution)/shard_map/all_to_all | solution.py:229
  75.5 9.1 %collective-permute-start.2 = (bf16[128,512]{1,0:T(8,128)(2,1)S(1)}, bf16[128,512]{1,0:T(8,128)(2,1)S(1)}, u32[]{:S(2)}, u32[]{:S(2)}) collective-permute-start(bf16[128,512]{1,0:T(8,128)(2,1)S(1)} %get-tuple-element.23), channel_id=1, source_target_pairs={{0,1016},{1,1009},{8,0},{9,1017},{16,8},{17,1},{24,16},{25,9},{32,... | collective-permute-start | bytes 393224 | tf_op jit(solution)/shard_map/ppermute | solution.py:221
  82.1 10.9 %collective-permute-start.3 = (bf16[128,512]{1,0:T(8,128)(2,1)S(1)}, bf16[128,512]{1,0:T(8,128)(2,1)S(1)}, u32[]{:S(2)}, u32[]{:S(2)}) collective-permute-start(bf16[128,512]{1,0:T(8,128)(2,1)S(1)} %get-tuple-element.24), channel_id=1, source_target_pairs={{0,8},{1,17},{8,16},{9,25},{16,24},{17,33},{24,32},{25,41},{32,40}... | collective-permute-start | bytes 393224 | tf_op jit(solution)/shard_map/ppermute | solution.py:221
  93.7 14.8 %all-to-all-start.4 = ((bf16[32,16,128]{2,1,0:T(8,128)(2,1)}), bf16[32,16,128]{2,1,0:T(8,128)(2,1)S(1)}, u32[]{:S(2)}, u32[]{:S(2)}) async-start(bf16[32,16,128]{2,1,0:T(8,128)(2,1)} %bitcast.12), calls=%async_computation.4 | async-start | bytes 262144 | tf_op jit(solution)/shard_map/all_to_all | solution.py:229

commit v8 on v7

--- a/solution.py
+++ b/solution.py
@@ -63,6 +63,12 @@
     inverse_ref[...] = 1.0 / jnp.maximum(degree[:8], 1.0)
 
 
+def stack_kernel(first_ref, second_ref, out_ref):
+    half = first_ref.shape[0]
+    out_ref[:half] = first_ref[...]
+    out_ref[half:] = second_ref[...]
+
+
 def near_kernel(core_ref, behind_ref, ahead_ref, weighted_ref, out_ref):
     reach = (weighted_ref.shape[0] - 1) // 2
     steps = core_ref[0] + 1
@@ -246,7 +252,10 @@
     pair = of_chip(own)
     behind = shift(pair.reshape(wide), 1)
     ahead = shift(pair.reshape(wide), -1)
-    weights = of_chip(jnp.concatenate([w_self, w_neigh], axis=0))
+    both = local_call(
+        stack_kernel, shape((2 * width, total), BF16), [VMEM] * 2, (w_self, w_neigh), 500 * adjacency.size
+    )
+    weights = of_chip(both)
     adj = adjacency.transpose(1, 0, 2)
     weighted, base, inverse = local_call(
         mask_kernel,
@@ -317,8 +326,8 @@
     summed = local_call(
         share_kernel,
         shape(share, BF16),
-        [VMEM, ANY, ANY],
-        (over_far, *arrived),
+        [VMEM],
+        (over_far,),
         adj.size,
     )
     gathered = exchange(summed.reshape(lines * cores, *share[2:]), BLOCK + ("core",))
@@ -333,7 +342,7 @@
         (gathered.reshape(share),),
         adj.size,
     )
-    returned = local_call(add_kernel, shape(wide, F32), [VMEM] * 2, arrived, nodes * depth)
+    returned = local_call(add_kernel, shape(wide, F32), [VMEM] * 2, arrived, 4000 * adj.size)
     grad_features = local_call(
         out_kernel,
         shape(panel, BF16),

time: 110 us -> 106 us (0.964)
  waiting for transfers between devices: 16.9 us -> 11.5 us
  starting transfers between devices: 36.3 us -> 39.2 us
    ppermute x4, waiting for transfers between devices: 9.02 us -> 0.02 us  [shift(): return lax.ppermute(value, axes, pairs)]
    all_to_all x3, waiting for transfers between devices: 7.9 us -> 11.5 us  [exchange(): return lax.all_to_all(chunks, axes, 0, 0, tiled=True)]
    all_to_all x3, starting transfers between devices: 16.8 us -> 19.7 us  [exchange(): return lax.all_to_all(chunks, axes, 0, 0, tiled=True)]
    unnamed x8 -> x12, local copies, waits for them, and re-layouts: 2.45 us -> 1.69 us
    pallas_call x11 -> x12, Pallas kernels: 7.41 us -> 7.42 us  [local_call(): pl.pallas_call(kernel, out_shape=out_shape, in_specs=in_specs, out_specs=...]
  transfers between devices with their start and end apart: 7 -> 7, of which waited for: 4 -> 3; matrix products, arithmetic and copies ran while one was open for 1% -> 0% of each run, Pallas kernels for 3% -> 3%
where the time goes in v8:
time: 106 us; the launch traced here: 105 us
  blocking collectives  44.8 us (42%)
  starting transfers between devices  39.2 us (37%)
  waiting for transfers between devices  11.5 us (11%)
  Pallas kernels  7.42 us (7%)
  local copies, waits for them, and re-layouts  1.69 us (2%)
    all_gather x5, blocking collectives, of_chip(): return lax.all_gather(value, 'core', axis=0, tiled=False)  26.8 us
    all_to_all x3, starting transfers between devices, exchange(): return lax.all_to_all(chunks, axes, 0, 0, tiled=True)  19.7 us
    ppermute x4, starting transfers between devices, shift(): return lax.ppermute(value, axes, pairs)  19.5 us
    all_to_all x2, blocking collectives, exchange(): return lax.all_to_all(chunks, axes, 0, 0, tiled=True)  18.1 us
    all_to_all x3, waiting for transfers between devices, exchange(): return lax.all_to_all(chunks, axes, 0, 0, tiled=True)  11.5 us
    pallas_call x12, Pallas kernels, local_call(): pl.pallas_call(kernel, out_shape=out_shape, in_specs=in_specs, out_specs=...  7.42 us
  transfers between devices with their start and end apart: 7, of which 3 were waited for; matrix products, arithmetic and copies ran while one was open for 0% of the time, Pallas kernels for 3%

profile of v8, /device:TPU:1, one launch (start us, length us, event | category | flops | bytes accessed | tf_op | source)
XLA Modules:
  0.0 105.4 jit_solution(3763188752034326381)
XLA Ops:
  0.6 15.9 %all-gather = bf16[128,512]{1,0:T(8,128)(2,1)S(1)} all-gather(bf16[64,512]{1,0:T(8,128)(2,1)} %bitcast.27), channel_id=2, replica_groups=mesh['far'=8,'near'=2,'y'=8,'x'=4,'core'=2] {'core'}, dimensions={0}, use_global_device_ids=true | all-gather | bytes 196608 | tf_op jit(solution)/shard_map/all_gather | solution.py:231
  16.6 1.9 %collective-permute-start = (bf16[128,512]{1,0:T(8,128)(2,1)S(1)}, bf16[128,512]{1,0:T(8,128)(2,1)S(1)}, u32[]{:S(2)}, u32[]{:S(2)}) collective-permute-start(bf16[128,512]{1,0:T(8,128)(2,1)S(1)} %all-gather), channel_id=1, source_target_pairs={{0,8},{1,17},{8,16},{9,25},{16,24},{17,33},{24,32},{25,41},{32,40}... | collective-permute-start | bytes 393224 | tf_op jit(solution)/shard_map/ppermute | solution.py:227
  18.5 9.0 %collective-permute-start.1 = (bf16[128,512]{1,0:T(8,128)(2,1)S(1)}, bf16[128,512]{1,0:T(8,128)(2,1)S(1)}, u32[]{:S(2)}, u32[]{:S(2)}) collective-permute-start(bf16[128,512]{1,0:T(8,128)(2,1)S(1)} %all-gather), channel_id=1, source_target_pairs={{0,1016},{1,1009},{8,0},{9,1017},{16,8},{17,1},{24,16},{25,9},{32,... | collective-permute-start | bytes 393224 | tf_op jit(solution)/shard_map/ppermute | solution.py:227
  27.5 0.0 copy-start.2
  27.5 0.8 copy-done.2
  28.3 0.8 copy-done.5
  29.2 2.1 %all-gather.1 = bf16[256,512]{1,0:T(8,128)(2,1)S(1)} all-gather(bf16[128,512]{1,0:T(8,128)(2,1)S(1)} %shard_map.93), channel_id=3, replica_groups=mesh['far'=8,'near'=2,'y'=8,'x'=4,'core'=2] {'core'}, dimensions={0}, use_global_device_ids=true | all-gather | bytes 393216 | tf_op jit(solution)/shard_map/all_gather | solution.py:231
  31.3 1.5 %shard_map.94 = (bf16[5,512,512]{2,1,0:T(8,128)(2,1)S(1)}, f32[128,512]{1,0:T(8,128)S(1)}, f32[8,512]{1,0:T(8,128)S(1)}) custom-call(s32[4,4,5]{2,1,0:T(4,128)S(1)} %bitcast.26, bf16[2,64,512]{2,1,0:T(8,128)(2,1)S(1)} %bitcast.18, bf16[5,512,512]{2,1,0:T(8,128)(2,1)S(1)} %bitcast.17, bf16[2,128,512]{2,1,0:T(8,128)(2,1)S(1)} %bitcast.14), custom_call_target="tpu_custom_call" | custom-call | flops 2621440 | bytes 5914944 | tf_op jit(solution)/shard_map/pallas_call | solution.py:28
  32.8 0.0 collective-permute-done.behind_ref
  32.9 0.0 copy-start.1
  32.9 0.5 shard_map.95
  33.4 2.3 %all-gather.2 = f32[256,512]{1,0:T(8,128)S(1)} all-gather(f32[128,512]{1,0:T(8,128)S(1)} %shard_map.95), channel_id=4, replica_groups=mesh['far'=8,'near'=2,'y'=8,'x'=4,'core'=2] {'core'}, dimensions={0}, use_global_device_ids=true | all-gather | bytes 786432 | tf_op jit(solution)/shard_map/all_gather | solution.py:231
  35.7 0.4 shard_map.96
  36.0 10.2 %all_to_all.25.parts_ref = bf16[4,64,512]{2,1,0:T(8,128)(2,1)S(1)} all-to-all(bf16[4,64,512]{2,1,0:T(8,128)(2,1)S(1)} %get-tuple-element.19), channel_id=1, replica_groups=mesh['far'=8,'near'=2,'y'=8,'x'=4,'core'=2] {'x'}, dimensions={0} | all-to-all | bytes 524288 | tf_op jit(solution)/shard_map/all_to_all | solution.py:235
  46.2 0.7 shard_map.97
  46.9 7.9 %all_to_all.26.refs_0_ = bf16[4,64,512]{2,1,0:T(8,128)(2,1)S(1)} all-to-all(bf16[4,64,512]{2,1,0:T(8,128)(2,1)S(1)} %get-tuple-element.21), channel_id=1, replica_groups=mesh['far'=8,'near'=2,'y'=8,'x'=4,'core'=2] {'x'}, dimensions={0} | all-to-all | bytes 524288 | tf_op jit(solution)/shard_map/all_to_all | solution.py:235
  54.8 0.9 shard_map.101
  55.7 3.5 %all-to-all-start.2 = ((bf16[16,16,256]{2,1,0:T(8,128)(2,1)}), bf16[16,16,256]{2,1,0:T(8,128)(2,1)S(1)}, u32[]{:S(2)}, u32[]{:S(2)}) async-start(bf16[16,16,256]{2,1,0:T(8,128)(2,1)} %shard_map.101), calls=%async_computation.2 | async-start | bytes 262144 | tf_op jit(solution)/shard_map/all_to_all | solution.py:235
  59.3 4.2 %all-gather.3 = bf16[8,64,512]{2,1,0:T(8,128)(2,1)S(1)} all-gather(bf16[4,64,512]{2,1,0:T(8,128)(2,1)S(1)} %all_to_all.26.refs_0_), channel_id=5, replica_groups=mesh['far'=8,'near'=2,'y'=8,'x'=4,'core'=2] {'core'}, dimensions={0}, use_global_device_ids=true | all-gather | bytes 786432 | tf_op jit(solution)/shard_map/all_gather | solution.py:231
  63.5 0.6 shard_map.98
  64.1 2.5 %all-to-all-done.2.in_ref = bf16[16,16,256]{2,1,0:T(8,128)(2,1)S(1)} async-done(((bf16[16,16,256]{2,1,0:T(8,128)(2,1)}), bf16[16,16,256]{2,1,0:T(8,128)(2,1)S(1)}, u32[]{:S(2)}, u32[]{:S(2)}) %all-to-all-start.2) | async-done | bytes 131104 | tf_op jit(solution)/shard_map/all_to_all | solution.py:235
  66.6 0.7 shard_map.102
  67.3 7.0 %all-to-all-start.3 = ((bf16[8,16,256]{2,1,0:T(8,128)(2,1)}), bf16[8,16,256]{2,1,0:T(8,128)(2,1)S(1)}, u32[]{:S(2)}, u32[]{:S(2)}) async-start(bf16[8,16,256]{2,1,0:T(8,128)(2,1)} %shard_map.102), calls=%async_computation.3 | async-start | bytes 131072 | tf_op jit(solution)/shard_map/all_to_all | solution.py:235
  74.3 6.7 %collective-permute-start.2 = (bf16[128,512]{1,0:T(8,128)(2,1)S(1)}, bf16[128,512]{1,0:T(8,128)(2,1)S(1)}, u32[]{:S(2)}, u32[]{:S(2)}) collective-permute-start(bf16[128,512]{1,0:T(8,128)(2,1)S(1)} %get-tuple-element.23), channel_id=1, source_target_pairs={{0,1016},{1,1009},{8,0},{9,1017},{16,8},{17,1},{24,16},{25,9},{32,... | collective-permute-start | bytes 393224 | tf_op jit(solution)/shard_map/ppermute | solution.py:227
  81.0 1.9 %collective-permute-start.3 = (bf16[128,512]{1,0:T(8,128)(2,1)S(1)}, bf16[128,512]{1,0:T(8,128)(2,1)S(1)}, u32[]{:S(2)}, u32[]{:S(2)}) collective-permute-start(bf16[128,512]{1,0:T(8,128)(2,1)S(1)} %get-tuple-element.24), channel_id=1, source_target_pairs={{0,8},{1,17},{8,16},{9,25},{16,24},{17,33},{24,32},{25,41},{32,40}... | collective-permute-start | bytes 393224 | tf_op jit(solution)/shard_map/ppermute | solution.py:227
  82.9 3.6 %all-to-all-done.3.in_ref = bf16[8,16,256]{2,1,0:T(8,128)(2,1)S(1)} async-done(((bf16[8,16,256]{2,1,0:T(8,128)(2,1)}), bf16[8,16,256]{2,1,0:T(8,128)(2,1)S(1)}, u32[]{:S(2)}, u32[]{:S(2)}) %all-to-all-start.3) | async-done | bytes 65568 | tf_op jit(solution)/shard_map/all_to_all | solution.py:235
  86.5 0.7 shard_map.103
  87.2 9.2 %all-to-all-start.4 = ((bf16[32,16,128]{2,1,0:T(8,128)(2,1)}), bf16[32,16,128]{2,1,0:T(8,128)(2,1)S(1)}, u32[]{:S(2)}, u32[]{:S(2)}) async-start(bf16[32,16,128]{2,1,0:T(8,128)(2,1)} %bitcast.12), calls=%async_computation.4 | async-start | bytes 262144 | tf_op jit(solution)/shard_map/all_to_all | solution.py:235
  96.4 2.2 %all-gather.4 = f32[256,512]{1,0:T(8,128)S(1)} all-gather(f32[128,512]{1,0:T(8,128)S(1)} %shard_map.99), channel_id=6, replica_groups=mesh['far'=8,'near'=2,'y'=8,'x'=4,'core'=2] {'core'}, dimensions={0}, use_global_device_ids=true | all-gather | bytes 786432 | tf_op jit(solution)/shard_map/all_gather | solution.py:231
  98.6 0.7 shard_map.100
  99.3 5.4 %all-to-all-done.4 = bf16[32,16,128]{2,1,0:T(8,128)(2,1)S(1)} async-done(((bf16[32,16,128]{2,1,0:T(8,128)(2,1)}), bf16[32,16,128]{2,1,0:T(8,128)(2,1)S(1)}, u32[]{:S(2)}, u32[]{:S(2)}) %all-to-all-start.4) | async-done | bytes 131104 | tf_op jit(solution)/shard_map/all_to_all | solution.py:235
  104.6 0.8 shard_map.104
  (13 shorter events, 0.1 us)
Async XLA Ops:
  0.6 30.7 %copy-start.4 = (s32[4,5,4]{1,2,0:T(4,128)S(1)}, s32[4,5,4]{1,2,0:T(4,128)}, u32[]{:S(2)}) copy-start(s32[4,5,4]{1,2,0:T(4,128)} %param.8) | copy-start | bytes 964
  16.6 16.3 %collective-permute-start = (bf16[128,512]{1,0:T(8,128)(2,1)S(1)}, bf16[128,512]{1,0:T(8,128)(2,1)S(1)}, u32[]{:S(2)}, u32[]{:S(2)}) collective-permute-start(bf16[128,512]{1,0:T(8,128)(2,1)S(1)} %all-gather), channel_id=1, source_target_pairs={{0,8},{1,17},{8,16},{9,25},{16,24},{17,33},{24,32},{25,41},{32,40}... | collective-permute-start | bytes 393224 | tf_op jit(solution)/shard_map/ppermute | solution.py:227
  18.5 14.4 %collective-permute-start.1 = (bf16[128,512]{1,0:T(8,128)(2,1)S(1)}, bf16[128,512]{1,0:T(8,128)(2,1)S(1)}, u32[]{:S(2)}, u32[]{:S(2)}) collective-permute-start(bf16[128,512]{1,0:T(8,128)(2,1)S(1)} %all-gather), channel_id=1, source_target_pairs={{0,1016},{1,1009},{8,0},{9,1017},{16,8},{17,1},{24,16},{25,9},{32,... | collective-permute-start | bytes 393224 | tf_op jit(solution)/shard_map/ppermute | solution.py:227
  27.5 0.8 copy-start.2
  28.3 0.8 copy-start.5
  29.2 2.1 %copy-start = (bf16[512,5,512]{2,0,1:T(8,128)(2,1)S(1)}, bf16[512,5,512]{2,0,1:T(8,128)(2,1)}, u32[]{:S(2)}) copy-start(bf16[512,5,512]{2,0,1:T(8,128)(2,1)} %param.7) | copy-start | bytes 7864324
  32.9 13.3 %copy-start.1 = (bf16[512,64]{0,1:T(8,128)(2,1)S(1)}, bf16[512,64]{0,1:T(8,128)(2,1)}, u32[]{:S(2)}) copy-start(bf16[512,64]{0,1:T(8,128)(2,1)} %param.11) | copy-start | bytes 196612
  33.4 30.2 %copy-start.3 = (bf16[64,512]{1,0:T(8,128)(2,1)S(1)}, bf16[64,512]{1,0:T(8,128)(2,1)}, u32[]{:S(2)}) copy-start(bf16[64,512]{1,0:T(8,128)(2,1)} %wself_ref.1) | copy-start | bytes 196612
  55.7 10.9 %all-to-all-start.2 = ((bf16[16,16,256]{2,1,0:T(8,128)(2,1)}), bf16[16,16,256]{2,1,0:T(8,128)(2,1)S(1)}, u32[]{:S(2)}, u32[]{:S(2)}) async-start(bf16[16,16,256]{2,1,0:T(8,128)(2,1)} %shard_map.101), calls=%async_computation.2 | async-start | bytes 262144 | tf_op jit(solution)/shard_map/all_to_all | solution.py:235
  67.3 19.2 %all-to-all-start.3 = ((bf16[8,16,256]{2,1,0:T(8,128)(2,1)}), bf16[8,16,256]{2,1,0:T(8,128)(2,1)S(1)}, u32[]{:S(2)}, u32[]{:S(2)}) async-start(bf16[8,16,256]{2,1,0:T(8,128)(2,1)} %shard_map.102), calls=%async_computation.3 | async-start | bytes 131072 | tf_op jit(solution)/shard_map/all_to_all | solution.py:235
  74.3 22.1 %collective-permute-start.2 = (bf16[128,512]{1,0:T(8,128)(2,1)S(1)}, bf16[128,512]{1,0:T(8,128)(2,1)S(1)}, u32[]{:S(2)}, u32[]{:S(2)}) collective-permute-start(bf16[128,512]{1,0:T(8,128)(2,1)S(1)} %get-tuple-element.23), channel_id=1, source_target_pairs={{0,1016},{1,1009},{8,0},{9,1017},{16,8},{17,1},{24,16},{25,9},{32,... | collective-permute-start | bytes 393224 | tf_op jit(solution)/shard_map/ppermute | solution.py:227
  81.0 15.4 %collective-permute-start.3 = (bf16[128,512]{1,0:T(8,128)(2,1)S(1)}, bf16[128,512]{1,0:T(8,128)(2,1)S(1)}, u32[]{:S(2)}, u32[]{:S(2)}) collective-permute-start(bf16[128,512]{1,0:T(8,128)(2,1)S(1)} %get-tuple-element.24), channel_id=1, source_target_pairs={{0,8},{1,17},{8,16},{9,25},{16,24},{17,33},{24,32},{25,41},{32,40}... | collective-permute-start | bytes 393224 | tf_op jit(solution)/shard_map/ppermute | solution.py:227
  87.2 17.5 %all-to-all-start.4 = ((bf16[32,16,128]{2,1,0:T(8,128)(2,1)}), bf16[32,16,128]{2,1,0:T(8,128)(2,1)S(1)}, u32[]{:S(2)}, u32[]{:S(2)}) async-start(bf16[32,16,128]{2,1,0:T(8,128)(2,1)} %bitcast.12), calls=%async_computation.4 | async-start | bytes 262144 | tf_op jit(solution)/shard_map/all_to_all | solution.py:235

commit v9 on v8

--- a/solution.py
+++ b/solution.py
@@ -40,7 +40,7 @@
     return lax.dot_general(a, b, dims, preferred_element_type=F32)
 
 
-def mask_kernel(mask_ref, pair_ref, adj_ref, *refs):
+def mask_kernel(mask_ref, lifted_ref, adj_ref, *refs):
     weighted_ref, base_ref, inverse_ref = refs[-3:]
     bands, nodes, _ = adj_ref.shape
     reach = (bands - 1) // 2
@@ -54,8 +54,7 @@
                 rows, columns = pl.ds(row * TILE, TILE), pl.ds(column * TILE, TILE)
                 weighted_ref[band, rows, columns] = adj_ref[band, rows, columns] * keep
         if band == reach:
-            pair = pair_ref[...].reshape(depth, nodes)
-            both = dot(jnp.concatenate([pair, ones], axis=0), weighted_ref[band], LAST)
+            both = dot(lifted_ref[...], weighted_ref[band], LAST)
             base_ref[...] = both[:depth]
             degree = degree + both[depth:]
         else:
@@ -63,7 +62,13 @@
     inverse_ref[...] = 1.0 / jnp.maximum(degree[:8], 1.0)
 
 
-def stack_kernel(first_ref, second_ref, out_ref):
+def lift_kernel(pair_ref, out_ref):
+    cores, width, nodes = pair_ref.shape
+    out_ref[: cores * width] = pair_ref[...].reshape(cores * width, nodes)
+    out_ref[cores * width :] = jnp.ones((out_ref.shape[0] - cores * width, nodes), BF16)
+
+
+def stack_kernel(first_ref, second_ref, _, out_ref):
     half = first_ref.shape[0]
     out_ref[:half] = first_ref[...]
     out_ref[half:] = second_ref[...]
@@ -252,8 +257,19 @@
     pair = of_chip(own)
     behind = shift(pair.reshape(wide), 1)
     ahead = shift(pair.reshape(wide), -1)
+    lifted = local_call(
+        lift_kernel,
+        shape((depth + 16, nodes), BF16),
+        [VMEM],
+        (pair,),
+        500 * adjacency.size,
+    )
     both = local_call(
-        stack_kernel, shape((2 * width, total), BF16), [VMEM] * 2, (w_self, w_neigh), 500 * adjacency.size
+        stack_kernel,
+        shape((2 * width, total), BF16),
+        [VMEM, VMEM, ANY],
+        (w_self, w_neigh, lifted),
+        adjacency.size,
     )
     weights = of_chip(both)
     adj = adjacency.transpose(1, 0, 2)
@@ -261,7 +277,7 @@
         mask_kernel,
         (shape(adj.shape, BF16), shape(wide, F32), shape((8, nodes), F32)),
         [SMEM, VMEM, VMEM, ANY],
-        (tile_mask.transpose(0, 2, 1), pair, adj, weights),
+        (tile_mask.transpose(0, 2, 1), lifted, adj, weights),
         2 * adj.size,
     )
     near = local_call(

time: 106 us -> 107 us (level)
  starting transfers between devices: 39.2 us -> 41.3 us
  local copies, waits for them, and re-layouts: 1.69 us -> 0.03 us
    all_to_all x3, starting transfers between devices: 19.7 us -> 21.9 us  [exchange(): return lax.all_to_all(chunks, axes, 0, 0, tiled=True)]
    unnamed x12 -> x10, local copies, waits for them, and re-layouts: 1.69 us -> 0.03 us
    pallas_call x12 -> x13, Pallas kernels: 7.42 us -> 8.38 us  [local_call(): pl.pallas_call(kernel, out_shape=out_shape, in_specs=in_specs, out_specs=...]
where the time goes in v9:
time: 107 us; the launch traced here: 106 us
  blocking collectives  44.8 us (42%)
  starting transfers between devices  41.3 us (39%)
  waiting for transfers between devices  11.1 us (10%)
  Pallas kernels  8.38 us (8%)
    all_gather x5, blocking collectives, of_chip(): return lax.all_gather(value, 'core', axis=0, tiled=False)  27.3 us
    all_to_all x3, starting transfers between devices, exchange(): return lax.all_to_all(chunks, axes, 0, 0, tiled=True)  21.9 us
    ppermute x4, starting transfers between devices, shift(): return lax.ppermute(value, axes, pairs)  19.5 us
    all_to_all x2, blocking collectives, exchange(): return lax.all_to_all(chunks, axes, 0, 0, tiled=True)  17.5 us
    all_to_all x3, waiting for transfers between devices, exchange(): return lax.all_to_all(chunks, axes, 0, 0, tiled=True)  11 us
    pallas_call x13, Pallas kernels, local_call(): pl.pallas_call(kernel, out_shape=out_shape, in_specs=in_specs, out_specs=...  8.38 us
  transfers between devices with their start and end apart: 7, of which 3 were waited for; matrix products, arithmetic and copies ran while one was open for 0% of the time, Pallas kernels for 3%

profile of v9, /device:TPU:1, one launch (start us, length us, event | category | flops | bytes accessed | tf_op | source)
XLA Modules:
  0.0 106.5 jit_solution(14314253882187506176)
XLA Ops:
  0.7 16.0 %all-gather = bf16[128,512]{1,0:T(8,128)(2,1)S(1)} all-gather(bf16[64,512]{1,0:T(8,128)(2,1)} %bitcast.27), channel_id=2, replica_groups=mesh['far'=8,'near'=2,'y'=8,'x'=4,'core'=2] {'core'}, dimensions={0}, use_global_device_ids=true | all-gather | bytes 196608 | tf_op jit(solution)/shard_map/all_gather | solution.py:236
  16.7 1.9 %collective-permute-start = (bf16[128,512]{1,0:T(8,128)(2,1)S(1)}, bf16[128,512]{1,0:T(8,128)(2,1)S(1)}, u32[]{:S(2)}, u32[]{:S(2)}) collective-permute-start(bf16[128,512]{1,0:T(8,128)(2,1)S(1)} %all-gather), channel_id=1, source_target_pairs={{0,8},{1,17},{8,16},{9,25},{16,24},{17,33},{24,32},{25,41},{32,40}... | collective-permute-start | bytes 393224 | tf_op jit(solution)/shard_map/ppermute | solution.py:232
  18.6 9.0 %collective-permute-start.1 = (bf16[128,512]{1,0:T(8,128)(2,1)S(1)}, bf16[128,512]{1,0:T(8,128)(2,1)}, u32[]{:S(2)}, u32[]{:S(2)}) collective-permute-start(bf16[128,512]{1,0:T(8,128)(2,1)S(1)} %all-gather), channel_id=1, source_target_pairs={{0,1016},{1,1009},{8,0},{9,1017},{16,8},{17,1},{24,16},{25,9},{32,... | collective-permute-start | bytes 393224 | tf_op jit(solution)/shard_map/ppermute | solution.py:232
  27.6 0.0 copy-start
  27.7 2.1 %all-gather.1 = bf16[256,512]{1,0:T(8,128)(2,1)S(1)} all-gather(bf16[128,512]{1,0:T(8,128)(2,1)S(1)} %shard_map.94), channel_id=3, replica_groups=mesh['far'=8,'near'=2,'y'=8,'x'=4,'core'=2] {'core'}, dimensions={0}, use_global_device_ids=true | all-gather | bytes 393216 | tf_op jit(solution)/shard_map/all_gather | solution.py:236
  29.8 1.5 %shard_map.95 = (bf16[5,512,512]{2,1,0:T(8,128)(2,1)S(1)}, f32[128,512]{1,0:T(8,128)S(1)}, f32[8,512]{1,0:T(8,128)S(1)}) custom-call(s32[4,4,5]{2,1,0:T(4,128)S(1)} %bitcast.26, bf16[144,512]{1,0:T(8,128)(2,1)S(1)} %shard_map.93._.lifted_ref, bf16[5,512,512]{2,1,0:T(8,128)(2,1)S(1)} %bitcast.17, bf16[2,128,512]{2,1,0:T(8,128)(2,1)S(1)} %bitcast.14), custom_call_target="tpu_custom_call" | custom-call | flops 2621440 | bytes 5931328 | tf_op jit(solution)/shard_map/pallas_call | solution.py:28
  31.4 0.0 collective-permute-done.behind_ref
  31.4 0.0 collective-permute-done.1.ahead_ref
  31.4 0.0 copy-start.3
  31.4 1.4 %shard_map.96 = f32[128,512]{1,0:T(8,128)S(1)} custom-call(s32[1]{0:T(128)} %bitcast.core_ref, bf16[128,512]{1,0:T(8,128)(2,1)S(1)} %collective-permute-done.behind_ref, bf16[128,512]{1,0:T(8,128)(2,1)} %collective-permute-done.1.ahead_ref, bf16[5,512,512]{2,1,0:T(8,128)(2,1)S(1)} %get-tuple-element.16.weighted_ref), custom_call_target="tpu_custom_call" | custom-call | flops 2621440 | bytes 3145732 | tf_op jit(solution)/shard_map/pallas_call | solution.py:28
  32.8 2.2 %all-gather.2 = f32[256,512]{1,0:T(8,128)S(1)} all-gather(f32[128,512]{1,0:T(8,128)S(1)} %shard_map.96), channel_id=4, replica_groups=mesh['far'=8,'near'=2,'y'=8,'x'=4,'core'=2] {'core'}, dimensions={0}, use_global_device_ids=true | all-gather | bytes 786432 | tf_op jit(solution)/shard_map/all_gather | solution.py:236
  35.0 0.4 shard_map.97
  35.4 9.6 %all_to_all.25.parts_ref = bf16[4,64,512]{2,1,0:T(8,128)(2,1)S(1)} all-to-all(bf16[4,64,512]{2,1,0:T(8,128)(2,1)S(1)} %get-tuple-element.19), channel_id=1, replica_groups=mesh['far'=8,'near'=2,'y'=8,'x'=4,'core'=2] {'x'}, dimensions={0} | all-to-all | bytes 524288 | tf_op jit(solution)/shard_map/all_to_all | solution.py:240
  45.0 0.7 shard_map.98
  45.7 7.9 %all_to_all.26.refs_0_ = bf16[4,64,512]{2,1,0:T(8,128)(2,1)S(1)} all-to-all(bf16[4,64,512]{2,1,0:T(8,128)(2,1)S(1)} %get-tuple-element.21), channel_id=1, replica_groups=mesh['far'=8,'near'=2,'y'=8,'x'=4,'core'=2] {'x'}, dimensions={0} | all-to-all | bytes 524288 | tf_op jit(solution)/shard_map/all_to_all | solution.py:240
  53.6 0.9 shard_map.102
  54.6 3.5 %all-to-all-start.2 = ((bf16[16,16,256]{2,1,0:T(8,128)(2,1)}), bf16[16,16,256]{2,1,0:T(8,128)(2,1)S(1)}, u32[]{:S(2)}, u32[]{:S(2)}) async-start(bf16[16,16,256]{2,1,0:T(8,128)(2,1)} %shard_map.102), calls=%async_computation.2 | async-start | bytes 262144 | tf_op jit(solution)/shard_map/all_to_all | solution.py:240
  58.1 4.8 %all-gather.3 = bf16[8,64,512]{2,1,0:T(8,128)(2,1)S(1)} all-gather(bf16[4,64,512]{2,1,0:T(8,128)(2,1)S(1)} %all_to_all.26.refs_0_), channel_id=5, replica_groups=mesh['far'=8,'near'=2,'y'=8,'x'=4,'core'=2] {'core'}, dimensions={0}, use_global_device_ids=true | all-gather | bytes 786432 | tf_op jit(solution)/shard_map/all_gather | solution.py:236
  62.8 0.6 shard_map.99
  63.4 2.0 %all-to-all-done.2.in_ref = bf16[16,16,256]{2,1,0:T(8,128)(2,1)S(1)} async-done(((bf16[16,16,256]{2,1,0:T(8,128)(2,1)}), bf16[16,16,256]{2,1,0:T(8,128)(2,1)S(1)}, u32[]{:S(2)}, u32[]{:S(2)}) %all-to-all-start.2) | async-done | bytes 131104 | tf_op jit(solution)/shard_map/all_to_all | solution.py:240
  65.5 0.7 shard_map.103
  66.1 9.2 %all-to-all-start.3 = ((bf16[8,16,256]{2,1,0:T(8,128)(2,1)}), bf16[8,16,256]{2,1,0:T(8,128)(2,1)S(1)}, u32[]{:S(2)}, u32[]{:S(2)}) async-start(bf16[8,16,256]{2,1,0:T(8,128)(2,1)} %shard_map.103), calls=%async_computation.3 | async-start | bytes 131072 | tf_op jit(solution)/shard_map/all_to_all | solution.py:240
  75.3 6.7 %collective-permute-start.2 = (bf16[128,512]{1,0:T(8,128)(2,1)S(1)}, bf16[128,512]{1,0:T(8,128)(2,1)S(1)}, u32[]{:S(2)}, u32[]{:S(2)}) collective-permute-start(bf16[128,512]{1,0:T(8,128)(2,1)S(1)} %get-tuple-element.23), channel_id=1, source_target_pairs={{0,1016},{1,1009},{8,0},{9,1017},{16,8},{17,1},{24,16},{25,9},{32,... | collective-permute-start | bytes 393224 | tf_op jit(solution)/shard_map/ppermute | solution.py:232
  82.0 1.9 %collective-permute-start.3 = (bf16[128,512]{1,0:T(8,128)(2,1)S(1)}, bf16[128,512]{1,0:T(8,128)(2,1)S(1)}, u32[]{:S(2)}, u32[]{:S(2)}) collective-permute-start(bf16[128,512]{1,0:T(8,128)(2,1)S(1)} %get-tuple-element.24), channel_id=1, source_target_pairs={{0,8},{1,17},{8,16},{9,25},{16,24},{17,33},{24,32},{25,41},{32,40}... | collective-permute-start | bytes 393224 | tf_op jit(solution)/shard_map/ppermute | solution.py:232
  83.9 3.6 %all-to-all-done.3.in_ref = bf16[8,16,256]{2,1,0:T(8,128)(2,1)S(1)} async-done(((bf16[8,16,256]{2,1,0:T(8,128)(2,1)}), bf16[8,16,256]{2,1,0:T(8,128)(2,1)S(1)}, u32[]{:S(2)}, u32[]{:S(2)}) %all-to-all-start.3) | async-done | bytes 65568 | tf_op jit(solution)/shard_map/all_to_all | solution.py:240
  87.6 0.7 shard_map.104
  88.2 9.1 %all-to-all-start.4 = ((bf16[32,16,128]{2,1,0:T(8,128)(2,1)}), bf16[32,16,128]{2,1,0:T(8,128)(2,1)S(1)}, u32[]{:S(2)}, u32[]{:S(2)}) async-start(bf16[32,16,128]{2,1,0:T(8,128)(2,1)} %bitcast.12), calls=%async_computation.4 | async-start | bytes 262144 | tf_op jit(solution)/shard_map/all_to_all | solution.py:240
  97.4 0.0 collective-permute-done.3.second_ref
  97.4 2.2 %all-gather.4 = f32[256,512]{1,0:T(8,128)S(1)} all-gather(f32[128,512]{1,0:T(8,128)S(1)} %shard_map.100), channel_id=6, replica_groups=mesh['far'=8,'near'=2,'y'=8,'x'=4,'core'=2] {'core'}, dimensions={0}, use_global_device_ids=true | all-gather | bytes 786432 | tf_op jit(solution)/shard_map/all_gather | solution.py:236
  99.6 0.7 shard_map.101
  100.3 5.4 %all-to-all-done.4 = bf16[32,16,128]{2,1,0:T(8,128)(2,1)S(1)} async-done(((bf16[32,16,128]{2,1,0:T(8,128)(2,1)}), bf16[32,16,128]{2,1,0:T(8,128)(2,1)S(1)}, u32[]{:S(2)}, u32[]{:S(2)}) %all-to-all-start.4) | async-done | bytes 131104 | tf_op jit(solution)/shard_map/all_to_all | solution.py:240
  105.7 0.8 shard_map.105
  (12 shorter events, 0.1 us)
Async XLA Ops:
  0.6 27.0 %copy-start.1 = (bf16[64,512]{1,0:T(8,128)(2,1)S(1)}, bf16[64,512]{1,0:T(8,128)(2,1)}, u32[]{:S(2)}) copy-start(bf16[64,512]{1,0:T(8,128)(2,1)} %wself_ref.1) | copy-start | bytes 196612
  0.6 27.0 %copy-start.2 = (bf16[64,512]{1,0:T(8,128)(2,1)S(1)}, bf16[64,512]{1,0:T(8,128)(2,1)}, u32[]{:S(2)}) copy-start(bf16[64,512]{1,0:T(8,128)(2,1)} %second_ref.1) | copy-start | bytes 196612
  0.7 29.2 %copy-start.4 = (s32[4,5,4]{1,2,0:T(4,128)S(1)}, s32[4,5,4]{1,2,0:T(4,128)}, u32[]{:S(2)}) copy-start(s32[4,5,4]{1,2,0:T(4,128)} %param.8) | copy-start | bytes 964
  16.7 14.7 %collective-permute-start = (bf16[128,512]{1,0:T(8,128)(2,1)S(1)}, bf16[128,512]{1,0:T(8,128)(2,1)S(1)}, u32[]{:S(2)}, u32[]{:S(2)}) collective-permute-start(bf16[128,512]{1,0:T(8,128)(2,1)S(1)} %all-gather), channel_id=1, source_target_pairs={{0,8},{1,17},{8,16},{9,25},{16,24},{17,33},{24,32},{25,41},{32,40}... | collective-permute-start | bytes 393224 | tf_op jit(solution)/shard_map/ppermute | solution.py:232
  18.6 12.8 %collective-permute-start.1 = (bf16[128,512]{1,0:T(8,128)(2,1)S(1)}, bf16[128,512]{1,0:T(8,128)(2,1)}, u32[]{:S(2)}, u32[]{:S(2)}) collective-permute-start(bf16[128,512]{1,0:T(8,128)(2,1)S(1)} %all-gather), channel_id=1, source_target_pairs={{0,1016},{1,1009},{8,0},{9,1017},{16,8},{17,1},{24,16},{25,9},{32,... | collective-permute-start | bytes 393224 | tf_op jit(solution)/shard_map/ppermute | solution.py:232
  27.6 2.2 %copy-start = (bf16[512,5,512]{2,0,1:T(8,128)(2,1)S(1)}, bf16[512,5,512]{2,0,1:T(8,128)(2,1)}, u32[]{:S(2)}) copy-start(bf16[512,5,512]{2,0,1:T(8,128)(2,1)} %param.7) | copy-start | bytes 7864324
  31.4 13.6 %copy-start.3 = (bf16[512,64]{0,1:T(8,128)(2,1)S(1)}, bf16[512,64]{0,1:T(8,128)(2,1)}, u32[]{:S(2)}) copy-start(bf16[512,64]{0,1:T(8,128)(2,1)} %param.11) | copy-start | bytes 196612
  54.6 10.9 %all-to-all-start.2 = ((bf16[16,16,256]{2,1,0:T(8,128)(2,1)}), bf16[16,16,256]{2,1,0:T(8,128)(2,1)S(1)}, u32[]{:S(2)}, u32[]{:S(2)}) async-start(bf16[16,16,256]{2,1,0:T(8,128)(2,1)} %shard_map.102), calls=%async_computation.2 | async-start | bytes 262144 | tf_op jit(solution)/shard_map/all_to_all | solution.py:240
  66.1 21.4 %all-to-all-start.3 = ((bf16[8,16,256]{2,1,0:T(8,128)(2,1)}), bf16[8,16,256]{2,1,0:T(8,128)(2,1)S(1)}, u32[]{:S(2)}, u32[]{:S(2)}) async-start(bf16[8,16,256]{2,1,0:T(8,128)(2,1)} %shard_map.103), calls=%async_computation.3 | async-start | bytes 131072 | tf_op jit(solution)/shard_map/all_to_all | solution.py:240
  75.3 22.0 %collective-permute-start.2 = (bf16[128,512]{1,0:T(8,128)(2,1)S(1)}, bf16[128,512]{1,0:T(8,128)(2,1)S(1)}, u32[]{:S(2)}, u32[]{:S(2)}) collective-permute-start(bf16[128,512]{1,0:T(8,128)(2,1)S(1)} %get-tuple-element.23), channel_id=1, source_target_pairs={{0,1016},{1,1009},{8,0},{9,1017},{16,8},{17,1},{24,16},{25,9},{32,... | collective-permute-start | bytes 393224 | tf_op jit(solution)/shard_map/ppermute | solution.py:232
  82.0 15.4 %collective-permute-start.3 = (bf16[128,512]{1,0:T(8,128)(2,1)S(1)}, bf16[128,512]{1,0:T(8,128)(2,1)S(1)}, u32[]{:S(2)}, u32[]{:S(2)}) collective-permute-start(bf16[128,512]{1,0:T(8,128)(2,1)S(1)} %get-tuple-element.24), channel_id=1, source_target_pairs={{0,8},{1,17},{8,16},{9,25},{16,24},{17,33},{24,32},{25,41},{32,40}... | collective-permute-start | bytes 393224 | tf_op jit(solution)/shard_map/ppermute | solution.py:232
  88.2 17.4 %all-to-all-start.4 = ((bf16[32,16,128]{2,1,0:T(8,128)(2,1)}), bf16[32,16,128]{2,1,0:T(8,128)(2,1)S(1)}, u32[]{:S(2)}, u32[]{:S(2)}) async-start(bf16[32,16,128]{2,1,0:T(8,128)(2,1)} %bitcast.12), calls=%async_computation.4 | async-start | bytes 262144 | tf_op jit(solution)/shard_map/all_to_all | solution.py:240
